TPU v7x, 1024 devices: a whole 4x4x32 slice. The times are simulated.
1024 devices in a mesh: section: 16 (over y_lo, x, core), expert: 64 (over y_hi, z).
Axes of the slice: x: 4, y: 4 (y_hi: 2, y_lo: 2; y = y_hi * 2 + y_lo), z: 32, core: 2. Of those that a mesh axis runs over, the one named last changes fastest.
Arguments:
- held_up: bfloat16 [16, 128, 28672], P('section', None, 'expert'), may hold values from -6 to 6
- held_down: bfloat16 [16, 128, 28672], P('section', None, 'expert'), may hold values from -6 to 6
- routes_up: int32 [16, 512, 8], P('section'), may hold values from 0 to 255, as said below
- routes_down: int32 [16, 512, 8], P('section'), may hold values from 0 to 255, as said below
- gates_up: float32 [16, 512, 8], P('section'), may hold values from 0.5 to 2.5
- gates_down: float32 [16, 512, 8], P('section'), may hold values from 0.5 to 2.5
- capacity: int32 [16, 4], P('section'), may hold values from 40 to 80, as said below
- w_gate: bfloat16 [16, 28672, 1024], P('section', 'expert'), may hold values from -0.0625 to 0.0625
- w_up: bfloat16 [16, 28672, 1024], P('section', 'expert'), may hold values from -0.0625 to 0.0625
- w_down: bfloat16 [16, 28672, 1024], P('section', 'expert'), may hold values from -0.1875 to 0.1875
Outputs:
- arrived_up: bfloat16 [16, 128, 28672], P('section', None, 'expert')
- arrived_down: bfloat16 [16, 128, 28672], P('section', None, 'expert')
Inputs may be any that keep to these rules, and one draw needn't show every extreme that they name: `routes_up`: each row names 8 different experts. At some section an expert in flight has capacity 80 and is named by at least 80 upward rows of every group. `routes_down`: each row names 8 different experts. At some section one expert in flight has capacity 80.
All inputs are finite; a program needn't handle non-finite values.
Results may differ from a plain program's by a relative error of at most 0.0051.
Values may be sent and summed in bfloat16 or wider, within the bound.
No kernel may reach another device: no remote copies, remote signals or barrier semaphores. Data moves between devices by JAX's collectives and lax.ppermute only.
A program may use at most 32 MiB of HBM per device.

v0:
```python
import jax
import jax.numpy as jnp
from jax import lax
from jax.sharding import PartitionSpec as P


def from_partner(block, axis, bit):
    count = lax.axis_size(axis)
    route = []
    for low in range(count):
        high = low | 1 << bit
        if high != low and high < count:
            route += [(low, high), (high, low)]
    return lax.ppermute(block, axis, route)


def from_behind(value, axis, steps):
    count = lax.axis_size(axis)
    pairs = [(source, (source + steps) % count) for source in range(count)]
    return lax.ppermute(value, axis, pairs)


def across_groups(buffer, group_index, group_bits, feature_bits):
    for level in range(group_bits):
        upper_bit = group_index // (1 << level) % 2 == 1
        buffer_dims = buffer.shape
        leading = buffer_dims[0] // (1 << level + 1)
        trailing = 1 << level
        shaped = buffer.reshape((leading, 2, trailing) + buffer_dims[1:])
        first_half = shaped[:, 0]
        second_half = shaped[:, 1]
        outbound = jnp.where(upper_bit, first_half, second_half)
        inbound = from_partner(outbound, "expert", feature_bits + level)
        new_first = jnp.where(upper_bit, inbound, first_half)
        new_second = jnp.where(upper_bit, second_half, inbound)
        buffer = jnp.stack([new_first, new_second], axis=1).reshape(buffer_dims)
    return buffer


def halve_sums(partial_value, my_index, level):
    half_rows = partial_value.shape[0] // 2
    lower_part = partial_value[:half_rows]
    upper_part = partial_value[half_rows:]
    upper_bit = my_index // (1 << level) % 2 == 1
    outbound = jnp.where(upper_bit, lower_part, upper_part)
    retained = jnp.where(upper_bit, upper_part, lower_part)
    return retained + from_partner(outbound, "expert", level)


def double_rows(hidden, my_index, level):
    partner_rows = from_partner(hidden, "expert", level)
    upper_bit = my_index // (1 << level) % 2 == 1
    return jnp.where(
        upper_bit,
        jnp.concatenate([partner_rows, hidden], axis=0),
        jnp.concatenate([hidden, partner_rows], axis=0),
    )


def local(
    held_up, held_down, routes_up, routes_down, gates_up, gates_down, capacity, w_gate, w_up, w_down
):
    expert_count = lax.axis_size("expert")
    feature_parts = min(16, expert_count)
    group_count = expert_count // feature_parts
    feature_bits = feature_parts.bit_length() - 1
    group_bits = group_count.bit_length() - 1
    my_index = lax.axis_index("expert")
    group_index = my_index // feature_parts
    tok_count = held_up.shape[1]
    slice_width = held_up.shape[2]
    hidden_width = w_gate.shape[2]
    cap_slots = 8 * max(1, tok_count * 5 // 64)
    local_rows = jnp.concatenate([held_up[0], held_down[0]], axis=0)
    start = group_index * tok_count
    route_rows = jnp.concatenate(
        [
            lax.dynamic_slice_in_dim(routes_up[0], start, tok_count, 0),
            lax.dynamic_slice_in_dim(routes_down[0], start, tok_count, 0),
        ],
        axis=0,
    )
    gate_rows = jnp.concatenate(
        [
            lax.dynamic_slice_in_dim(gates_up[0], start, tok_count, 0),
            lax.dynamic_slice_in_dim(gates_down[0], start, tok_count, 0),
        ],
        axis=0,
    )
    window_ids = jnp.arange(group_count, dtype=jnp.int32)
    matches = route_rows[:, :, None] == window_ids[None, None, :]
    hit_mask = jnp.sum(matches.astype(jnp.int32), axis=1)
    gate_sel = jnp.sum(jnp.where(matches, gate_rows[:, :, None], jnp.float32(0.0)), axis=1)
    rank_before = jnp.cumsum(hit_mask, axis=0) - hit_mask
    kept_mask = hit_mask * (rank_before < capacity[0][None, :]).astype(jnp.int32)
    slot_ids = jnp.arange(cap_slots, dtype=jnp.int32)
    slot_mask = (kept_mask[:, :, None] == 1) & (rank_before[:, :, None] == slot_ids[None, None, :])
    outgoing = jnp.einsum(
        "rec,rd->ecd",
        slot_mask.astype(jnp.bfloat16),
        local_rows,
        preferred_element_type=jnp.float32,
    ).astype(jnp.bfloat16)
    incoming = across_groups(outgoing, group_index, group_bits, feature_bits)
    received = incoming.reshape(group_count * cap_slots, slice_width)
    gate_part = jnp.dot(received, w_gate[0], preferred_element_type=jnp.float32)
    up_part = jnp.dot(received, w_up[0], preferred_element_type=jnp.float32)
    partial_value = jnp.concatenate([gate_part, up_part], axis=1)
    bit_order = list(range(feature_bits))
    for level in bit_order:
        partial_value = halve_sums(partial_value, my_index, level)
    hidden = (
        jax.nn.silu(partial_value[:, :hidden_width]) * partial_value[:, hidden_width:]
    ).astype(jnp.bfloat16)
    for level in reversed(bit_order):
        hidden = double_rows(hidden, my_index, level)
    expert_out = lax.dot_general(
        hidden, w_down[0], (((1,), (1,)), ((), ())), preferred_element_type=jnp.float32
    ).astype(jnp.bfloat16)
    returned = across_groups(
        expert_out.reshape(group_count, cap_slots, slice_width),
        group_index,
        group_bits,
        feature_bits,
    )
    combine_weights = slot_mask.astype(jnp.float32) * gate_sel[:, :, None]
    branch_sum = jnp.einsum(
        "rec,ecd->rd",
        combine_weights,
        returned.astype(jnp.float32),
        precision=lax.Precision.HIGHEST,
    )
    finished = (local_rows.astype(jnp.float32) + branch_sum).astype(jnp.bfloat16)
    arrived_up = from_behind(finished[:tok_count], "section", 1)
    arrived_down = from_behind(finished[tok_count:], "section", -1)
    return (arrived_up[None], arrived_down[None])


def solution(mesh):
    placed = (
        P("section", None, "expert"),
        P("section", None, "expert"),
        P("section", None, None),
        P("section", None, None),
        P("section", None, None),
        P("section", None, None),
        P("section", None),
        P("section", "expert", None),
        P("section", "expert", None),
        P("section", "expert", None),
    )
    return jax.shard_map(
        local,
        mesh=mesh,
        in_specs=placed,
        out_specs=(P("section", None, "expert"), P("section", None, "expert")),
        check_vma=False,
    )
```

profile of v0, /device:TPU:7, one launch (start us, length us, event | category | flops | bytes accessed | tf_op | source)
XLA Modules:
  0.0 321.1 jit_solution(11200557881254208477)
XLA Ops:
  0.7 0.8 dynamic-slice_bitcast_fusion.2
  1.5 1.2 reduce-window.6
  3.9 1.2 convolution_convert_fusion.1
  5.1 28.7 %collective-permute-start = (bf16[2,1,80,448]{3,2,0,1:T(8,128)(2,1)S(1)}, bf16[2,1,80,448]{3,2,0,1:T(8,128)(2,1)S(1)}, u32[]{:S(2)}, u32[]{:S(2)}) collective-permute-start(bf16[2,1,80,448]{3,2,0,1:T(8,128)(2,1)S(1)} %broadcast_select_fusion.2), channel_id=1, source_target_pairs={{0,16},{16,0},{1,17},{17,1},{2,18},{18,2},{3,19},{19,3},{4,20},{20... | collective-permute-start | bytes 430088 | tf_op jit(solution)/shard_map/ppermute | solution.py:14
  33.9 4.3 %collective-permute-done = bf16[2,1,80,448]{3,2,0,1:T(8,128)(2,1)S(1)} collective-permute-done((bf16[2,1,80,448]{3,2,0,1:T(8,128)(2,1)S(1)}, bf16[2,1,80,448]{3,2,0,1:T(8,128)(2,1)S(1)}, u32[]{:S(2)}, u32[]{:S(2)}) %collective-permute-start) | collective-permute-done | bytes 143392 | tf_op jit(solution)/shard_map/ppermute | solution.py:14
  38.2 4.8 %collective-permute-start.1 = (bf16[1,2,80,448]{3,2,1,0:T(8,128)(2,1)S(1)}, bf16[1,2,80,448]{3,2,1,0:T(8,128)(2,1)S(1)}, u32[]{:S(2)}, u32[]{:S(2)}) collective-permute-start(bf16[1,2,80,448]{3,2,1,0:T(8,128)(2,1)S(1)} %broadcast_select_fusion.4), channel_id=1, source_target_pairs={{0,32},{32,0},{1,33},{33,1},{2,34},{34,2},{3,35},{35,3},{4,36},{36... | collective-permute-start | bytes 430088 | tf_op jit(solution)/shard_map/ppermute | solution.py:14
  43.1 2.7 collective-permute-done.1
  47.8 0.9 copy-done.1
  48.7 25.7 %collective-permute-start.2 = (f32[160,2048]{1,0:T(8,128)S(1)}, f32[160,2048]{1,0:T(8,128)}, u32[]{:S(2)}, u32[]{:S(2)}) collective-permute-start(f32[160,2048]{1,0:T(8,128)S(1)} %broadcast_select_fusion), channel_id=1, source_target_pairs={{0,1},{1,0},{2,3},{3,2},{4,5},{5,4},{6,7},{7,6},{8,9},{9,8},{10,11... | collective-permute-start | bytes 3932168 | tf_op jit(solution)/shard_map/ppermute | solution.py:14
  74.4 26.5 %collective-permute-done.2 = f32[160,2048]{1,0:T(8,128)} collective-permute-done((f32[160,2048]{1,0:T(8,128)S(1)}, f32[160,2048]{1,0:T(8,128)}, u32[]{:S(2)}, u32[]{:S(2)}) %collective-permute-start.2) | collective-permute-done | bytes 1310752 | tf_op jit(solution)/shard_map/ppermute | solution.py:14
  100.8 1.9 select_add_fusion
  102.8 1.9 collective-permute-start.3
  104.8 30.6 %collective-permute-done.3 = f32[80,2048]{1,0:T(8,128)S(1)} collective-permute-done((f32[80,2048]{1,0:T(8,128)S(1)}, f32[80,2048]{1,0:T(8,128)S(1)}, u32[]{:S(2)}, u32[]{:S(2)}) %collective-permute-start.3) | collective-permute-done | bytes 655392 | tf_op jit(solution)/shard_map/ppermute | solution.py:14
  135.5 1.9 collective-permute-start.4
  137.5 33.3 %collective-permute-done.4 = f32[40,2048]{1,0:T(8,128)S(1)} collective-permute-done((f32[40,2048]{1,0:T(8,128)S(1)}, f32[40,2048]{1,0:T(8,128)S(1)}, u32[]{:S(2)}, u32[]{:S(2)}) %collective-permute-start.4) | collective-permute-done | bytes 327712 | tf_op jit(solution)/shard_map/ppermute | solution.py:14
  170.8 20.9 %collective-permute-start.5 = (f32[20,2048]{1,0:T(8,128)S(1)}, f32[20,2048]{1,0:T(8,128)S(1)}, u32[]{:S(2)}, u32[]{:S(2)}) collective-permute-start(f32[20,2048]{1,0:T(8,128)S(1)} %slice_select_fusion.2), channel_id=1, source_target_pairs={{0,8},{8,0},{1,9},{9,1},{2,10},{10,2},{3,11},{11,3},{4,12},{12,4},... | collective-permute-start | bytes 491528 | tf_op jit(solution)/shard_map/ppermute | solution.py:14
  191.8 25.3 %collective-permute-done.5 = f32[20,2048]{1,0:T(8,128)S(1)} collective-permute-done((f32[20,2048]{1,0:T(8,128)S(1)}, f32[20,2048]{1,0:T(8,128)S(1)}, u32[]{:S(2)}, u32[]{:S(2)}) %collective-permute-start.5) | collective-permute-done | bytes 163872 | tf_op jit(solution)/shard_map/ppermute | solution.py:14
  217.2 1.9 collective-permute-start.6
  219.1 11.6 %collective-permute-done.6 = bf16[20,1024]{1,0:T(8,128)(2,1)S(1)} collective-permute-done((bf16[20,1024]{1,0:T(8,128)(2,1)S(1)}, bf16[20,1024]{1,0:T(8,128)(2,1)S(1)}, u32[]{:S(2)}, u32[]{:S(2)}) %collective-permute-start.6) | collective-permute-done | bytes 40992 | tf_op jit(solution)/shard_map/ppermute | solution.py:14
  230.8 1.9 collective-permute-start.7
  232.7 7.2 %collective-permute-done.7 = bf16[40,1024]{1,0:T(8,128)(2,1)S(1)} collective-permute-done((bf16[40,1024]{1,0:T(8,128)(2,1)S(1)}, bf16[40,1024]{1,0:T(8,128)(2,1)S(1)}, u32[]{:S(2)}, u32[]{:S(2)}) %collective-permute-start.7) | collective-permute-done | bytes 81952 | tf_op jit(solution)/shard_map/ppermute | solution.py:14
  239.9 1.9 collective-permute-start.8
  241.8 5.4 %collective-permute-done.8 = bf16[80,1024]{1,0:T(8,128)(2,1)S(1)} collective-permute-done((bf16[80,1024]{1,0:T(8,128)(2,1)S(1)}, bf16[80,1024]{1,0:T(8,128)(2,1)S(1)}, u32[]{:S(2)}, u32[]{:S(2)}) %collective-permute-start.8) | collective-permute-done | bytes 163872 | tf_op jit(solution)/shard_map/ppermute | solution.py:14
  247.3 1.9 collective-permute-start.9
  249.2 5.9 %collective-permute-done.9 = bf16[160,1024]{1,0:T(8,128)(2,1)S(1)} collective-permute-done((bf16[160,1024]{1,0:T(8,128)(2,1)S(1)}, bf16[160,1024]{1,0:T(8,128)(2,1)S(1)}, u32[]{:S(2)}, u32[]{:S(2)}) %collective-permute-start.9) | collective-permute-done | bytes 327712 | tf_op jit(solution)/shard_map/ppermute | solution.py:14
  255.7 13.9 %collective-permute-start.10 = (bf16[2,1,80,448]{3,2,0,1:T(8,128)(2,1)S(1)}, bf16[2,1,80,448]{3,2,0,1:T(8,128)(2,1)S(1)}, u32[]{:S(2)}, u32[]{:S(2)}) collective-permute-start(bf16[2,1,80,448]{3,2,0,1:T(8,128)(2,1)S(1)} %broadcast_select_fusion.1), channel_id=1, source_target_pairs={{0,16},{16,0},{1,17},{17,1},{2,18},{18,2},{3,19},{19,3},{4,20},{20... | collective-permute-start | bytes 430088 | tf_op jit(solution)/shard_map/ppermute | solution.py:14
  270.3 28.1 %collective-permute-done.10 = bf16[2,1,80,448]{3,2,0,1:T(8,128)(2,1)S(1)} collective-permute-done((bf16[2,1,80,448]{3,2,0,1:T(8,128)(2,1)S(1)}, bf16[2,1,80,448]{3,2,0,1:T(8,128)(2,1)S(1)}, u32[]{:S(2)}, u32[]{:S(2)}) %collective-permute-start.10) | collective-permute-done | bytes 143392 | tf_op jit(solution)/shard_map/ppermute | solution.py:14
  298.5 2.1 collective-permute-start.11
  300.6 5.6 %collective-permute-done.11 = bf16[1,2,80,448]{3,2,1,0:T(8,128)(2,1)S(1)} collective-permute-done((bf16[1,2,80,448]{3,2,1,0:T(8,128)(2,1)S(1)}, bf16[1,2,80,448]{3,2,1,0:T(8,128)(2,1)S(1)}, u32[]{:S(2)}, u32[]{:S(2)}) %collective-permute-start.11) | collective-permute-done | bytes 143392 | tf_op jit(solution)/shard_map/ppermute | solution.py:14
  307.1 8.0 %collective-permute-start.13 = (bf16[128,448]{0,1:T(8,128)(2,1)S(1)}, bf16[128,448]{0,1:T(8,128)(2,1)S(1)}, u32[]{:S(2)}, u32[]{:S(2)}) collective-permute-start(bf16[128,448]{0,1:T(8,128)(2,1)S(1)} %get-tuple-element.12), channel_id=1, source_target_pairs={{0,960},{64,0},{128,64},{192,128},{256,192},{320,256},{384,320},{4... | collective-permute-start | bytes 344072 | tf_op jit(solution)/shard_map/ppermute | solution.py:20
  315.0 3.0 collective-permute-start.12
  318.6 1.2 collective-permute-done.12
  (55 shorter events, 7.6 us)
Async XLA Ops:
  0.6 45.3 %copy-start = (bf16[1,448,1024]{2,1,0:T(8,128)(2,1)S(1)}, bf16[1,448,1024]{2,1,0:T(8,128)(2,1)}, u32[]{:S(2)}) copy-start(bf16[1,448,1024]{2,1,0:T(8,128)(2,1)} %param.18) | copy-start | bytes 2752516
  5.1 33.0 %collective-permute-start = (bf16[2,1,80,448]{3,2,0,1:T(8,128)(2,1)S(1)}, bf16[2,1,80,448]{3,2,0,1:T(8,128)(2,1)S(1)}, u32[]{:S(2)}, u32[]{:S(2)}) collective-permute-start(bf16[2,1,80,448]{3,2,0,1:T(8,128)(2,1)S(1)} %broadcast_select_fusion.2), channel_id=1, source_target_pairs={{0,16},{16,0},{1,17},{17,1},{2,18},{18,2},{3,19},{19,3},{4,20},{20... | collective-permute-start | bytes 430088 | tf_op jit(solution)/shard_map/ppermute | solution.py:14
  38.2 7.6 %collective-permute-start.1 = (bf16[1,2,80,448]{3,2,1,0:T(8,128)(2,1)S(1)}, bf16[1,2,80,448]{3,2,1,0:T(8,128)(2,1)S(1)}, u32[]{:S(2)}, u32[]{:S(2)}) collective-permute-start(bf16[1,2,80,448]{3,2,1,0:T(8,128)(2,1)S(1)} %broadcast_select_fusion.4), channel_id=1, source_target_pairs={{0,32},{32,0},{1,33},{33,1},{2,34},{34,2},{3,35},{35,3},{4,36},{36... | collective-permute-start | bytes 430088 | tf_op jit(solution)/shard_map/ppermute | solution.py:14
  45.9 1.2 copy-start.2
  47.6 1.1 copy-start.1
  48.7 52.2 %collective-permute-start.2 = (f32[160,2048]{1,0:T(8,128)S(1)}, f32[160,2048]{1,0:T(8,128)}, u32[]{:S(2)}, u32[]{:S(2)}) collective-permute-start(f32[160,2048]{1,0:T(8,128)S(1)} %broadcast_select_fusion), channel_id=1, source_target_pairs={{0,1},{1,0},{2,3},{3,2},{4,5},{5,4},{6,7},{7,6},{8,9},{9,8},{10,11... | collective-permute-start | bytes 3932168 | tf_op jit(solution)/shard_map/ppermute | solution.py:14
  102.8 32.5 %collective-permute-start.3 = (f32[80,2048]{1,0:T(8,128)S(1)}, f32[80,2048]{1,0:T(8,128)S(1)}, u32[]{:S(2)}, u32[]{:S(2)}) collective-permute-start(f32[80,2048]{1,0:T(8,128)S(1)} %slice_select_fusion), channel_id=1, source_target_pairs={{0,2},{2,0},{1,3},{3,1},{4,6},{6,4},{5,7},{7,5},{8,10},{10,8},{9,1... | collective-permute-start | bytes 1966088 | tf_op jit(solution)/shard_map/ppermute | solution.py:14
  135.5 35.3 %collective-permute-start.4 = (f32[40,2048]{1,0:T(8,128)S(1)}, f32[40,2048]{1,0:T(8,128)S(1)}, u32[]{:S(2)}, u32[]{:S(2)}) collective-permute-start(f32[40,2048]{1,0:T(8,128)S(1)} %slice_select_fusion.1), channel_id=1, source_target_pairs={{0,4},{4,0},{1,5},{5,1},{2,6},{6,2},{3,7},{7,3},{8,12},{12,8},{9,1... | collective-permute-start | bytes 983048 | tf_op jit(solution)/shard_map/ppermute | solution.py:14
  170.8 84.3 %copy-start.3 = (bf16[1,448,1024]{2,1,0:T(8,128)(2,1)S(1)}, bf16[1,448,1024]{2,1,0:T(8,128)(2,1)}, u32[]{:S(2)}) copy-start(bf16[1,448,1024]{2,1,0:T(8,128)(2,1)} %param.19) | copy-start | bytes 2752516
  170.8 46.3 %collective-permute-start.5 = (f32[20,2048]{1,0:T(8,128)S(1)}, f32[20,2048]{1,0:T(8,128)S(1)}, u32[]{:S(2)}, u32[]{:S(2)}) collective-permute-start(f32[20,2048]{1,0:T(8,128)S(1)} %slice_select_fusion.2), channel_id=1, source_target_pairs={{0,8},{8,0},{1,9},{9,1},{2,10},{10,2},{3,11},{11,3},{4,12},{12,4},... | collective-permute-start | bytes 491528 | tf_op jit(solution)/shard_map/ppermute | solution.py:14
  217.2 13.5 %collective-permute-start.6 = (bf16[20,1024]{1,0:T(8,128)(2,1)S(1)}, bf16[20,1024]{1,0:T(8,128)(2,1)S(1)}, u32[]{:S(2)}, u32[]{:S(2)}) collective-permute-start(bf16[20,1024]{1,0:T(8,128)(2,1)S(1)} %fusion.25), channel_id=1, source_target_pairs={{0,8},{8,0},{1,9},{9,1},{2,10},{10,2},{3,11},{11,3},{4,12},{12,4},... | collective-permute-start | bytes 122888 | tf_op jit(solution)/shard_map/ppermute | solution.py:14
  230.8 9.1 %collective-permute-start.7 = (bf16[40,1024]{1,0:T(8,128)(2,1)S(1)}, bf16[40,1024]{1,0:T(8,128)(2,1)S(1)}, u32[]{:S(2)}, u32[]{:S(2)}) collective-permute-start(bf16[40,1024]{1,0:T(8,128)(2,1)S(1)} %maximum_select_fusion.4), channel_id=1, source_target_pairs={{0,4},{4,0},{1,5},{5,1},{2,6},{6,2},{3,7},{7,3},{8,12},{12,8},{9,1... | collective-permute-start | bytes 245768 | tf_op jit(solution)/shard_map/ppermute | solution.py:14
  239.9 7.3 %collective-permute-start.8 = (bf16[80,1024]{1,0:T(8,128)(2,1)S(1)}, bf16[80,1024]{1,0:T(8,128)(2,1)S(1)}, u32[]{:S(2)}, u32[]{:S(2)}) collective-permute-start(bf16[80,1024]{1,0:T(8,128)(2,1)S(1)} %maximum_select_fusion.3), channel_id=1, source_target_pairs={{0,2},{2,0},{1,3},{3,1},{4,6},{6,4},{5,7},{7,5},{8,10},{10,8},{9,1... | collective-permute-start | bytes 491528 | tf_op jit(solution)/shard_map/ppermute | solution.py:14
  247.3 7.8 %collective-permute-start.9 = (bf16[160,1024]{1,0:T(8,128)(2,1)S(1)}, bf16[160,1024]{1,0:T(8,128)(2,1)S(1)}, u32[]{:S(2)}, u32[]{:S(2)}) collective-permute-start(bf16[160,1024]{1,0:T(8,128)(2,1)S(1)} %maximum_select_fusion.2), channel_id=1, source_target_pairs={{0,1},{1,0},{2,3},{3,2},{4,5},{5,4},{6,7},{7,6},{8,9},{9,8},{10,11... | collective-permute-start | bytes 983048 | tf_op jit(solution)/shard_map/ppermute | solution.py:14
  255.7 42.7 %collective-permute-start.10 = (bf16[2,1,80,448]{3,2,0,1:T(8,128)(2,1)S(1)}, bf16[2,1,80,448]{3,2,0,1:T(8,128)(2,1)S(1)}, u32[]{:S(2)}, u32[]{:S(2)}) collective-permute-start(bf16[2,1,80,448]{3,2,0,1:T(8,128)(2,1)S(1)} %broadcast_select_fusion.1), channel_id=1, source_target_pairs={{0,16},{16,0},{1,17},{17,1},{2,18},{18,2},{3,19},{19,3},{4,20},{20... | collective-permute-start | bytes 430088 | tf_op jit(solution)/shard_map/ppermute | solution.py:14
  298.4 7.9 %copy-start.4 = (bf16[1,128,448]{1,2,0:T(8,128)(2,1)S(1)}, bf16[1,128,448]{1,2,0:T(8,128)(2,1)}, u32[]{:S(2)}) copy-start(bf16[1,128,448]{1,2,0:T(8,128)(2,1)} %param.11) | copy-start | bytes 344068
  298.5 7.9 %copy-start.5 = (bf16[1,128,448]{1,2,0:T(8,128)(2,1)S(1)}, bf16[1,128,448]{1,2,0:T(8,128)(2,1)}, u32[]{:S(2)}) copy-start(bf16[1,128,448]{1,2,0:T(8,128)(2,1)} %param.10) | copy-start | bytes 344068
  298.5 7.7 %collective-permute-start.11 = (bf16[1,2,80,448]{3,2,1,0:T(8,128)(2,1)S(1)}, bf16[1,2,80,448]{3,2,1,0:T(8,128)(2,1)S(1)}, u32[]{:S(2)}, u32[]{:S(2)}) collective-permute-start(bf16[1,2,80,448]{3,2,1,0:T(8,128)(2,1)S(1)} %broadcast_select_fusion.3), channel_id=1, source_target_pairs={{0,32},{32,0},{1,33},{33,1},{2,34},{34,2},{3,35},{35,3},{4,36},{36... | collective-permute-start | bytes 430088 | tf_op jit(solution)/shard_map/ppermute | solution.py:14
  307.1 11.5 %collective-permute-start.13 = (bf16[128,448]{0,1:T(8,128)(2,1)S(1)}, bf16[128,448]{0,1:T(8,128)(2,1)S(1)}, u32[]{:S(2)}, u32[]{:S(2)}) collective-permute-start(bf16[128,448]{0,1:T(8,128)(2,1)S(1)} %get-tuple-element.12), channel_id=1, source_target_pairs={{0,960},{64,0},{128,64},{192,128},{256,192},{320,256},{384,320},{4... | collective-permute-start | bytes 344072 | tf_op jit(solution)/shard_map/ppermute | solution.py:20
  315.0 4.8 %collective-permute-start.12 = (bf16[128,448]{0,1:T(8,128)(2,1)S(1)}, bf16[128,448]{0,1:T(8,128)(2,1)S(1)}, u32[]{:S(2)}, u32[]{:S(2)}) collective-permute-start(bf16[128,448]{0,1:T(8,128)(2,1)S(1)} %get-tuple-element.13), channel_id=1, source_target_pairs={{0,64},{64,128},{128,192},{192,256},{256,320},{320,384},{384,448},... | collective-permute-start | bytes 344072 | tf_op jit(solution)/shard_map/ppermute | solution.py:20
where the time goes:
time: 325 us; the launch traced here: 321 us
  waiting for transfers between devices  188 us (58%)
  starting transfers between devices  119 us (37%)
  other arithmetic  5.02 us (2%)
  local copies, waits for them, and re-layouts  4.67 us (1%)
  matrix products  3.44 us (1%)
    ppermute x12, waiting for transfers between devices, from_partner(): return lax.ppermute(block, axis, route)  186 us
    ppermute x12, starting transfers between devices, from_partner(): return lax.ppermute(block, axis, route)  108 us
    ppermute x2, starting transfers between devices, from_behind(): return lax.ppermute(value, axis, pairs)  11 us
  transfers between devices with their start and end apart: 14, of which 14 were waited for; matrix products, arithmetic and copies ran while one was open for 0% of the time, Pallas kernels for 0%

commit v1 on v0

v1 whole, which is shorter than its diff:
```python
import functools

import jax
import jax.numpy as jnp
from jax import lax
from jax.experimental import pallas as pl
from jax.experimental.pallas import tpu as pltpu
from jax.sharding import PartitionSpec as P

SUM = jnp.float16
PARTS = 16
GROUPS = 4
DEEP = 18
VMEM = pltpu.VMEM
SMEM = pltpu.SMEM
VMEM_LIMIT = 40 * 1024 * 1024


def swap(value, pattern):
    count = lax.axis_size("expert")
    return lax.ppermute(value, "expert", [(i, i ^ pattern) for i in range(count)])


def along(value, pairs):
    groups = lax.axis_size("expert") // PARTS
    return lax.ppermute(value, "expert", [(g * PARTS + a, g * PARTS + b) for g in range(groups) for a, b in pairs])


def shift(value, axis, steps):
    count = lax.axis_size(axis)
    return lax.ppermute(value, axis, [(i, (i + steps) % count) for i in range(count)])


def call(kernel, out_shape, in_spaces, args, scratch=(), after=(), flops=0, moved=0):
    taken = len(args)

    def body(*refs):
        kernel(*refs[:taken], *refs[taken + len(after) :])

    return pl.pallas_call(
        body,
        out_shape=out_shape,
        in_specs=[pl.BlockSpec(memory_space=space) for space in in_spaces + [pl.ANY] * len(after)],
        out_specs=jax.tree.map(lambda _: pl.BlockSpec(memory_space=VMEM), out_shape),
        scratch_shapes=list(scratch),
        compiler_params=pltpu.CompilerParams(vmem_limit_bytes=VMEM_LIMIT),
        cost_estimate=pl.CostEstimate(flops=flops, bytes_accessed=moved, transcendentals=0),
    )(*args, *after)


def route_kernel(cap, place_ref, up_ref, down_ref, ru_ref, rd_ref, gu_ref, gd_ref, capacity_ref,
                 own_ref, sent_ref, across_ref, mask_ref, share_ref):
    slot_refs = {0: own_ref, 1: across_ref.at[0], 2: sent_ref.at[0], 3: sent_ref.at[1]}
    group = place_ref[0]
    tokens = up_ref.shape[1]
    rows = 2 * tokens
    start = pl.multiple_of(group * tokens, tokens)
    routes = jnp.concatenate([ru_ref[:, pl.ds(start, tokens)], rd_ref[:, pl.ds(start, tokens)]], axis=1)
    gates = jnp.concatenate([gu_ref[:, pl.ds(start, tokens)], gd_ref[:, pl.ds(start, tokens)]], axis=1)
    hits, shares = [], []
    for k in range(GROUPS):
        match = routes == (group ^ k)
        hits.append(jnp.sum(jnp.where(match, 1.0, 0.0), axis=0, keepdims=True))
        shares.append(jnp.sum(jnp.where(match, gates, 0.0), axis=0, keepdims=True))
    pad = [jnp.zeros((8 - GROUPS, rows), jnp.float32)]
    hit = jnp.concatenate(hits + pad, axis=0)
    share_ref[...] = jnp.concatenate(shares + pad, axis=0)
    before = lax.broadcasted_iota(jnp.int32, (rows, rows), 0) < lax.broadcasted_iota(jnp.int32, (rows, rows), 1)
    rank = jnp.dot(hit.astype(jnp.bfloat16), jnp.where(before, 1.0, 0.0).astype(jnp.bfloat16),
                   preferred_element_type=jnp.float32)
    block = jnp.concatenate([up_ref[...], down_ref[...]], axis=1)
    slot_ids = lax.broadcasted_iota(jnp.int32, (cap, rows), 0)
    for k in (2, 3, 1, 0):
        limit = capacity_ref[0, group ^ k].astype(jnp.float32)
        kept = (hit[k : k + 1] > 0.5) & (rank[k : k + 1] < limit)
        target = jnp.where(kept, rank[k : k + 1], -1.0).astype(jnp.int32)
        mask = jnp.where(target == slot_ids, 1.0, 0.0).astype(jnp.bfloat16)
        mask_ref[k] = mask
        slot_refs[k][...] = lax.dot_general(
            mask, block, (((1,), (1,)), ((), ())), preferred_element_type=jnp.float32
        ).astype(jnp.bfloat16)


def up_kernel(place_ref, first_ref, second_ref, gate_ref, up_ref, keep_ref, right_ref, left_ref, blocks):
    part = place_ref[1]
    half = first_ref.shape[0]
    x = jnp.concatenate([first_ref[...], second_ref[...]], axis=0)
    for n in range(8):
        column = slice(n * 128, n * 128 + 128)
        for z, ref in enumerate((gate_ref, up_ref)):
            result = jnp.dot(x, ref[:, column], preferred_element_type=jnp.float32)
            blocks[n, :, z * 128 : z * 128 + 128] = result[:half]
            blocks[8 + n, :, z * 128 : z * 128 + 128] = result[half:]
    for n in range(PARTS, DEEP):
        blocks[n] = jnp.zeros_like(blocks[n])
    for offset, ref in enumerate((keep_ref, right_ref, left_ref)):
        first = (part + offset) % 3
        for m in range(6):
            ref[m] = blocks[first + 3 * m]


def down_kernel(place_ref, own_ref, before_ref, behind_ref, edge_ref, down_ref, near_own_ref, near_ref, far_ref, hidden):
    part = place_ref[1]
    half = near_own_ref.shape[0]
    before = jnp.where(part == 0, 2, (part + 2) % 3)
    behind = jnp.where(part == PARTS - 1, 1, (part + 1) % 3)
    first_edge, last_edge = part == 0, part == PARTS - 1
    for kind in range(3):
        first = (part % 3, before, behind)[kind]
        for m in range(6):
            owner = first + 3 * m
            if kind == 0:
                value = own_ref[m]
            elif kind == 1:
                value = jnp.where(first_edge, edge_ref[m], before_ref[m])
            else:
                value = jnp.where(last_edge, edge_ref[m], behind_ref[m])
            column = pl.multiple_of(owner % 8 * 128, 128)
            for chunk in range(2):
                row = pl.multiple_of((owner // 8 * 2 + chunk) * half, 16)
                hidden[pl.ds(row, half), pl.ds(column, 128)] = value[chunk * half : (chunk + 1) * half]
    out = lax.dot_general(hidden[: 4 * half], down_ref[...], (((1,), (1,)), ((), ())),
                          preferred_element_type=jnp.float32).astype(jnp.bfloat16)
    near_own_ref[...] = out[:half]
    far_ref[0] = out[half : 2 * half]
    near_ref[...] = out[2 * half : 3 * half]
    far_ref[1] = out[3 * half :]


def combine_kernel(up_ref, down_ref, mask_ref, share_ref, *refs):
    back_refs, out_up_ref, out_down_ref = refs[:GROUPS], refs[GROUPS], refs[GROUPS + 1]
    tokens = up_ref.shape[1]
    total = jnp.concatenate([up_ref[...], down_ref[...]], axis=1).astype(jnp.float32)
    for k in range(GROUPS):
        placed = lax.dot_general(back_refs[k][...], mask_ref[k], (((0,), (0,)), ((), ())),
                                 preferred_element_type=jnp.float32)
        total = total + share_ref[k : k + 1] * placed
    out_up_ref[...] = total[:, :tokens].astype(jnp.bfloat16)
    out_down_ref[...] = total[:, tokens:].astype(jnp.bfloat16)


RIGHT = [(i, i + 1) for i in range(PARTS - 1)]
LEFT = [(i + 1, i) for i in range(PARTS - 1)]
RIGHT3 = [(i, i + 3) for i in range(PARTS - 3)]
LEFT3 = [(i + 3, i) for i in range(PARTS - 3)]
EDGE = [(0, 2), (PARTS - 1, PARTS - 3)]
EDGE3 = [(0, 6), (1, 7), (2, 8), (15, 9)]
EDGE3_MORE = [(13, 7), (14, 8)]
SWAP9 = [(i, i + 9) for i in range(7)] + [(i + 9, i) for i in range(7)]


def back(pairs):
    return [(b, a) for a, b in pairs]


def sum_chunk(place, first, second, gate_w, up_w, after=()):
    part = place[1]
    half, width = first.shape
    shapes = (jax.ShapeDtypeStruct((6, half, 256), jnp.float32),) * 3
    keep, right, left = call(up_kernel, shapes, [SMEM] + [VMEM] * 4, (place, first, second, gate_w, up_w),
                             scratch=[pltpu.VMEM((DEEP, half, 256), jnp.float32)], after=after,
                             flops=2 * 2 * half * width * 2048, moved=4 * width * 1024)
    right, left = right.astype(SUM), left.astype(SUM)
    got = [along(right, RIGHT), along(left, LEFT), along(jnp.where(part == 0, left, right), EDGE)]
    for value in got:
        keep = keep + value.astype(jnp.float32)
    return keep


def sum_pairs(place, keep):
    part = place[1]
    keep = keep.reshape((2, 3) + keep.shape[1:])

    def of_class(offset):
        return lax.dynamic_index_in_dim(keep, (part // 3 + offset) % 3, 1, keepdims=False)

    right, left = of_class(1).astype(SUM), of_class(2).astype(SUM)
    got = [along(right, RIGHT3), along(left, LEFT3), along(jnp.where(part < 3, left, right), EDGE3),
           along(right, EDGE3_MORE)]
    total = of_class(0)
    for value in got:
        total = total + value.astype(jnp.float32)
    return total


def hidden_blocks(place, total):
    part = place[1]
    upper = part >= 9
    sent = jnp.where(upper, total[0], total[1]).astype(SUM)
    value = jnp.where(upper, total[1], total[0]) + along(sent, SWAP9).astype(jnp.float32)
    own = (jax.nn.silu(value[:, :128]) * value[:, 128:]).astype(jnp.bfloat16)
    other = along(own, SWAP9)
    pair = jnp.stack([jnp.where(upper, other, own), jnp.where(upper, own, other)])
    place3 = part // 3
    before, behind = along(pair, RIGHT3), along(pair, LEFT3)
    edge, edge_more = along(pair, back(EDGE3)), along(pair, back(EDGE3_MORE))
    before = jnp.where(part < 3, edge, before)
    behind = jnp.where(part == 15, edge, jnp.where(part > 12, edge_more, behind))
    cases = []
    for m in range(3):
        offset = (m - place3) % 3
        cases.append(jnp.where(offset == 0, pair, jnp.where(offset == 1, behind, before)))
    third = jnp.stack(cases, axis=1).reshape((6,) + own.shape)
    return third, along(third, RIGHT), along(third, LEFT), along(third, back(EDGE))


def local(held_up, held_down, routes_up, routes_down, gates_up, gates_down, capacity, w_gate, w_up, w_down):
    index = lax.axis_index("expert")
    place = jnp.stack([index // PARTS, index % PARTS]).astype(jnp.int32)
    up_rows, down_rows = held_up[0].T, held_down[0].T
    width, tokens = up_rows.shape
    cap = 8 * max(1, tokens * 5 // 64)
    slot = jax.ShapeDtypeStruct((cap, width), jnp.bfloat16)
    two = jax.ShapeDtypeStruct((2, cap, width), jnp.bfloat16)
    one = jax.ShapeDtypeStruct((1, cap, width), jnp.bfloat16)
    shapes = (slot, two, one, jax.ShapeDtypeStruct((GROUPS, cap, 2 * tokens), jnp.bfloat16),
              jax.ShapeDtypeStruct((8, 2 * tokens), jnp.float32))
    own, sent, across, mask, share = call(
        functools.partial(route_kernel, cap), shapes, [SMEM] + [VMEM] * 6 + [SMEM],
        (place, up_rows, down_rows, routes_up[0].T, routes_down[0].T, gates_up[0].T, gates_down[0].T, capacity),
        flops=2 * 4 * cap * 256 * width, moved=10**6)
    got = swap(sent, 32)
    far = swap(jnp.concatenate([across, got[1:]]), 16)
    near_sums = sum_chunk(place, own, got[0], w_gate[0], w_up[0])
    far_sums = sum_chunk(place, far[0], far[1], w_gate[0], w_up[0], after=(near_sums,))
    sums = sum_pairs(place, jnp.concatenate([near_sums, far_sums], axis=1))
    third = hidden_blocks(place, sums)
    near_own, near, far = call(down_kernel, (slot, slot, two), [SMEM] + [VMEM] * 5, (place, *third, w_down[0]),
                               scratch=[pltpu.VMEM((6 * cap, 1024), jnp.bfloat16)],
                               flops=2 * 4 * cap * width * 1024, moved=2 * width * 1024)
    far = swap(far, 16)
    near = swap(jnp.stack([near, far[1]]), 32)
    back_slots = (near_own, far[0], near[0], near[1])
    rows = jax.ShapeDtypeStruct((width, tokens), jnp.bfloat16)
    out_up, out_down = call(combine_kernel, (rows, rows), [VMEM] * (4 + GROUPS),
                            (up_rows, down_rows, mask, share, *back_slots),
                            flops=2 * 4 * cap * 256 * width, moved=10**6)
    return shift(out_up, "section", 1).T[None], shift(out_down, "section", -1).T[None]


def solution(mesh):
    rows = P("section", None, "expert")
    table = P("section", None, None)
    weight = P("section", "expert", None)
    return jax.shard_map(
        local,
        mesh=mesh,
        in_specs=(rows, rows, table, table, table, table, P("section", None), weight, weight, weight),
        out_specs=(rows, rows),
        check_vma=False,
    )
```

time: 325 us -> 257 us (0.79)
  waiting for transfers between devices: 188 us -> 109 us
  starting transfers between devices: 119 us -> 131 us
  Pallas kernels: 0 us -> 5.77 us
  other arithmetic: 5.02 us -> 1.15 us
  matrix products: 3.44 us -> 0 us
  local copies, waits for them, and re-layouts: 4.67 us -> 7.92 us
    ppermute x14 -> x25, waiting for transfers between devices: 188 us -> 109 us  [the longest x19 67 us: along(): lax.ppermute(value, 'expert', [(g * PARTS + a, g * PARTS + b) for g in ra...]
    ppermute x14 -> x25, starting transfers between devices: 119 us -> 131 us  [the longest x19 69.9 us: along(): lax.ppermute(value, 'expert', [(g * PARTS + a, g * PARTS + b) for g in ra...]
    pallas_call x0 -> x5, Pallas kernels: none -> 5.77 us  [call(): pl.pallas_call(body, out_shape=out_shape, in_specs=[pl.BlockSpec(memory_s...]
    unnamed x14 -> x26, local copies, waits for them, and re-layouts: 2.87 us -> 7.87 us
    dot_general x5 -> x0, matrix products: 3.44 us -> none  [the longest x1 1.22 us: local(): jnp.einsum('rec,rd->ecd', slot_mask.astype(jnp.bfloat16), local_rows, pre...]
  transfers between devices with their start and end apart: 14 -> 25, of which waited for: 14 -> 17; matrix products, arithmetic and copies ran while one was open for 0% -> 0% of each run, Pallas kernels for 0% -> 1%
where the time goes in v1:
time: 257 us; the launch traced here: 256 us
  starting transfers between devices  131 us (51%)
  waiting for transfers between devices  109 us (42%)
  local copies, waits for them, and re-layouts  7.92 us (3%)
  Pallas kernels  5.77 us (2%)
    ppermute x19, starting transfers between devices, along(): lax.ppermute(value, 'expert', [(g * PARTS + a, g * PARTS + b) for g in ra...  69.9 us
    ppermute x19, waiting for transfers between devices, along(): lax.ppermute(value, 'expert', [(g * PARTS + a, g * PARTS + b) for g in ra...  67 us
    ppermute x4, starting transfers between devices, swap(): lax.ppermute(value, 'expert', [(i, i ^ pattern) for i in range(count)])  54.5 us
    ppermute x4, waiting for transfers between devices, swap(): lax.ppermute(value, 'expert', [(i, i ^ pattern) for i in range(count)])  35.5 us
    unnamed x26, local copies, waits for them, and re-layouts  7.87 us
    ppermute x2, starting transfers between devices, shift(): lax.ppermute(value, axis, [(i, (i + steps) % count) for i in range(count)])  6.58 us
    ppermute x2, waiting for transfers between devices, shift(): lax.ppermute(value, axis, [(i, (i + steps) % count) for i in range(count)])  6.28 us
    pallas_call x5, Pallas kernels, call(): pl.pallas_call(body, out_shape=out_shape, in_specs=[pl.BlockSpec(memory_s...  5.77 us
  transfers between devices with their start and end apart: 25, of which 17 were waited for; matrix products, arithmetic and copies ran while one was open for 0% of the time, Pallas kernels for 1%

profile of v1, /device:TPU:7, one launch (start us, length us, event | category | flops | bytes accessed | tf_op | source)
XLA Modules:
  0.0 255.9 jit_solution(5053474103380098930)
XLA Ops:
  7.2 4.8 %collective-permute-start = (bf16[2,80,448]{2,1,0:T(8,128)(2,1)S(1)}, bf16[2,80,448]{2,1,0:T(8,128)(2,1)S(1)}, u32[]{:S(2)}, u32[]{:S(2)}) collective-permute-start(bf16[2,80,448]{2,1,0:T(8,128)(2,1)S(1)} %get-tuple-element.21), channel_id=1, source_target_pairs={{0,32},{1,33},{2,34},{3,35},{4,36},{5,37},{6,38},{7,39},{8,40},{9,... | collective-permute-start | bytes 430088 | tf_op jit(solution)/shard_map/ppermute | solution.py:21
  12.0 3.6 %collective-permute-done = bf16[2,80,448]{2,1,0:T(8,128)(2,1)S(1)} collective-permute-done((bf16[2,80,448]{2,1,0:T(8,128)(2,1)S(1)}, bf16[2,80,448]{2,1,0:T(8,128)(2,1)S(1)}, u32[]{:S(2)}, u32[]{:S(2)}) %collective-permute-start) | collective-permute-done | bytes 143392 | tf_op jit(solution)/shard_map/ppermute | solution.py:21
  15.7 28.7 %collective-permute-start.4 = (bf16[2,80,448]{2,1,0:T(8,128)(2,1)S(1)}, bf16[2,80,448]{2,1,0:T(8,128)(2,1)S(1)}, u32[]{:S(2)}, u32[]{:S(2)}) collective-permute-start(bf16[2,80,448]{2,1,0:T(8,128)(2,1)S(1)} %pad_maximum_fusion.2), channel_id=1, source_target_pairs={{0,16},{1,17},{2,18},{3,19},{4,20},{5,21},{6,22},{7,23},{8,24},{9,... | collective-permute-start | bytes 430088 | tf_op jit(solution)/shard_map/ppermute | solution.py:21
  47.2 2.7 %collective-permute-start.1 = (f16[6,80,256]{2,1,0:T(8,128)(2,1)S(1)}, f16[6,80,256]{2,1,0:T(8,128)(2,1)S(1)}, u32[]{:S(2)}, u32[]{:S(2)}) collective-permute-start(f16[6,80,256]{2,1,0:T(8,128)(2,1)S(1)} %get-tuple-element.44), channel_id=1, source_target_pairs={{0,1},{1,2},{2,3},{3,4},{4,5},{5,6},{6,7},{7,8},{8,9},{9,10},{10,1... | collective-permute-start | bytes 737288 | tf_op jit(solution)/shard_map/ppermute | solution.py:26
  51.2 4.4 %collective-permute-start.3 = (f16[6,80,256]{2,1,0:T(8,128)(2,1)S(1)}, f16[6,80,256]{2,1,0:T(8,128)(2,1)S(1)}, u32[]{:S(2)}, u32[]{:S(2)}) collective-permute-start(f16[6,80,256]{2,1,0:T(8,128)(2,1)S(1)} %get-tuple-element.43), channel_id=1, source_target_pairs={{0,2},{15,13},{16,18},{31,29},{32,34},{47,45},{48,50},{63,61},{64,... | collective-permute-start | bytes 737288 | tf_op jit(solution)/shard_map/ppermute | solution.py:26
  55.7 18.3 %collective-permute-done.1 = f16[6,80,256]{2,1,0:T(8,128)(2,1)S(1)} collective-permute-done((f16[6,80,256]{2,1,0:T(8,128)(2,1)S(1)}, f16[6,80,256]{2,1,0:T(8,128)(2,1)S(1)}, u32[]{:S(2)}, u32[]{:S(2)}) %collective-permute-start.1) | collective-permute-done | bytes 245792 | tf_op jit(solution)/shard_map/ppermute | solution.py:26
  74.0 4.7 %collective-permute-done.2 = f16[6,80,256]{2,1,0:T(8,128)(2,1)S(1)} collective-permute-done((f16[6,80,256]{2,1,0:T(8,128)(2,1)S(1)}, f16[6,80,256]{2,1,0:T(8,128)(2,1)S(1)}, u32[]{:S(2)}, u32[]{:S(2)}) %collective-permute-start.2) | collective-permute-done | bytes 245792 | tf_op jit(solution)/shard_map/ppermute | solution.py:26
  79.4 1.5 shard_map.115
  81.0 2.5 collective-permute-start.5
  84.8 6.5 %collective-permute-start.7 = (f16[6,80,256]{2,1,0:T(8,128)(2,1)S(1)}, f16[6,80,256]{2,1,0:T(8,128)(2,1)S(1)}, u32[]{:S(2)}, u32[]{:S(2)}) collective-permute-start(f16[6,80,256]{2,1,0:T(8,128)(2,1)S(1)} %get-tuple-element.40), channel_id=1, source_target_pairs={{0,2},{15,13},{16,18},{31,29},{32,34},{47,45},{48,50},{63,61},{64,... | collective-permute-start | bytes 737288 | tf_op jit(solution)/shard_map/ppermute | solution.py:26
  91.4 2.4 collective-permute-done.6
  93.8 1.7 collective-permute-done.7
  95.8 3.3 %collective-permute-start.10 = (f16[2,160,256]{2,1,0:T(8,128)(2,1)S(1)}, f16[2,160,256]{2,1,0:T(8,128)(2,1)S(1)}, u32[]{:S(2)}, u32[]{:S(2)}) collective-permute-start(f16[2,160,256]{2,1,0:T(8,128)(2,1)S(1)} %get-tuple-element.37), channel_id=1, source_target_pairs={{0,6},{1,7},{2,8},{15,9},{16,22},{17,23},{18,24},{31,25},{32,38},{... | collective-permute-start | bytes 491528 | tf_op jit(solution)/shard_map/ppermute | solution.py:26
  102.5 2.7 %collective-permute-done.8 = f16[2,160,256]{2,1,0:T(8,128)(2,1)S(1)} collective-permute-done((f16[2,160,256]{2,1,0:T(8,128)(2,1)S(1)}, f16[2,160,256]{2,1,0:T(8,128)(2,1)S(1)}, u32[]{:S(2)}, u32[]{:S(2)}) %collective-permute-start.8) | collective-permute-done | bytes 163872 | tf_op jit(solution)/shard_map/ppermute | solution.py:26
  105.2 3.8 %collective-permute-done.9 = f16[2,160,256]{2,1,0:T(8,128)(2,1)S(1)} collective-permute-done((f16[2,160,256]{2,1,0:T(8,128)(2,1)S(1)}, f16[2,160,256]{2,1,0:T(8,128)(2,1)S(1)}, u32[]{:S(2)}, u32[]{:S(2)}) %collective-permute-start.9) | collective-permute-done | bytes 163872 | tf_op jit(solution)/shard_map/ppermute | solution.py:26
  109.1 13.5 %collective-permute-start.12 = (f16[160,256]{1,0:T(8,128)(2,1)S(1)}, f16[160,256]{1,0:T(8,128)(2,1)S(1)}, u32[]{:S(2)}, u32[]{:S(2)}) collective-permute-start(f16[160,256]{1,0:T(8,128)(2,1)S(1)} %fusion.5), channel_id=1, source_target_pairs={{0,9},{1,10},{2,11},{3,12},{4,13},{5,14},{6,15},{9,0},{10,1},{11,2... | collective-permute-start | bytes 245768 | tf_op jit(solution)/shard_map/ppermute | solution.py:26
  122.6 10.0 %collective-permute-done.12 = f16[160,256]{1,0:T(8,128)(2,1)S(1)} collective-permute-done((f16[160,256]{1,0:T(8,128)(2,1)S(1)}, f16[160,256]{1,0:T(8,128)(2,1)S(1)}, u32[]{:S(2)}, u32[]{:S(2)}) %collective-permute-start.12) | collective-permute-done | bytes 81952 | tf_op jit(solution)/shard_map/ppermute | solution.py:26
  132.6 5.0 %collective-permute-start.13 = (bf16[160,128]{1,0:T(8,128)(2,1)S(1)}, bf16[160,128]{1,0:T(8,128)(2,1)S(1)}, u32[]{:S(2)}, u32[]{:S(2)}) collective-permute-start(bf16[160,128]{1,0:T(8,128)(2,1)S(1)} %fusion.6), channel_id=1, source_target_pairs={{0,9},{1,10},{2,11},{3,12},{4,13},{5,14},{6,15},{9,0},{10,1},{11,2... | collective-permute-start | bytes 122888 | tf_op jit(solution)/shard_map/ppermute | solution.py:26
  137.7 9.3 %collective-permute-done.13 = bf16[160,128]{1,0:T(8,128)(2,1)S(1)} collective-permute-done((bf16[160,128]{1,0:T(8,128)(2,1)S(1)}, bf16[160,128]{1,0:T(8,128)(2,1)S(1)}, u32[]{:S(2)}, u32[]{:S(2)}) %collective-permute-start.13) | collective-permute-done | bytes 40992 | tf_op jit(solution)/shard_map/ppermute | solution.py:26
  150.5 5.8 %collective-permute-start.17 = (bf16[2,160,128]{2,1,0:T(8,128)(2,1)S(1)}, bf16[2,160,128]{2,1,0:T(8,128)(2,1)S(1)}, u32[]{:S(2)}, u32[]{:S(2)}) collective-permute-start(bf16[2,160,128]{2,1,0:T(8,128)(2,1)S(1)} %pad_maximum_fusion.4), channel_id=1, source_target_pairs={{0,3},{1,4},{2,5},{3,6},{4,7},{5,8},{6,9},{7,10},{8,11},{9,12},{10... | collective-permute-start | bytes 245768 | tf_op jit(solution)/shard_map/ppermute | solution.py:26
  156.4 2.2 collective-permute-done.14
  158.7 14.4 %collective-permute-start.18 = (bf16[6,160,128]{2,1,0:T(8,128)(2,1)S(1)}, bf16[6,160,128]{2,1,0:T(8,128)(2,1)S(1)}, u32[]{:S(2)}, u32[]{:S(2)}) collective-permute-start(bf16[6,160,128]{2,1,0:T(8,128)(2,1)S(1)} %bitcast.90), channel_id=1, source_target_pairs={{0,1},{1,2},{2,3},{3,4},{4,5},{5,6},{6,7},{7,8},{8,9},{9,10},{10,1... | collective-permute-start | bytes 737288 | tf_op jit(solution)/shard_map/ppermute | solution.py:26
  175.7 2.2 collective-permute-done.18.refs_2_
  177.8 3.8 %collective-permute-done.19.refs_3_ = bf16[6,160,128]{2,1,0:T(8,128)(2,1)S(1)} collective-permute-done((bf16[6,160,128]{2,1,0:T(8,128)(2,1)S(1)}, bf16[6,160,128]{2,1,0:T(8,128)(2,1)S(1)}, u32[]{:S(2)}, u32[]{:S(2)}) %collective-permute-start.19) | collective-permute-done | bytes 245792 | tf_op jit(solution)/shard_map/ppermute | solution.py:26
  181.7 5.4 %collective-permute-done.20.refs_4_ = bf16[6,160,128]{2,1,0:T(8,128)(2,1)S(1)} collective-permute-done((bf16[6,160,128]{2,1,0:T(8,128)(2,1)S(1)}, bf16[6,160,128]{2,1,0:T(8,128)(2,1)S(1)}, u32[]{:S(2)}, u32[]{:S(2)}) %collective-permute-start.20) | collective-permute-done | bytes 245792 | tf_op jit(solution)/shard_map/ppermute | solution.py:26
  188.3 16.1 %collective-permute-start.21 = (bf16[2,80,448]{2,1,0:T(8,128)(2,1)S(1)}, bf16[2,80,448]{2,1,0:T(8,128)(2,1)S(1)}, u32[]{:S(2)}, u32[]{:S(2)}) collective-permute-start(bf16[2,80,448]{2,1,0:T(8,128)(2,1)S(1)} %get-tuple-element.30), channel_id=1, source_target_pairs={{0,16},{1,17},{2,18},{3,19},{4,20},{5,21},{6,22},{7,23},{8,24},{9,... | collective-permute-start | bytes 430088 | tf_op jit(solution)/shard_map/ppermute | solution.py:21
  204.4 28.3 %collective-permute-done.21 = bf16[2,80,448]{2,1,0:T(8,128)(2,1)S(1)} collective-permute-done((bf16[2,80,448]{2,1,0:T(8,128)(2,1)S(1)}, bf16[2,80,448]{2,1,0:T(8,128)(2,1)S(1)}, u32[]{:S(2)}, u32[]{:S(2)}) %collective-permute-start.21) | collective-permute-done | bytes 143392 | tf_op jit(solution)/shard_map/ppermute | solution.py:21
  232.8 4.9 %collective-permute-start.22 = (bf16[2,80,448]{2,1,0:T(8,128)(2,1)S(1)}, bf16[2,80,448]{2,1,0:T(8,128)(2,1)S(1)}, u32[]{:S(2)}, u32[]{:S(2)}) collective-permute-start(bf16[2,80,448]{2,1,0:T(8,128)(2,1)S(1)} %pad_maximum_fusion.3), channel_id=1, source_target_pairs={{0,32},{1,33},{2,34},{3,35},{4,36},{5,37},{6,38},{7,39},{8,40},{9,... | collective-permute-start | bytes 430088 | tf_op jit(solution)/shard_map/ppermute | solution.py:21
  237.7 3.6 %collective-permute-done.22 = bf16[2,80,448]{2,1,0:T(8,128)(2,1)S(1)} collective-permute-done((bf16[2,80,448]{2,1,0:T(8,128)(2,1)S(1)}, bf16[2,80,448]{2,1,0:T(8,128)(2,1)S(1)}, u32[]{:S(2)}, u32[]{:S(2)}) %collective-permute-start.22) | collective-permute-done | bytes 143392 | tf_op jit(solution)/shard_map/ppermute | solution.py:21
  241.8 4.7 %collective-permute-start.23 = (bf16[448,128]{1,0:T(8,128)(2,1)S(1)}, bf16[448,128]{1,0:T(8,128)(2,1)S(1)}, u32[]{:S(2)}, u32[]{:S(2)}) collective-permute-start(bf16[448,128]{1,0:T(8,128)(2,1)S(1)} %get-tuple-element.32), channel_id=1, source_target_pairs={{0,64},{64,128},{128,192},{192,256},{256,320},{320,384},{384,448},... | collective-permute-start | bytes 344072 | tf_op jit(solution)/shard_map/ppermute | solution.py:31
  246.4 1.9 collective-permute-start.24
  248.4 6.3 %collective-permute-done.24 = bf16[448,128]{1,0:T(8,128)(2,1)S(1)} collective-permute-done((bf16[448,128]{1,0:T(8,128)(2,1)S(1)}, bf16[448,128]{1,0:T(8,128)(2,1)S(1)}, u32[]{:S(2)}, u32[]{:S(2)}) %collective-permute-start.24) | collective-permute-done | bytes 114720 | tf_op jit(solution)/shard_map/ppermute | solution.py:31
  (71 shorter events, 25.8 us)
Async XLA Ops:
  0.6 43.8 %copy-start = (bf16[1,448,1024]{2,1,0:T(8,128)(2,1)S(1)}, bf16[1,448,1024]{2,1,0:T(8,128)(2,1)}, u32[]{:S(2)}) copy-start(bf16[1,448,1024]{2,1,0:T(8,128)(2,1)} %param.17) | copy-start | bytes 2752516
  0.7 1.0 copy-start.3
  1.7 0.9 copy-start.5
  7.2 8.5 %collective-permute-start = (bf16[2,80,448]{2,1,0:T(8,128)(2,1)S(1)}, bf16[2,80,448]{2,1,0:T(8,128)(2,1)S(1)}, u32[]{:S(2)}, u32[]{:S(2)}) collective-permute-start(bf16[2,80,448]{2,1,0:T(8,128)(2,1)S(1)} %get-tuple-element.21), channel_id=1, source_target_pairs={{0,32},{1,33},{2,34},{3,35},{4,36},{5,37},{6,38},{7,39},{8,40},{9,... | collective-permute-start | bytes 430088 | tf_op jit(solution)/shard_map/ppermute | solution.py:21
  15.7 39.9 %collective-permute-start.4 = (bf16[2,80,448]{2,1,0:T(8,128)(2,1)S(1)}, bf16[2,80,448]{2,1,0:T(8,128)(2,1)S(1)}, u32[]{:S(2)}, u32[]{:S(2)}) collective-permute-start(bf16[2,80,448]{2,1,0:T(8,128)(2,1)S(1)} %pad_maximum_fusion.2), channel_id=1, source_target_pairs={{0,16},{1,17},{2,18},{3,19},{4,20},{5,21},{6,22},{7,23},{8,24},{9,... | collective-permute-start | bytes 430088 | tf_op jit(solution)/shard_map/ppermute | solution.py:21
  44.4 1.2 copy-start.1
  47.2 26.8 %collective-permute-start.1 = (f16[6,80,256]{2,1,0:T(8,128)(2,1)S(1)}, f16[6,80,256]{2,1,0:T(8,128)(2,1)S(1)}, u32[]{:S(2)}, u32[]{:S(2)}) collective-permute-start(f16[6,80,256]{2,1,0:T(8,128)(2,1)S(1)} %get-tuple-element.44), channel_id=1, source_target_pairs={{0,1},{1,2},{2,3},{3,4},{4,5},{5,6},{6,7},{7,8},{8,9},{9,10},{10,1... | collective-permute-start | bytes 737288 | tf_op jit(solution)/shard_map/ppermute | solution.py:26
  49.9 28.8 %collective-permute-start.2 = (f16[6,80,256]{2,1,0:T(8,128)(2,1)S(1)}, f16[6,80,256]{2,1,0:T(8,128)(2,1)S(1)}, u32[]{:S(2)}, u32[]{:S(2)}) collective-permute-start(f16[6,80,256]{2,1,0:T(8,128)(2,1)S(1)} %get-tuple-element.45), channel_id=1, source_target_pairs={{1,0},{2,1},{3,2},{4,3},{5,4},{6,5},{7,6},{8,7},{9,8},{10,9},{11,1... | collective-permute-start | bytes 737288 | tf_op jit(solution)/shard_map/ppermute | solution.py:26
  51.2 28.1 %collective-permute-start.3 = (f16[6,80,256]{2,1,0:T(8,128)(2,1)S(1)}, f16[6,80,256]{2,1,0:T(8,128)(2,1)S(1)}, u32[]{:S(2)}, u32[]{:S(2)}) collective-permute-start(f16[6,80,256]{2,1,0:T(8,128)(2,1)S(1)} %get-tuple-element.43), channel_id=1, source_target_pairs={{0,2},{15,13},{16,18},{31,29},{32,34},{47,45},{48,50},{63,61},{64,... | collective-permute-start | bytes 737288 | tf_op jit(solution)/shard_map/ppermute | solution.py:26
  81.0 10.4 %collective-permute-start.5 = (f16[6,80,256]{2,1,0:T(8,128)(2,1)S(1)}, f16[6,80,256]{2,1,0:T(8,128)(2,1)S(1)}, u32[]{:S(2)}, u32[]{:S(2)}) collective-permute-start(f16[6,80,256]{2,1,0:T(8,128)(2,1)S(1)} %get-tuple-element.41), channel_id=1, source_target_pairs={{0,1},{1,2},{2,3},{3,4},{4,5},{5,6},{6,7},{7,8},{8,9},{9,10},{10,1... | collective-permute-start | bytes 737288 | tf_op jit(solution)/shard_map/ppermute | solution.py:26
  83.5 10.2 %collective-permute-start.6 = (f16[6,80,256]{2,1,0:T(8,128)(2,1)S(1)}, f16[6,80,256]{2,1,0:T(8,128)(2,1)S(1)}, u32[]{:S(2)}, u32[]{:S(2)}) collective-permute-start(f16[6,80,256]{2,1,0:T(8,128)(2,1)S(1)} %get-tuple-element.42), channel_id=1, source_target_pairs={{1,0},{2,1},{3,2},{4,3},{5,4},{6,5},{7,6},{8,7},{9,8},{10,9},{11,1... | collective-permute-start | bytes 737288 | tf_op jit(solution)/shard_map/ppermute | solution.py:26
  84.8 10.7 %collective-permute-start.7 = (f16[6,80,256]{2,1,0:T(8,128)(2,1)S(1)}, f16[6,80,256]{2,1,0:T(8,128)(2,1)S(1)}, u32[]{:S(2)}, u32[]{:S(2)}) collective-permute-start(f16[6,80,256]{2,1,0:T(8,128)(2,1)S(1)} %get-tuple-element.40), channel_id=1, source_target_pairs={{0,2},{15,13},{16,18},{31,29},{32,34},{47,45},{48,50},{63,61},{64,... | collective-permute-start | bytes 737288 | tf_op jit(solution)/shard_map/ppermute | solution.py:26
  95.8 6.6 %collective-permute-start.10 = (f16[2,160,256]{2,1,0:T(8,128)(2,1)S(1)}, f16[2,160,256]{2,1,0:T(8,128)(2,1)S(1)}, u32[]{:S(2)}, u32[]{:S(2)}) collective-permute-start(f16[2,160,256]{2,1,0:T(8,128)(2,1)S(1)} %get-tuple-element.37), channel_id=1, source_target_pairs={{0,6},{1,7},{2,8},{15,9},{16,22},{17,23},{18,24},{31,25},{32,38},{... | collective-permute-start | bytes 491528 | tf_op jit(solution)/shard_map/ppermute | solution.py:26
  99.1 3.3 %collective-permute-start.11 = (f16[2,160,256]{2,1,0:T(8,128)(2,1)S(1)}, f16[2,160,256]{2,1,0:T(8,128)(2,1)S(1)}, u32[]{:S(2)}, u32[]{:S(2)}) collective-permute-start(f16[2,160,256]{2,1,0:T(8,128)(2,1)S(1)} %get-tuple-element.39), channel_id=1, source_target_pairs={{13,7},{14,8},{29,23},{30,24},{45,39},{46,40},{61,55},{62,56},{77,... | collective-permute-start | bytes 491528 | tf_op jit(solution)/shard_map/ppermute | solution.py:26
  99.8 5.4 %collective-permute-start.8 = (f16[2,160,256]{2,1,0:T(8,128)(2,1)S(1)}, f16[2,160,256]{2,1,0:T(8,128)(2,1)S(1)}, u32[]{:S(2)}, u32[]{:S(2)}) collective-permute-start(f16[2,160,256]{2,1,0:T(8,128)(2,1)S(1)} %get-tuple-element.39), channel_id=1, source_target_pairs={{0,3},{1,4},{2,5},{3,6},{4,7},{5,8},{6,9},{7,10},{8,11},{9,12},{10... | collective-permute-start | bytes 491528 | tf_op jit(solution)/shard_map/ppermute | solution.py:26
  101.1 7.9 %collective-permute-start.9 = (f16[2,160,256]{2,1,0:T(8,128)(2,1)S(1)}, f16[2,160,256]{2,1,0:T(8,128)(2,1)S(1)}, u32[]{:S(2)}, u32[]{:S(2)}) collective-permute-start(f16[2,160,256]{2,1,0:T(8,128)(2,1)S(1)} %get-tuple-element.38), channel_id=1, source_target_pairs={{3,0},{4,1},{5,2},{6,3},{7,4},{8,5},{9,6},{10,7},{11,8},{12,9},{13... | collective-permute-start | bytes 491528 | tf_op jit(solution)/shard_map/ppermute | solution.py:26
  109.1 23.4 %collective-permute-start.12 = (f16[160,256]{1,0:T(8,128)(2,1)S(1)}, f16[160,256]{1,0:T(8,128)(2,1)S(1)}, u32[]{:S(2)}, u32[]{:S(2)}) collective-permute-start(f16[160,256]{1,0:T(8,128)(2,1)S(1)} %fusion.5), channel_id=1, source_target_pairs={{0,9},{1,10},{2,11},{3,12},{4,13},{5,14},{6,15},{9,0},{10,1},{11,2... | collective-permute-start | bytes 245768 | tf_op jit(solution)/shard_map/ppermute | solution.py:26
  132.6 14.4 %collective-permute-start.13 = (bf16[160,128]{1,0:T(8,128)(2,1)S(1)}, bf16[160,128]{1,0:T(8,128)(2,1)S(1)}, u32[]{:S(2)}, u32[]{:S(2)}) collective-permute-start(bf16[160,128]{1,0:T(8,128)(2,1)S(1)} %fusion.6), channel_id=1, source_target_pairs={{0,9},{1,10},{2,11},{3,12},{4,13},{5,14},{6,15},{9,0},{10,1},{11,2... | collective-permute-start | bytes 122888 | tf_op jit(solution)/shard_map/ppermute | solution.py:26
  147.1 40.0 %copy-start.2 = (bf16[1,448,1024]{2,1,0:T(8,128)(2,1)S(1)}, bf16[1,448,1024]{2,1,0:T(8,128)(2,1)}, u32[]{:S(2)}) copy-start(bf16[1,448,1024]{2,1,0:T(8,128)(2,1)} %param.19) | copy-start | bytes 2752516
  147.1 11.5 %collective-permute-start.14 = (bf16[2,160,128]{2,1,0:T(8,128)(2,1)S(1)}, bf16[2,160,128]{2,1,0:T(8,128)(2,1)S(1)}, u32[]{:S(2)}, u32[]{:S(2)}) collective-permute-start(bf16[2,160,128]{2,1,0:T(8,128)(2,1)S(1)} %pad_maximum_fusion.4), channel_id=1, source_target_pairs={{6,0},{7,1},{8,2},{9,15},{22,16},{23,17},{24,18},{25,31},{38,32},{... | collective-permute-start | bytes 245768 | tf_op jit(solution)/shard_map/ppermute | solution.py:26
  148.5 10.0 %collective-permute-start.15 = (bf16[2,160,128]{2,1,0:T(8,128)(2,1)S(1)}, bf16[2,160,128]{2,1,0:T(8,128)(2,1)S(1)}, u32[]{:S(2)}, u32[]{:S(2)}) collective-permute-start(bf16[2,160,128]{2,1,0:T(8,128)(2,1)S(1)} %pad_maximum_fusion.4), channel_id=1, source_target_pairs={{7,13},{8,14},{23,29},{24,30},{39,45},{40,46},{55,61},{56,62},{71,... | collective-permute-start | bytes 245768 | tf_op jit(solution)/shard_map/ppermute | solution.py:26
  149.2 9.4 %collective-permute-start.16 = (bf16[2,160,128]{2,1,0:T(8,128)(2,1)S(1)}, bf16[2,160,128]{2,1,0:T(8,128)(2,1)S(1)}, u32[]{:S(2)}, u32[]{:S(2)}) collective-permute-start(bf16[2,160,128]{2,1,0:T(8,128)(2,1)S(1)} %pad_maximum_fusion.4), channel_id=1, source_target_pairs={{3,0},{4,1},{5,2},{6,3},{7,4},{8,5},{9,6},{10,7},{11,8},{12,9},{13... | collective-permute-start | bytes 245768 | tf_op jit(solution)/shard_map/ppermute | solution.py:26
  150.5 8.1 %collective-permute-start.17 = (bf16[2,160,128]{2,1,0:T(8,128)(2,1)S(1)}, bf16[2,160,128]{2,1,0:T(8,128)(2,1)S(1)}, u32[]{:S(2)}, u32[]{:S(2)}) collective-permute-start(bf16[2,160,128]{2,1,0:T(8,128)(2,1)S(1)} %pad_maximum_fusion.4), channel_id=1, source_target_pairs={{0,3},{1,4},{2,5},{3,6},{4,7},{5,8},{6,9},{7,10},{8,11},{9,12},{10... | collective-permute-start | bytes 245768 | tf_op jit(solution)/shard_map/ppermute | solution.py:26
  158.7 19.2 %collective-permute-start.18 = (bf16[6,160,128]{2,1,0:T(8,128)(2,1)S(1)}, bf16[6,160,128]{2,1,0:T(8,128)(2,1)S(1)}, u32[]{:S(2)}, u32[]{:S(2)}) collective-permute-start(bf16[6,160,128]{2,1,0:T(8,128)(2,1)S(1)} %bitcast.90), channel_id=1, source_target_pairs={{0,1},{1,2},{2,3},{3,4},{4,5},{5,6},{6,7},{7,8},{8,9},{9,10},{10,1... | collective-permute-start | bytes 737288 | tf_op jit(solution)/shard_map/ppermute | solution.py:26
  173.1 8.6 %collective-permute-start.19 = (bf16[6,160,128]{2,1,0:T(8,128)(2,1)S(1)}, bf16[6,160,128]{2,1,0:T(8,128)(2,1)S(1)}, u32[]{:S(2)}, u32[]{:S(2)}) collective-permute-start(bf16[6,160,128]{2,1,0:T(8,128)(2,1)S(1)} %bitcast.91), channel_id=1, source_target_pairs={{1,0},{2,1},{3,2},{4,3},{5,4},{6,5},{7,6},{8,7},{9,8},{10,9},{11,1... | collective-permute-start | bytes 737288 | tf_op jit(solution)/shard_map/ppermute | solution.py:26
  174.4 12.7 %collective-permute-start.20 = (bf16[6,160,128]{2,1,0:T(8,128)(2,1)S(1)}, bf16[6,160,128]{2,1,0:T(8,128)(2,1)S(1)}, u32[]{:S(2)}, u32[]{:S(2)}) collective-permute-start(bf16[6,160,128]{2,1,0:T(8,128)(2,1)S(1)} %bitcast.92), channel_id=1, source_target_pairs={{2,0},{13,15},{18,16},{29,31},{34,32},{45,47},{50,48},{61,63},{66,... | collective-permute-start | bytes 737288 | tf_op jit(solution)/shard_map/ppermute | solution.py:26
  188.3 44.4 %collective-permute-start.21 = (bf16[2,80,448]{2,1,0:T(8,128)(2,1)S(1)}, bf16[2,80,448]{2,1,0:T(8,128)(2,1)S(1)}, u32[]{:S(2)}, u32[]{:S(2)}) collective-permute-start(bf16[2,80,448]{2,1,0:T(8,128)(2,1)S(1)} %get-tuple-element.30), channel_id=1, source_target_pairs={{0,16},{1,17},{2,18},{3,19},{4,20},{5,21},{6,22},{7,23},{8,24},{9,... | collective-permute-start | bytes 430088 | tf_op jit(solution)/shard_map/ppermute | solution.py:21
  232.8 8.5 %copy-start.4 = (bf16[1,128,448]{1,2,0:T(8,128)(2,1)S(1)}, bf16[1,128,448]{1,2,0:T(8,128)(2,1)}, u32[]{:S(2)}) copy-start(bf16[1,128,448]{1,2,0:T(8,128)(2,1)} %param.10) | copy-start | bytes 344068
  232.8 8.5 %copy-start.6 = (bf16[1,128,448]{1,2,0:T(8,128)(2,1)S(1)}, bf16[1,128,448]{1,2,0:T(8,128)(2,1)}, u32[]{:S(2)}) copy-start(bf16[1,128,448]{1,2,0:T(8,128)(2,1)} %param.11) | copy-start | bytes 344068
  232.8 8.5 %collective-permute-start.22 = (bf16[2,80,448]{2,1,0:T(8,128)(2,1)S(1)}, bf16[2,80,448]{2,1,0:T(8,128)(2,1)S(1)}, u32[]{:S(2)}, u32[]{:S(2)}) collective-permute-start(bf16[2,80,448]{2,1,0:T(8,128)(2,1)S(1)} %pad_maximum_fusion.3), channel_id=1, source_target_pairs={{0,32},{1,33},{2,34},{3,35},{4,36},{5,37},{6,38},{7,39},{8,40},{9,... | collective-permute-start | bytes 430088 | tf_op jit(solution)/shard_map/ppermute | solution.py:21
  241.8 6.6 %collective-permute-start.23 = (bf16[448,128]{1,0:T(8,128)(2,1)S(1)}, bf16[448,128]{1,0:T(8,128)(2,1)S(1)}, u32[]{:S(2)}, u32[]{:S(2)}) collective-permute-start(bf16[448,128]{1,0:T(8,128)(2,1)S(1)} %get-tuple-element.32), channel_id=1, source_target_pairs={{0,64},{64,128},{128,192},{192,256},{256,320},{320,384},{384,448},... | collective-permute-start | bytes 344072 | tf_op jit(solution)/shard_map/ppermute | solution.py:31
  246.4 8.2 %collective-permute-start.24 = (bf16[448,128]{1,0:T(8,128)(2,1)S(1)}, bf16[448,128]{1,0:T(8,128)(2,1)S(1)}, u32[]{:S(2)}, u32[]{:S(2)}) collective-permute-start(bf16[448,128]{1,0:T(8,128)(2,1)S(1)} %get-tuple-element.33), channel_id=1, source_target_pairs={{0,960},{64,0},{128,64},{192,128},{256,192},{320,256},{384,320},{4... | collective-permute-start | bytes 344072 | tf_op jit(solution)/shard_map/ppermute | solution.py:31
  (5 other events, 3.5 us)

commit v2 on v1

v2 whole, which is shorter than its diff:
```python
import functools

import jax
import jax.numpy as jnp
from jax import lax
from jax.experimental import pallas as pl
from jax.experimental.pallas import tpu as pltpu
from jax.sharding import PartitionSpec as P

SUM = jnp.float16
PARTS = 16
GROUPS = 4
VMEM = pltpu.VMEM
SMEM = pltpu.SMEM
VMEM_LIMIT = 40 * 1024 * 1024


NEAR = 4


def quads():
    count = lax.axis_size("expert")
    return [list(range(first, first + NEAR)) for first in range(0, count, NEAR)]


def swap(value, pattern):
    count = lax.axis_size("expert")
    return lax.ppermute(value, "expert", [(i, i ^ pattern) for i in range(count)])


def shift(value, axis, steps):
    count = lax.axis_size(axis)
    return lax.ppermute(value, axis, [(i, (i + steps) % count) for i in range(count)])


def call(kernel, out_shape, in_spaces, args, scratch=(), after=(), vmem=VMEM_LIMIT, flops=0, moved=0):
    taken = len(args)

    def body(*refs):
        kernel(*refs[:taken], *refs[taken + len(after) :])

    return pl.pallas_call(
        body,
        out_shape=out_shape,
        in_specs=[pl.BlockSpec(memory_space=space) for space in in_spaces + [pl.ANY] * len(after)],
        out_specs=jax.tree.map(lambda _: pl.BlockSpec(memory_space=VMEM), out_shape),
        scratch_shapes=list(scratch),
        compiler_params=pltpu.CompilerParams(vmem_limit_bytes=vmem),
        cost_estimate=pl.CostEstimate(flops=flops, bytes_accessed=moved, transcendentals=0),
    )(*args, *after)


def pack(first, second, ref):
    for n in range(3):
        ref[n] = first[:, n * 128 : n * 128 + 128]
        ref[3 + n] = second[:, n * 128 : n * 128 + 128]
    ref[6] = jnp.concatenate([first[:, 384:], second[:, 384:]], axis=1)


def unpack(ref):
    last = ref[6]
    return (jnp.concatenate([ref[0], ref[1], ref[2], last[:, :64]], axis=1),
            jnp.concatenate([ref[3], ref[4], ref[5], last[:, 64:]], axis=1))


def route_kernel(cap, place_ref, up_ref, down_ref, ru_ref, rd_ref, gu_ref, gd_ref, capacity_ref,
                 own_ref, sent_ref, across_ref, mask_ref, share_ref, slots):
    group = place_ref[0]
    tokens = up_ref.shape[1]
    rows = 2 * tokens
    start = pl.multiple_of(group * tokens, tokens)
    routes = jnp.concatenate([ru_ref[:, pl.ds(start, tokens)], rd_ref[:, pl.ds(start, tokens)]], axis=1)
    gates = jnp.concatenate([gu_ref[:, pl.ds(start, tokens)], gd_ref[:, pl.ds(start, tokens)]], axis=1)
    hits, shares = [], []
    for e in range(GROUPS):
        match = routes == e
        hits.append(jnp.sum(jnp.where(match, 1.0, 0.0), axis=0, keepdims=True))
        shares.append(jnp.sum(jnp.where(match, gates, 0.0), axis=0, keepdims=True))
    pad = [jnp.zeros((8 - GROUPS, rows), jnp.float32)]
    hit = jnp.concatenate(hits + pad, axis=0)
    share_ref[...] = jnp.concatenate(shares + pad, axis=0)
    before = lax.broadcasted_iota(jnp.int32, (rows, rows), 0) < lax.broadcasted_iota(jnp.int32, (rows, rows), 1)
    rank = jnp.dot(hit.astype(jnp.bfloat16), jnp.where(before, 1.0, 0.0).astype(jnp.bfloat16),
                   preferred_element_type=jnp.float32)
    block = jnp.concatenate([up_ref[...], down_ref[...]], axis=1)
    slot_ids = lax.broadcasted_iota(jnp.int32, (cap, rows), 0)
    for e in range(GROUPS):
        limit = capacity_ref[0, e].astype(jnp.float32)
        kept = (hit[e : e + 1] > 0.5) & (rank[e : e + 1] < limit)
        target = jnp.where(kept, rank[e : e + 1], -1.0).astype(jnp.int32)
        mask = jnp.where(target == slot_ids, 1.0, 0.0).astype(jnp.bfloat16)
        mask_ref[e] = mask
        slots[group ^ e] = lax.dot_general(
            mask, block, (((1,), (1,)), ((), ())), preferred_element_type=jnp.float32
        ).astype(jnp.bfloat16)
    own_ref[...] = slots[0]
    pack(slots[1], jnp.zeros_like(slots[1]), across_ref)
    pack(slots[2], slots[3], sent_ref)


def up_kernel(far, place_ref, *refs):
    part = place_ref[1]
    if far:
        packed_ref, gate_ref, up_ref, out_ref = refs
        first, second = unpack(packed_ref)
    else:
        own_ref, packed_ref, across_ref, gate_ref, up_ref, out_ref, message_ref = refs
        first, second = own_ref[...], unpack(packed_ref)[0]
        message_ref[:3] = across_ref[:3]
        message_ref[3:6] = packed_ref[3:6]
        message_ref[6] = jnp.concatenate([across_ref[6][:, :64], packed_ref[6][:, 64:]], axis=1)
    half = first.shape[0]
    x = jnp.concatenate([first, second], axis=0)
    upper = part // 8 == 1
    for q in range(NEAR):
        for differs in range(2):
            start = pl.multiple_of(((differs ^ (part // 4 % 2)) * NEAR + q) * 128, 128)
            for z, ref in enumerate((gate_ref, up_ref)):
                result = jnp.dot(x, ref[:, pl.ds(start, 128)], preferred_element_type=jnp.float32)
                one, two = result[:half], result[half:]
                out_ref[q, differs * 2, :, z * 128 : z * 128 + 128] = jnp.where(upper, two, one)
                out_ref[q, differs * 2 + 1, :, z * 128 : z * 128 + 128] = jnp.where(upper, one, two)


def hidden_kernel(sums_ref, out_ref):
    value = sums_ref[...]
    out_ref[...] = (jax.nn.silu(value[:, :128]) * value[:, 128:]).astype(jnp.bfloat16)


def down_kernel(place_ref, blocks_ref, down_ref, own_ref, beside_ref, packed_ref, hidden):
    part = place_ref[1]
    cap = own_ref.shape[0]
    for q in range(NEAR):
        for n in range(NEAR):
            row = pl.multiple_of(((n % 2) ^ (part // 8)) * 2 * cap, 16)
            column = pl.multiple_of((((n // 2) ^ (part // 4 % 2)) * NEAR + q) * 128, 128)
            hidden[pl.ds(row, 2 * cap), pl.ds(column, 128)] = blocks_ref[q, n]
    out = lax.dot_general(hidden[...], down_ref[...], (((1,), (1,)), ((), ())),
                          preferred_element_type=jnp.float32).astype(jnp.bfloat16)
    pack(out[cap : 2 * cap], out[3 * cap :], packed_ref)
    own_ref[...] = out[:cap]
    beside = out[2 * cap : 3 * cap]
    for n in range(3):
        beside_ref[n] = beside[:, n * 128 : n * 128 + 128]
    beside_ref[3] = jnp.concatenate([beside[:, 384:]] * 2, axis=1)


def combine_kernel(place_ref, up_ref, down_ref, mask_ref, share_ref, own_ref, beside_ref, packed_ref,
                   out_up_ref, out_down_ref):
    group = place_ref[0]
    tokens = up_ref.shape[1]
    total = jnp.concatenate([up_ref[...], down_ref[...]], axis=1).astype(jnp.float32)
    near_last, far_last = beside_ref[3], beside_ref[7]
    beside = jnp.concatenate([beside_ref[0], beside_ref[1], beside_ref[2], near_last[:, :64]], axis=1)
    far = jnp.concatenate([beside_ref[4], beside_ref[5], beside_ref[6], far_last[:, 64:]], axis=1)
    for k, rows in enumerate((own_ref[...], unpack(packed_ref)[0], beside, far)):
        placed = lax.dot_general(rows, mask_ref[group ^ k], (((0,), (0,)), ((), ())),
                                 preferred_element_type=jnp.float32)
        total = total + share_ref[pl.ds(group ^ k, 1), :] * placed
    out_up_ref[...] = total[:, :tokens].astype(jnp.bfloat16)
    out_down_ref[...] = total[:, tokens:].astype(jnp.bfloat16)


def halve(kept, sent, pattern):
    return kept + swap(sent.astype(SUM), pattern).astype(jnp.float32)


def sum_chunk(place, chunk, gate_w, up_w, far, after=()):
    cap = chunk[-1].shape[1]
    shape = jax.ShapeDtypeStruct((NEAR, PARTS // NEAR, cap, 256), jnp.float32)
    shapes = (shape,) if far else (shape, jax.ShapeDtypeStruct(chunk[-1].shape, chunk[-1].dtype))
    sums, *message = call(functools.partial(up_kernel, far), shapes, [SMEM] + [VMEM] * (2 + len(chunk)),
                (place, *chunk, gate_w, up_w), after=after, vmem=VMEM_LIMIT if far else 62 * 1024 * 1024,
                flops=2 * 2 * cap * 448 * 2048, moved=2 * 10**6)
    got = lax.all_to_all(sums.astype(SUM), "expert", 0, 0, axis_index_groups=quads(), tiled=True)
    return (jnp.sum(got.astype(jnp.float32), axis=0), *message)


def local(held_up, held_down, routes_up, routes_down, gates_up, gates_down, capacity, w_gate, w_up, w_down):
    index = lax.axis_index("expert")
    place = jnp.stack([index // PARTS, index % PARTS]).astype(jnp.int32)
    up_rows, down_rows = held_up[0].T, held_down[0].T
    width, tokens = up_rows.shape
    cap = 8 * max(1, tokens * 5 // 64)
    slot = jax.ShapeDtypeStruct((cap, width), jnp.bfloat16)
    packed = jax.ShapeDtypeStruct((7, cap, 128), jnp.bfloat16)
    shapes = (slot, packed, packed, jax.ShapeDtypeStruct((GROUPS, cap, 2 * tokens), jnp.bfloat16),
              jax.ShapeDtypeStruct((8, 2 * tokens), jnp.float32))
    own, sent, across, mask, share = call(
        functools.partial(route_kernel, cap), shapes, [SMEM] + [VMEM] * 6 + [SMEM],
        (place, up_rows, down_rows, routes_up[0].T, routes_down[0].T, gates_up[0].T, gates_down[0].T, capacity),
        scratch=[pltpu.VMEM((GROUPS, cap, width), jnp.bfloat16)], vmem=62 * 1024 * 1024,
        flops=2 * 4 * cap * 256 * width, moved=10**6)
    got = swap(sent, 32)
    near_sums, message = sum_chunk(place, (own, got, across), w_gate[0], w_up[0], False)
    far_sums = sum_chunk(place, (swap(message, 16),), w_gate[0], w_up[0], True, after=(near_sums,))[0]
    sums = jnp.concatenate([near_sums, far_sums], axis=1)
    sums = halve(sums[:2], sums[2:], 4)
    sums = halve(sums[0], sums[1], 8)
    block = jax.ShapeDtypeStruct((2 * cap, 128), jnp.bfloat16)
    blocks = call(hidden_kernel, (block,), [VMEM], (sums,))[0][None]
    for pattern in (8, 4):
        blocks = jnp.concatenate([blocks, swap(blocks, pattern)])
    blocks = lax.all_gather(blocks, "expert", axis_index_groups=quads())
    near_own, near_out, far_out = call(
        down_kernel, (slot, jax.ShapeDtypeStruct((4, cap, 128), jnp.bfloat16), packed), [SMEM] + [VMEM] * 2, (place, blocks, w_down[0]),
        scratch=[pltpu.VMEM((4 * cap, 1024), jnp.bfloat16)], flops=2 * 4 * cap * width * 1024, moved=2 * width * 1024)
    returned = swap(far_out, 16)
    beside = swap(jnp.concatenate([near_out, returned[3:]]), 32)
    rows = jax.ShapeDtypeStruct((width, tokens), jnp.bfloat16)
    out_up, out_down = call(combine_kernel, (rows, rows), [SMEM] + [VMEM] * 7,
                            (place, up_rows, down_rows, mask, share, near_own, beside, returned),
                            flops=2 * 4 * cap * 256 * width, moved=10**6)
    return shift(out_up, "section", 1).T[None], shift(out_down, "section", -1).T[None]


def solution(mesh):
    rows = P("section", None, "expert")
    table = P("section", None, None)
    weight = P("section", "expert", None)
    return jax.shard_map(
        local,
        mesh=mesh,
        in_specs=(rows, rows, table, table, table, table, P("section", None), weight, weight, weight),
        out_specs=(rows, rows),
        check_vma=False,
    )
```

time: 257 us -> 253 us (0.984)
  the two profiles are of different devices: /device:TPU:7 before, /device:TPU:39 now
where the time goes in v2:
time: 253 us
  starting transfers between devices  92 us (36%)
  waiting for transfers between devices  90.7 us (36%)
  blocking collectives  54 us (21%)
  Pallas kernels  9.62 us (4%)
  other arithmetic  3.32 us (1%)
    ppermute x8, waiting for transfers between devices, swap(): lax.ppermute(value, 'expert', [(i, i ^ pattern) for i in range(count)])  84.4 us
    ppermute x8, starting transfers between devices, swap(): lax.ppermute(value, 'expert', [(i, i ^ pattern) for i in range(count)])  72.3 us
    all_to_all x1, blocking collectives, sum_chunk(): lax.all_to_all(sums.astype(SUM), 'expert', 0, 0, axis_index_groups=quads(...  36.7 us
    all_gather x1, blocking collectives, local(): blocks = lax.all_gather(blocks, 'expert', axis_index_groups=quads())  17.3 us
    ppermute x2, starting transfers between devices, shift(): lax.ppermute(value, axis, [(i, (i + steps) % count) for i in range(count)])  14.1 us
    pallas_call x6, Pallas kernels, call(): pl.pallas_call(body, out_shape=out_shape, in_specs=[pl.BlockSpec(memory_s...  9.62 us
    ppermute x2, waiting for transfers between devices, shift(): lax.ppermute(value, axis, [(i, (i + steps) % count) for i in range(count)])  6.28 us
    all_to_all x1, starting transfers between devices, sum_chunk(): lax.all_to_all(sums.astype(SUM), 'expert', 0, 0, axis_index_groups=quads(...  5.57 us
  transfers between devices with their start and end apart: 11, of which 9 were waited for; matrix products, arithmetic and copies ran while one was open for 0% of the time, Pallas kernels for 0%

profile of v2, /device:TPU:39, one launch (start us, length us, event | category | flops | bytes accessed | tf_op | source)
XLA Modules:
  0.0 252.5 jit_solution(6397551735476067768)
XLA Ops:
  0.6 0.6 pad_add_fusion.refs_0_
  1.2 2.3 shard_map.113
  3.5 4.8 %collective-permute-start = (bf16[7,80,128]{2,1,0:T(8,128)(2,1)}, bf16[7,80,128]{2,1,0:T(8,128)(2,1)S(1)}, u32[]{:S(2)}, u32[]{:S(2)}) collective-permute-start(bf16[7,80,128]{2,1,0:T(8,128)(2,1)} %get-tuple-element.17), channel_id=1, source_target_pairs={{0,32},{1,33},{2,34},{3,35},{4,36},{5,37},{6,38},{7,39},{8,40},{9,... | collective-permute-start | bytes 430088 | tf_op jit(solution)/shard_map/ppermute | solution.py:28
  8.4 3.4 %collective-permute-done.refs_2_ = bf16[7,80,128]{2,1,0:T(8,128)(2,1)S(1)} collective-permute-done((bf16[7,80,128]{2,1,0:T(8,128)(2,1)}, bf16[7,80,128]{2,1,0:T(8,128)(2,1)S(1)}, u32[]{:S(2)}, u32[]{:S(2)}) %collective-permute-start) | collective-permute-done | bytes 143392 | tf_op jit(solution)/shard_map/ppermute | solution.py:28
  11.8 0.6 copy-done.8
  12.4 3.6 %shard_map.114 = (f32[4,4,80,256]{3,2,1,0:T(8,128)}, bf16[7,80,128]{2,1,0:T(8,128)(2,1)}) custom-call(s32[2]{0:T(128)} %pad_add_fusion.refs_0_, bf16[80,448]{1,0:T(8,128)(2,1)} %get-tuple-element.16.refs_1_, bf16[7,80,128]{2,1,0:T(8,128)(2,1)} %copy-done.8, bf16[7,80,128]{2,1,0:T(8,128)(2,1)} %get-tuple-element.18.refs_3_, bf16[448,1024]{1,0:T(8,128)(2,1)} %bitcast.37, ...), custom_call_target="tpu_custom_call" | custom-call | flops 293601280 | bytes 2000000 | tf_op jit(solution)/shard_map/pallas_call | solution.py:42
  16.0 2.3 convert_element_type.23
  18.3 5.6 %all-to-all-start = ((f16[4,4,80,256]{3,2,1,0:T(8,128)(2,1)}), f16[4,4,80,256]{3,2,1,0:T(8,128)(2,1)S(1)}, u32[]{:S(2)}, u32[]{:S(2)}) async-start(f16[4,4,80,256]{3,2,1,0:T(8,128)(2,1)} %convert_element_type.23), calls=%async_computation | async-start | bytes 1310720 | tf_op jit(solution)/shard_map/all_to_all | solution.py:175
  23.9 26.5 %collective-permute-start.1 = (bf16[7,80,128]{2,1,0:T(8,128)(2,1)S(1)}, bf16[7,80,128]{2,1,0:T(8,128)(2,1)S(1)}, u32[]{:S(2)}, u32[]{:S(2)}) collective-permute-start(bf16[7,80,128]{2,1,0:T(8,128)(2,1)S(1)} %copy-done.9), channel_id=1, source_target_pairs={{0,16},{1,17},{2,18},{3,19},{4,20},{5,21},{6,22},{7,23},{8,24},{9,... | collective-permute-start | bytes 430088 | tf_op jit(solution)/shard_map/ppermute | solution.py:28
  50.5 9.3 %collective-permute-done.1.refs_1_ = bf16[7,80,128]{2,1,0:T(8,128)(2,1)S(1)} collective-permute-done((bf16[7,80,128]{2,1,0:T(8,128)(2,1)S(1)}, bf16[7,80,128]{2,1,0:T(8,128)(2,1)S(1)}, u32[]{:S(2)}, u32[]{:S(2)}) %collective-permute-start.1) | collective-permute-done | bytes 143392 | tf_op jit(solution)/shard_map/ppermute | solution.py:28
  59.8 1.4 shard_map.115
  61.4 36.7 %all_to_all.10 = f16[4,4,80,256]{3,2,1,0:T(8,128)(2,1)S(1)} all-to-all(f16[4,4,80,256]{3,2,1,0:T(8,128)(2,1)S(1)} %convert_element_type.25), channel_id=1, replica_groups={{0,1,2,3},{4,5,6,7},{8,9,10,11},{12,13,14,15},{16,17,18,19},{20,21,22,2..., dimensions={0} | all-to-all | bytes 1310720 | tf_op jit(solution)/shard_map/all_to_all | solution.py:175
  98.2 3.4 %collective-permute-start.2 = (f16[2,160,256]{2,1,0:T(8,128)(2,1)S(1)}, f16[2,160,256]{2,1,0:T(8,128)(2,1)S(1)}, u32[]{:S(2)}, u32[]{:S(2)}) collective-permute-start(f16[2,160,256]{2,1,0:T(8,128)(2,1)S(1)} %fusion.2), channel_id=1, source_target_pairs={{0,4},{1,5},{2,6},{3,7},{4,0},{5,1},{6,2},{7,3},{8,12},{9,13},{10,... | collective-permute-start | bytes 491528 | tf_op jit(solution)/shard_map/ppermute | solution.py:28
  101.6 14.3 %collective-permute-done.2 = f16[2,160,256]{2,1,0:T(8,128)(2,1)S(1)} collective-permute-done((f16[2,160,256]{2,1,0:T(8,128)(2,1)S(1)}, f16[2,160,256]{2,1,0:T(8,128)(2,1)S(1)}, u32[]{:S(2)}, u32[]{:S(2)}) %collective-permute-start.2) | collective-permute-done | bytes 163872 | tf_op jit(solution)/shard_map/ppermute | solution.py:28
  116.0 12.2 %collective-permute-start.3 = (f16[160,256]{1,0:T(8,128)(2,1)S(1)}, f16[160,256]{1,0:T(8,128)(2,1)S(1)}, u32[]{:S(2)}, u32[]{:S(2)}) collective-permute-start(f16[160,256]{1,0:T(8,128)(2,1)S(1)} %fusion.4), channel_id=1, source_target_pairs={{0,8},{1,9},{2,10},{3,11},{4,12},{5,13},{6,14},{7,15},{8,0},{9,1},... | collective-permute-start | bytes 245768 | tf_op jit(solution)/shard_map/ppermute | solution.py:28
  128.2 13.7 %collective-permute-done.3 = f16[160,256]{1,0:T(8,128)(2,1)S(1)} collective-permute-done((f16[160,256]{1,0:T(8,128)(2,1)S(1)}, f16[160,256]{1,0:T(8,128)(2,1)S(1)}, u32[]{:S(2)}, u32[]{:S(2)}) %collective-permute-start.3) | collective-permute-done | bytes 81952 | tf_op jit(solution)/shard_map/ppermute | solution.py:28
  142.0 1.9 collective-permute-start.4
  143.9 11.5 %collective-permute-done.4 = bf16[1,160,128]{2,1,0:T(8,128)(2,1)S(1)} collective-permute-done((bf16[1,160,128]{2,1,0:T(8,128)(2,1)S(1)}, bf16[1,160,128]{2,1,0:T(8,128)(2,1)S(1)}, u32[]{:S(2)}, u32[]{:S(2)}) %collective-permute-start.4) | collective-permute-done | bytes 40992 | tf_op jit(solution)/shard_map/ppermute | solution.py:28
  155.4 1.9 collective-permute-start.5
  157.4 8.7 %collective-permute-done.5 = bf16[2,160,128]{2,1,0:T(8,128)(2,1)S(1)} collective-permute-done((bf16[2,160,128]{2,1,0:T(8,128)(2,1)S(1)}, bf16[2,160,128]{2,1,0:T(8,128)(2,1)S(1)}, u32[]{:S(2)}, u32[]{:S(2)}) %collective-permute-start.5) | collective-permute-done | bytes 81952 | tf_op jit(solution)/shard_map/ppermute | solution.py:28
  166.2 17.3 %all-gather = bf16[16,160,128]{2,1,0:T(8,128)(2,1)S(1)} all-gather(bf16[4,160,128]{2,1,0:T(8,128)(2,1)S(1)} %pad_maximum_fusion.1), channel_id=2, replica_groups={{0,1,2,3},{4,5,6,7},{8,9,10,11},{12,13,14,15},{16,17,18,19},{20,21,22,2..., dimensions={0}, use_global_device_ids=true | all-gather | bytes 819200 | tf_op jit(solution)/shard_map/all_gather | solution.py:204
  183.5 1.3 shard_map.117
  184.8 16.6 %collective-permute-start.6 = (bf16[7,80,128]{2,1,0:T(8,128)(2,1)S(1)}, bf16[7,80,128]{2,1,0:T(8,128)(2,1)S(1)}, u32[]{:S(2)}, u32[]{:S(2)}) collective-permute-start(bf16[7,80,128]{2,1,0:T(8,128)(2,1)S(1)} %get-tuple-element.23), channel_id=1, source_target_pairs={{0,16},{1,17},{2,18},{3,19},{4,20},{5,21},{6,22},{7,23},{8,24},{9,... | collective-permute-start | bytes 430088 | tf_op jit(solution)/shard_map/ppermute | solution.py:28
  201.4 20.7 %collective-permute-done.6.refs_7_ = bf16[7,80,128]{2,1,0:T(8,128)(2,1)S(1)} collective-permute-done((bf16[7,80,128]{2,1,0:T(8,128)(2,1)S(1)}, bf16[7,80,128]{2,1,0:T(8,128)(2,1)S(1)}, u32[]{:S(2)}, u32[]{:S(2)}) %collective-permute-start.6) | collective-permute-done | bytes 143392 | tf_op jit(solution)/shard_map/ppermute | solution.py:28
  222.2 4.9 %collective-permute-start.7 = (bf16[8,80,128]{2,1,0:T(8,128)(2,1)S(1)}, bf16[8,80,128]{2,1,0:T(8,128)(2,1)S(1)}, u32[]{:S(2)}, u32[]{:S(2)}) collective-permute-start(bf16[8,80,128]{2,1,0:T(8,128)(2,1)S(1)} %pad_maximum_fusion.2), channel_id=1, source_target_pairs={{0,32},{1,33},{2,34},{3,35},{4,36},{5,37},{6,38},{7,39},{8,40},{9,... | collective-permute-start | bytes 491528 | tf_op jit(solution)/shard_map/ppermute | solution.py:28
  227.1 2.7 %collective-permute-done.7.refs_6_ = bf16[8,80,128]{2,1,0:T(8,128)(2,1)S(1)} collective-permute-done((bf16[8,80,128]{2,1,0:T(8,128)(2,1)S(1)}, bf16[8,80,128]{2,1,0:T(8,128)(2,1)S(1)}, u32[]{:S(2)}, u32[]{:S(2)}) %collective-permute-start.7) | collective-permute-done | bytes 163872 | tf_op jit(solution)/shard_map/ppermute | solution.py:28
  229.8 1.0 shard_map.118
  230.8 12.2 %collective-permute-start.8 = (bf16[448,128]{1,0:T(8,128)(2,1)S(1)}, bf16[448,128]{1,0:T(8,128)(2,1)S(1)}, u32[]{:S(2)}, u32[]{:S(2)}) collective-permute-start(bf16[448,128]{1,0:T(8,128)(2,1)S(1)} %get-tuple-element.24), channel_id=1, source_target_pairs={{0,64},{64,128},{128,192},{192,256},{256,320},{320,384},{384,448},... | collective-permute-start | bytes 344072 | tf_op jit(solution)/shard_map/ppermute | solution.py:33
  243.0 1.9 collective-permute-start.9
  245.0 6.3 %collective-permute-done.9 = bf16[448,128]{1,0:T(8,128)(2,1)S(1)} collective-permute-done((bf16[448,128]{1,0:T(8,128)(2,1)S(1)}, bf16[448,128]{1,0:T(8,128)(2,1)S(1)}, u32[]{:S(2)}, u32[]{:S(2)}) %collective-permute-start.9) | collective-permute-done | bytes 114720 | tf_op jit(solution)/shard_map/ppermute | solution.py:33
  251.2 0.6 copy.14
  251.9 0.6 copy.15
  (33 shorter events, 0.5 us)
Async XLA Ops:
  3.5 8.2 %collective-permute-start = (bf16[7,80,128]{2,1,0:T(8,128)(2,1)}, bf16[7,80,128]{2,1,0:T(8,128)(2,1)S(1)}, u32[]{:S(2)}, u32[]{:S(2)}) collective-permute-start(bf16[7,80,128]{2,1,0:T(8,128)(2,1)} %get-tuple-element.17), channel_id=1, source_target_pairs={{0,32},{1,33},{2,34},{3,35},{4,36},{5,37},{6,38},{7,39},{8,40},{9,... | collective-permute-start | bytes 430088 | tf_op jit(solution)/shard_map/ppermute | solution.py:28
  11.8 0.6 copy-start.8
  16.0 7.9 %copy-start.9 = (bf16[7,80,128]{2,1,0:T(8,128)(2,1)S(1)}, bf16[7,80,128]{2,1,0:T(8,128)(2,1)}, u32[]{:S(2)}) copy-start(bf16[7,80,128]{2,1,0:T(8,128)(2,1)} %get-tuple-element.20) | copy-start | bytes 430084
  18.3 41.5 %copy-start = (bf16[1,448,1024]{2,1,0:T(8,128)(2,1)S(1)}, bf16[1,448,1024]{2,1,0:T(8,128)(2,1)}, u32[]{:S(2)}) copy-start(bf16[1,448,1024]{2,1,0:T(8,128)(2,1)} %param.17) | copy-start | bytes 2752516
  18.3 41.5 %copy-start.1 = (bf16[1,448,1024]{2,1,0:T(8,128)(2,1)S(1)}, bf16[1,448,1024]{2,1,0:T(8,128)(2,1)}, u32[]{:S(2)}) copy-start(bf16[1,448,1024]{2,1,0:T(8,128)(2,1)} %param.18) | copy-start | bytes 2752516
  18.3 41.5 %copy-start.6 = (s32[2]{0:T(128)S(1)}, s32[2]{0:T(128)}, u32[]{:S(2)}) copy-start(s32[2]{0:T(128)} %pad_add_fusion.refs_0_) | copy-start | bytes 28
  18.3 32.1 %all-to-all-start = ((f16[4,4,80,256]{3,2,1,0:T(8,128)(2,1)}), f16[4,4,80,256]{3,2,1,0:T(8,128)(2,1)S(1)}, u32[]{:S(2)}, u32[]{:S(2)}) async-start(f16[4,4,80,256]{3,2,1,0:T(8,128)(2,1)} %convert_element_type.23), calls=%async_computation | async-start | bytes 1310720 | tf_op jit(solution)/shard_map/all_to_all | solution.py:175
  23.9 35.9 %collective-permute-start.1 = (bf16[7,80,128]{2,1,0:T(8,128)(2,1)S(1)}, bf16[7,80,128]{2,1,0:T(8,128)(2,1)S(1)}, u32[]{:S(2)}, u32[]{:S(2)}) collective-permute-start(bf16[7,80,128]{2,1,0:T(8,128)(2,1)S(1)} %copy-done.9), channel_id=1, source_target_pairs={{0,16},{1,17},{2,18},{3,19},{4,20},{5,21},{6,22},{7,23},{8,24},{9,... | collective-permute-start | bytes 430088 | tf_op jit(solution)/shard_map/ppermute | solution.py:28
  98.2 17.7 %collective-permute-start.2 = (f16[2,160,256]{2,1,0:T(8,128)(2,1)S(1)}, f16[2,160,256]{2,1,0:T(8,128)(2,1)S(1)}, u32[]{:S(2)}, u32[]{:S(2)}) collective-permute-start(f16[2,160,256]{2,1,0:T(8,128)(2,1)S(1)} %fusion.2), channel_id=1, source_target_pairs={{0,4},{1,5},{2,6},{3,7},{4,0},{5,1},{6,2},{7,3},{8,12},{9,13},{10,... | collective-permute-start | bytes 491528 | tf_op jit(solution)/shard_map/ppermute | solution.py:28
  115.9 67.6 %copy-start.2 = (bf16[1,448,1024]{2,1,0:T(8,128)(2,1)S(1)}, bf16[1,448,1024]{2,1,0:T(8,128)(2,1)}, u32[]{:S(2)}) copy-start(bf16[1,448,1024]{2,1,0:T(8,128)(2,1)} %param.19) | copy-start | bytes 2752516
  116.0 25.9 %collective-permute-start.3 = (f16[160,256]{1,0:T(8,128)(2,1)S(1)}, f16[160,256]{1,0:T(8,128)(2,1)S(1)}, u32[]{:S(2)}, u32[]{:S(2)}) collective-permute-start(f16[160,256]{1,0:T(8,128)(2,1)S(1)} %fusion.4), channel_id=1, source_target_pairs={{0,8},{1,9},{2,10},{3,11},{4,12},{5,13},{6,14},{7,15},{8,0},{9,1},... | collective-permute-start | bytes 245768 | tf_op jit(solution)/shard_map/ppermute | solution.py:28
  142.0 13.5 %collective-permute-start.4 = (bf16[1,160,128]{2,1,0:T(8,128)(2,1)S(1)}, bf16[1,160,128]{2,1,0:T(8,128)(2,1)S(1)}, u32[]{:S(2)}, u32[]{:S(2)}) collective-permute-start(bf16[1,160,128]{2,1,0:T(8,128)(2,1)S(1)} %bitcast.47), channel_id=1, source_target_pairs={{0,8},{1,9},{2,10},{3,11},{4,12},{5,13},{6,14},{7,15},{8,0},{9,1},... | collective-permute-start | bytes 122888 | tf_op jit(solution)/shard_map/ppermute | solution.py:28
  155.4 10.6 %collective-permute-start.5 = (bf16[2,160,128]{2,1,0:T(8,128)(2,1)S(1)}, bf16[2,160,128]{2,1,0:T(8,128)(2,1)S(1)}, u32[]{:S(2)}, u32[]{:S(2)}) collective-permute-start(bf16[2,160,128]{2,1,0:T(8,128)(2,1)S(1)} %pad_maximum_fusion.3), channel_id=1, source_target_pairs={{0,4},{1,5},{2,6},{3,7},{4,0},{5,1},{6,2},{7,3},{8,12},{9,13},{10,... | collective-permute-start | bytes 245768 | tf_op jit(solution)/shard_map/ppermute | solution.py:28
  166.1 63.7 %copy-start.3 = (bf16[1,128,448]{1,2,0:T(8,128)(2,1)S(1)}, bf16[1,128,448]{1,2,0:T(8,128)(2,1)}, u32[]{:S(2)}) copy-start(bf16[1,128,448]{1,2,0:T(8,128)(2,1)} %param.10) | copy-start | bytes 344068
  166.1 63.7 %copy-start.4 = (bf16[1,128,448]{1,2,0:T(8,128)(2,1)S(1)}, bf16[1,128,448]{1,2,0:T(8,128)(2,1)}, u32[]{:S(2)}) copy-start(bf16[1,128,448]{1,2,0:T(8,128)(2,1)} %param.11) | copy-start | bytes 344068
  166.1 63.7 %copy-start.5 = (bf16[4,80,256]{2,1,0:T(8,128)(2,1)S(1)}, bf16[4,80,256]{2,1,0:T(8,128)(2,1)}, u32[]{:S(2)}) copy-start(bf16[4,80,256]{2,1,0:T(8,128)(2,1)} %get-tuple-element.14.refs_3_) | copy-start | bytes 491524
  166.1 63.7 %copy-start.7 = (f32[8,256]{1,0:T(8,128)S(1)}, f32[8,256]{1,0:T(8,128)}, u32[]{:S(2)}) copy-start(f32[8,256]{1,0:T(8,128)} %get-tuple-element.15.refs_4_) | copy-start | bytes 24580
  184.8 37.3 %collective-permute-start.6 = (bf16[7,80,128]{2,1,0:T(8,128)(2,1)S(1)}, bf16[7,80,128]{2,1,0:T(8,128)(2,1)S(1)}, u32[]{:S(2)}, u32[]{:S(2)}) collective-permute-start(bf16[7,80,128]{2,1,0:T(8,128)(2,1)S(1)} %get-tuple-element.23), channel_id=1, source_target_pairs={{0,16},{1,17},{2,18},{3,19},{4,20},{5,21},{6,22},{7,23},{8,24},{9,... | collective-permute-start | bytes 430088 | tf_op jit(solution)/shard_map/ppermute | solution.py:28
  222.2 7.6 %collective-permute-start.7 = (bf16[8,80,128]{2,1,0:T(8,128)(2,1)S(1)}, bf16[8,80,128]{2,1,0:T(8,128)(2,1)S(1)}, u32[]{:S(2)}, u32[]{:S(2)}) collective-permute-start(bf16[8,80,128]{2,1,0:T(8,128)(2,1)S(1)} %pad_maximum_fusion.2), channel_id=1, source_target_pairs={{0,32},{1,33},{2,34},{3,35},{4,36},{5,37},{6,38},{7,39},{8,40},{9,... | collective-permute-start | bytes 491528 | tf_op jit(solution)/shard_map/ppermute | solution.py:28
  230.8 14.1 %collective-permute-start.8 = (bf16[448,128]{1,0:T(8,128)(2,1)S(1)}, bf16[448,128]{1,0:T(8,128)(2,1)S(1)}, u32[]{:S(2)}, u32[]{:S(2)}) collective-permute-start(bf16[448,128]{1,0:T(8,128)(2,1)S(1)} %get-tuple-element.24), channel_id=1, source_target_pairs={{0,64},{64,128},{128,192},{192,256},{256,320},{320,384},{384,448},... | collective-permute-start | bytes 344072 | tf_op jit(solution)/shard_map/ppermute | solution.py:33
  243.0 8.2 %collective-permute-start.9 = (bf16[448,128]{1,0:T(8,128)(2,1)S(1)}, bf16[448,128]{1,0:T(8,128)(2,1)S(1)}, u32[]{:S(2)}, u32[]{:S(2)}) collective-permute-start(bf16[448,128]{1,0:T(8,128)(2,1)S(1)} %get-tuple-element.25), channel_id=1, source_target_pairs={{0,960},{64,0},{128,64},{192,128},{256,192},{320,256},{384,320},{4... | collective-permute-start | bytes 344072 | tf_op jit(solution)/shard_map/ppermute | solution.py:33

commit v3 on v2

--- a/solution.py
+++ b/solution.py
@@ -194,9 +194,8 @@
     got = swap(sent, 32)
     near_sums, message = sum_chunk(place, (own, got, across), w_gate[0], w_up[0], False)
     far_sums = sum_chunk(place, (swap(message, 16),), w_gate[0], w_up[0], True, after=(near_sums,))[0]
-    sums = jnp.concatenate([near_sums, far_sums], axis=1)
-    sums = halve(sums[:2], sums[2:], 4)
-    sums = halve(sums[0], sums[1], 8)
+    sums = [halve(value[:2], value[2:], 4) for value in (near_sums, far_sums)]
+    sums = jnp.concatenate([halve(value[0], value[1], 8) for value in sums])
     block = jax.ShapeDtypeStruct((2 * cap, 128), jnp.bfloat16)
     blocks = call(hidden_kernel, (block,), [VMEM], (sums,))[0][None]
     for pattern in (8, 4):

time: 253 us -> 243 us (0.960)
  the two profiles are of different devices: /device:TPU:39 before, /device:TPU:7 now
where the time goes in v3:
time: 243 us; the launch traced here: 241 us
  starting transfers between devices  128 us (53%)
  waiting for transfers between devices  82.3 us (34%)
  blocking collectives  14.2 us (6%)
  Pallas kernels  9.59 us (4%)
  other arithmetic  4.3 us (2%)
    ppermute x10, starting transfers between devices, swap(): lax.ppermute(value, 'expert', [(i, i ^ pattern) for i in range(count)])  84.5 us
    ppermute x10, waiting for transfers between devices, swap(): lax.ppermute(value, 'expert', [(i, i ^ pattern) for i in range(count)])  69 us
    ppermute x2, starting transfers between devices, shift(): lax.ppermute(value, axis, [(i, (i + steps) % count) for i in range(count)])  24.2 us
    all_to_all x2, starting transfers between devices, sum_chunk(): lax.all_to_all(sums.astype(SUM), 'expert', 0, 0, axis_index_groups=quads(...  19 us
    all_gather x1, blocking collectives, local(): blocks = lax.all_gather(blocks, 'expert', axis_index_groups=quads())  14.2 us
    pallas_call x6, Pallas kernels, call(): pl.pallas_call(body, out_shape=out_shape, in_specs=[pl.BlockSpec(memory_s...  9.59 us
    all_to_all x2, waiting for transfers between devices, sum_chunk(): lax.all_to_all(sums.astype(SUM), 'expert', 0, 0, axis_index_groups=quads(...  7.02 us
    ppermute x2, waiting for transfers between devices, shift(): lax.ppermute(value, axis, [(i, (i + steps) % count) for i in range(count)])  6.28 us
  transfers between devices with their start and end apart: 14, of which 10 were waited for; matrix products, arithmetic and copies ran while one was open for 0% of the time, Pallas kernels for 0%

profile of v3, /device:TPU:7, one launch (start us, length us, event | category | flops | bytes accessed | tf_op | source)
XLA Modules:
  0.0 241.0 jit_solution(9251607167647108117)
XLA Ops:
  1.3 2.3 shard_map.113
  3.6 4.8 %collective-permute-start = (bf16[7,80,128]{2,1,0:T(8,128)(2,1)}, bf16[7,80,128]{2,1,0:T(8,128)(2,1)S(1)}, u32[]{:S(2)}, u32[]{:S(2)}) collective-permute-start(bf16[7,80,128]{2,1,0:T(8,128)(2,1)} %get-tuple-element.17), channel_id=1, source_target_pairs={{0,32},{1,33},{2,34},{3,35},{4,36},{5,37},{6,38},{7,39},{8,40},{9,... | collective-permute-start | bytes 430088 | tf_op jit(solution)/shard_map/ppermute | solution.py:28
  8.4 3.4 %collective-permute-done.refs_2_ = bf16[7,80,128]{2,1,0:T(8,128)(2,1)S(1)} collective-permute-done((bf16[7,80,128]{2,1,0:T(8,128)(2,1)}, bf16[7,80,128]{2,1,0:T(8,128)(2,1)S(1)}, u32[]{:S(2)}, u32[]{:S(2)}) %collective-permute-start) | collective-permute-done | bytes 143392 | tf_op jit(solution)/shard_map/ppermute | solution.py:28
  12.5 3.6 %shard_map.114 = (f32[4,4,80,256]{3,2,1,0:T(8,128)}, bf16[7,80,128]{2,1,0:T(8,128)(2,1)}) custom-call(s32[2]{0:T(128)} %pad_add_fusion.refs_0_, bf16[80,448]{1,0:T(8,128)(2,1)} %get-tuple-element.16.refs_1_, bf16[7,80,128]{2,1,0:T(8,128)(2,1)} %copy-done.8, bf16[7,80,128]{2,1,0:T(8,128)(2,1)} %get-tuple-element.18.refs_3_, bf16[448,1024]{1,0:T(8,128)(2,1)} %bitcast.43, ...), custom_call_target="tpu_custom_call" | custom-call | flops 293601280 | bytes 2000000 | tf_op jit(solution)/shard_map/pallas_call | solution.py:42
  16.1 2.3 convert_element_type.34
  18.4 5.7 %all-to-all-start = ((f16[4,4,80,256]{3,2,1,0:T(8,128)(2,1)}), f16[4,4,80,256]{3,2,1,0:T(8,128)(2,1)S(1)}, u32[]{:S(2)}, u32[]{:S(2)}) async-start(f16[4,4,80,256]{3,2,1,0:T(8,128)(2,1)} %convert_element_type.34), calls=%async_computation | async-start | bytes 1310720 | tf_op jit(solution)/shard_map/all_to_all | solution.py:175
  24.1 26.6 %collective-permute-start.3 = (bf16[7,80,128]{2,1,0:T(8,128)(2,1)S(1)}, bf16[7,80,128]{2,1,0:T(8,128)(2,1)S(1)}, u32[]{:S(2)}, u32[]{:S(2)}) collective-permute-start(bf16[7,80,128]{2,1,0:T(8,128)(2,1)S(1)} %copy-done.9), channel_id=1, source_target_pairs={{0,16},{1,17},{2,18},{3,19},{4,20},{5,21},{6,22},{7,23},{8,24},{9,... | collective-permute-start | bytes 430088 | tf_op jit(solution)/shard_map/ppermute | solution.py:28
  50.8 20.3 %collective-permute-done.3.refs_1_ = bf16[7,80,128]{2,1,0:T(8,128)(2,1)S(1)} collective-permute-done((bf16[7,80,128]{2,1,0:T(8,128)(2,1)S(1)}, bf16[7,80,128]{2,1,0:T(8,128)(2,1)S(1)}, u32[]{:S(2)}, u32[]{:S(2)}) %collective-permute-start.3) | collective-permute-done | bytes 143392 | tf_op jit(solution)/shard_map/ppermute | solution.py:28
  71.1 1.4 shard_map.115
  72.6 1.0 convert_element_type.39
  73.6 13.2 %all-to-all-start.1 = ((f16[4,4,80,256]{3,2,1,0:T(8,128)(2,1)}), f16[4,4,80,256]{3,2,1,0:T(8,128)(2,1)S(1)}, u32[]{:S(2)}, u32[]{:S(2)}) async-start(f16[4,4,80,256]{3,2,1,0:T(8,128)(2,1)} %convert_element_type.39), calls=%async_computation.1 | async-start | bytes 1310720 | tf_op jit(solution)/shard_map/all_to_all | solution.py:175
  86.8 2.5 %collective-permute-start.1 = (f16[2,80,256]{2,1,0:T(8,128)(2,1)S(1)}, f16[2,80,256]{2,1,0:T(8,128)(2,1)S(1)}, u32[]{:S(2)}, u32[]{:S(2)}) collective-permute-start(f16[2,80,256]{2,1,0:T(8,128)(2,1)S(1)} %slice_convert_fusion.1), channel_id=1, source_target_pairs={{0,4},{1,5},{2,6},{3,7},{4,0},{5,1},{6,2},{7,3},{8,12},{9,13},{10,... | collective-permute-start | bytes 245768 | tf_op jit(solution)/shard_map/ppermute | solution.py:28
  89.3 6.9 %collective-permute-done.1 = f16[2,80,256]{2,1,0:T(8,128)(2,1)S(1)} collective-permute-done((f16[2,80,256]{2,1,0:T(8,128)(2,1)S(1)}, f16[2,80,256]{2,1,0:T(8,128)(2,1)S(1)}, u32[]{:S(2)}, u32[]{:S(2)}) %collective-permute-start.1) | collective-permute-done | bytes 81952 | tf_op jit(solution)/shard_map/ppermute | solution.py:28
  96.2 7.0 %all-to-all-done.1 = f16[4,4,80,256]{3,2,1,0:T(8,128)(2,1)S(1)} async-done(((f16[4,4,80,256]{3,2,1,0:T(8,128)(2,1)}), f16[4,4,80,256]{3,2,1,0:T(8,128)(2,1)S(1)}, u32[]{:S(2)}, u32[]{:S(2)}) %all-to-all-start.1) | async-done | bytes 655392 | tf_op jit(solution)/shard_map/all_to_all | solution.py:175
  103.4 1.9 collective-permute-start.4
  105.3 16.4 %collective-permute-start.2 = (f16[80,256]{1,0:T(8,128)(2,1)S(1)}, f16[80,256]{1,0:T(8,128)(2,1)S(1)}, u32[]{:S(2)}, u32[]{:S(2)}) collective-permute-start(f16[80,256]{1,0:T(8,128)(2,1)S(1)} %fusion.2), channel_id=1, source_target_pairs={{0,8},{1,9},{2,10},{3,11},{4,12},{5,13},{6,14},{7,15},{8,0},{9,1},... | collective-permute-start | bytes 122888 | tf_op jit(solution)/shard_map/ppermute | solution.py:28
  121.8 1.9 collective-permute-start.5
  123.7 12.0 %collective-permute-done.5 = f16[80,256]{1,0:T(8,128)(2,1)S(1)} collective-permute-done((f16[80,256]{1,0:T(8,128)(2,1)S(1)}, f16[80,256]{1,0:T(8,128)(2,1)S(1)}, u32[]{:S(2)}, u32[]{:S(2)}) %collective-permute-start.5) | collective-permute-done | bytes 40992 | tf_op jit(solution)/shard_map/ppermute | solution.py:28
  135.8 1.9 collective-permute-start.6
  137.7 11.7 %collective-permute-done.6 = bf16[1,160,128]{2,1,0:T(8,128)(2,1)S(1)} collective-permute-done((bf16[1,160,128]{2,1,0:T(8,128)(2,1)S(1)}, bf16[1,160,128]{2,1,0:T(8,128)(2,1)S(1)}, u32[]{:S(2)}, u32[]{:S(2)}) %collective-permute-start.6) | collective-permute-done | bytes 40992 | tf_op jit(solution)/shard_map/ppermute | solution.py:28
  149.4 1.9 collective-permute-start.7
  151.3 8.5 %collective-permute-done.7 = bf16[2,160,128]{2,1,0:T(8,128)(2,1)S(1)} collective-permute-done((bf16[2,160,128]{2,1,0:T(8,128)(2,1)S(1)}, bf16[2,160,128]{2,1,0:T(8,128)(2,1)S(1)}, u32[]{:S(2)}, u32[]{:S(2)}) %collective-permute-start.7) | collective-permute-done | bytes 81952 | tf_op jit(solution)/shard_map/ppermute | solution.py:28
  159.9 14.2 %all-gather = bf16[16,160,128]{2,1,0:T(8,128)(2,1)S(1)} all-gather(bf16[4,160,128]{2,1,0:T(8,128)(2,1)S(1)} %pad_maximum_fusion.1), channel_id=2, replica_groups={{0,1,2,3},{4,5,6,7},{8,9,10,11},{12,13,14,15},{16,17,18,19},{20,21,22,2..., dimensions={0}, use_global_device_ids=true | all-gather | bytes 819200 | tf_op jit(solution)/shard_map/all_gather | solution.py:203
  174.1 1.3 shard_map.117
  175.4 21.8 %collective-permute-start.8 = (bf16[7,80,128]{2,1,0:T(8,128)(2,1)S(1)}, bf16[7,80,128]{2,1,0:T(8,128)(2,1)S(1)}, u32[]{:S(2)}, u32[]{:S(2)}) collective-permute-start(bf16[7,80,128]{2,1,0:T(8,128)(2,1)S(1)} %get-tuple-element.23), channel_id=1, source_target_pairs={{0,16},{1,17},{2,18},{3,19},{4,20},{5,21},{6,22},{7,23},{8,24},{9,... | collective-permute-start | bytes 430088 | tf_op jit(solution)/shard_map/ppermute | solution.py:28
  197.2 3.1 %collective-permute-done.8.refs_7_ = bf16[7,80,128]{2,1,0:T(8,128)(2,1)S(1)} collective-permute-done((bf16[7,80,128]{2,1,0:T(8,128)(2,1)S(1)}, bf16[7,80,128]{2,1,0:T(8,128)(2,1)S(1)}, u32[]{:S(2)}, u32[]{:S(2)}) %collective-permute-start.8) | collective-permute-done | bytes 143392 | tf_op jit(solution)/shard_map/ppermute | solution.py:28
  200.4 4.7 %collective-permute-start.9 = (bf16[8,80,128]{2,1,0:T(8,128)(2,1)S(1)}, bf16[8,80,128]{2,1,0:T(8,128)(2,1)S(1)}, u32[]{:S(2)}, u32[]{:S(2)}) collective-permute-start(bf16[8,80,128]{2,1,0:T(8,128)(2,1)S(1)} %pad_maximum_fusion.2), channel_id=1, source_target_pairs={{0,32},{1,33},{2,34},{3,35},{4,36},{5,37},{6,38},{7,39},{8,40},{9,... | collective-permute-start | bytes 491528 | tf_op jit(solution)/shard_map/ppermute | solution.py:28
  205.0 3.2 %collective-permute-done.9.refs_6_ = bf16[8,80,128]{2,1,0:T(8,128)(2,1)S(1)} collective-permute-done((bf16[8,80,128]{2,1,0:T(8,128)(2,1)S(1)}, bf16[8,80,128]{2,1,0:T(8,128)(2,1)S(1)}, u32[]{:S(2)}, u32[]{:S(2)}) %collective-permute-start.9) | collective-permute-done | bytes 163872 | tf_op jit(solution)/shard_map/ppermute | solution.py:28
  208.2 1.0 shard_map.118
  209.2 22.2 %collective-permute-start.10 = (bf16[448,128]{1,0:T(8,128)(2,1)S(1)}, bf16[448,128]{1,0:T(8,128)(2,1)S(1)}, u32[]{:S(2)}, u32[]{:S(2)}) collective-permute-start(bf16[448,128]{1,0:T(8,128)(2,1)S(1)} %get-tuple-element.24), channel_id=1, source_target_pairs={{0,64},{64,128},{128,192},{192,256},{256,320},{320,384},{384,448},... | collective-permute-start | bytes 344072 | tf_op jit(solution)/shard_map/ppermute | solution.py:33
  231.5 1.9 collective-permute-start.11
  233.4 6.3 %collective-permute-done.11 = bf16[448,128]{1,0:T(8,128)(2,1)S(1)} collective-permute-done((bf16[448,128]{1,0:T(8,128)(2,1)S(1)}, bf16[448,128]{1,0:T(8,128)(2,1)S(1)}, u32[]{:S(2)}, u32[]{:S(2)}) %collective-permute-start.11) | collective-permute-done | bytes 114720 | tf_op jit(solution)/shard_map/ppermute | solution.py:33
  (43 shorter events, 3.1 us)
Async XLA Ops:
  3.6 8.2 %collective-permute-start = (bf16[7,80,128]{2,1,0:T(8,128)(2,1)}, bf16[7,80,128]{2,1,0:T(8,128)(2,1)S(1)}, u32[]{:S(2)}, u32[]{:S(2)}) collective-permute-start(bf16[7,80,128]{2,1,0:T(8,128)(2,1)} %get-tuple-element.17), channel_id=1, source_target_pairs={{0,32},{1,33},{2,34},{3,35},{4,36},{5,37},{6,38},{7,39},{8,40},{9,... | collective-permute-start | bytes 430088 | tf_op jit(solution)/shard_map/ppermute | solution.py:28
  11.8 0.7 copy-start.8
  16.1 8.1 %copy-start.9 = (bf16[7,80,128]{2,1,0:T(8,128)(2,1)S(1)}, bf16[7,80,128]{2,1,0:T(8,128)(2,1)}, u32[]{:S(2)}) copy-start(bf16[7,80,128]{2,1,0:T(8,128)(2,1)} %get-tuple-element.20) | copy-start | bytes 430084
  18.4 52.7 %copy-start = (bf16[1,448,1024]{2,1,0:T(8,128)(2,1)S(1)}, bf16[1,448,1024]{2,1,0:T(8,128)(2,1)}, u32[]{:S(2)}) copy-start(bf16[1,448,1024]{2,1,0:T(8,128)(2,1)} %param.17) | copy-start | bytes 2752516
  18.4 52.7 %copy-start.1 = (bf16[1,448,1024]{2,1,0:T(8,128)(2,1)S(1)}, bf16[1,448,1024]{2,1,0:T(8,128)(2,1)}, u32[]{:S(2)}) copy-start(bf16[1,448,1024]{2,1,0:T(8,128)(2,1)} %param.18) | copy-start | bytes 2752516
  18.4 52.7 %copy-start.6 = (s32[2]{0:T(128)S(1)}, s32[2]{0:T(128)}, u32[]{:S(2)}) copy-start(s32[2]{0:T(128)} %pad_add_fusion.refs_0_) | copy-start | bytes 28
  18.4 32.3 %all-to-all-start = ((f16[4,4,80,256]{3,2,1,0:T(8,128)(2,1)}), f16[4,4,80,256]{3,2,1,0:T(8,128)(2,1)S(1)}, u32[]{:S(2)}, u32[]{:S(2)}) async-start(f16[4,4,80,256]{3,2,1,0:T(8,128)(2,1)} %convert_element_type.34), calls=%async_computation | async-start | bytes 1310720 | tf_op jit(solution)/shard_map/all_to_all | solution.py:175
  24.1 47.0 %collective-permute-start.3 = (bf16[7,80,128]{2,1,0:T(8,128)(2,1)S(1)}, bf16[7,80,128]{2,1,0:T(8,128)(2,1)S(1)}, u32[]{:S(2)}, u32[]{:S(2)}) collective-permute-start(bf16[7,80,128]{2,1,0:T(8,128)(2,1)S(1)} %copy-done.9), channel_id=1, source_target_pairs={{0,16},{1,17},{2,18},{3,19},{4,20},{5,21},{6,22},{7,23},{8,24},{9,... | collective-permute-start | bytes 430088 | tf_op jit(solution)/shard_map/ppermute | solution.py:28
  73.6 29.7 %all-to-all-start.1 = ((f16[4,4,80,256]{3,2,1,0:T(8,128)(2,1)}), f16[4,4,80,256]{3,2,1,0:T(8,128)(2,1)S(1)}, u32[]{:S(2)}, u32[]{:S(2)}) async-start(f16[4,4,80,256]{3,2,1,0:T(8,128)(2,1)} %convert_element_type.39), calls=%async_computation.1 | async-start | bytes 1310720 | tf_op jit(solution)/shard_map/all_to_all | solution.py:175
  86.8 9.4 %collective-permute-start.1 = (f16[2,80,256]{2,1,0:T(8,128)(2,1)S(1)}, f16[2,80,256]{2,1,0:T(8,128)(2,1)S(1)}, u32[]{:S(2)}, u32[]{:S(2)}) collective-permute-start(f16[2,80,256]{2,1,0:T(8,128)(2,1)S(1)} %slice_convert_fusion.1), channel_id=1, source_target_pairs={{0,4},{1,5},{2,6},{3,7},{4,0},{5,1},{6,2},{7,3},{8,12},{9,13},{10,... | collective-permute-start | bytes 245768 | tf_op jit(solution)/shard_map/ppermute | solution.py:28
  103.4 18.4 %collective-permute-start.4 = (f16[2,80,256]{2,1,0:T(8,128)(2,1)S(1)}, f16[2,80,256]{2,1,0:T(8,128)(2,1)S(1)}, u32[]{:S(2)}, u32[]{:S(2)}) collective-permute-start(f16[2,80,256]{2,1,0:T(8,128)(2,1)S(1)} %slice_convert_fusion), channel_id=1, source_target_pairs={{0,4},{1,5},{2,6},{3,7},{4,0},{5,1},{6,2},{7,3},{8,12},{9,13},{10,... | collective-permute-start | bytes 245768 | tf_op jit(solution)/shard_map/ppermute | solution.py:28
  105.3 68.8 %copy-start.2 = (bf16[1,448,1024]{2,1,0:T(8,128)(2,1)S(1)}, bf16[1,448,1024]{2,1,0:T(8,128)(2,1)}, u32[]{:S(2)}) copy-start(bf16[1,448,1024]{2,1,0:T(8,128)(2,1)} %param.19) | copy-start | bytes 2752516
  105.3 18.4 %collective-permute-start.2 = (f16[80,256]{1,0:T(8,128)(2,1)S(1)}, f16[80,256]{1,0:T(8,128)(2,1)S(1)}, u32[]{:S(2)}, u32[]{:S(2)}) collective-permute-start(f16[80,256]{1,0:T(8,128)(2,1)S(1)} %fusion.2), channel_id=1, source_target_pairs={{0,8},{1,9},{2,10},{3,11},{4,12},{5,13},{6,14},{7,15},{8,0},{9,1},... | collective-permute-start | bytes 122888 | tf_op jit(solution)/shard_map/ppermute | solution.py:28
  121.8 13.9 %collective-permute-start.5 = (f16[80,256]{1,0:T(8,128)(2,1)S(1)}, f16[80,256]{1,0:T(8,128)(2,1)S(1)}, u32[]{:S(2)}, u32[]{:S(2)}) collective-permute-start(f16[80,256]{1,0:T(8,128)(2,1)S(1)} %fusion.3), channel_id=1, source_target_pairs={{0,8},{1,9},{2,10},{3,11},{4,12},{5,13},{6,14},{7,15},{8,0},{9,1},... | collective-permute-start | bytes 122888 | tf_op jit(solution)/shard_map/ppermute | solution.py:28
  135.8 13.6 %collective-permute-start.6 = (bf16[1,160,128]{2,1,0:T(8,128)(2,1)S(1)}, bf16[1,160,128]{2,1,0:T(8,128)(2,1)S(1)}, u32[]{:S(2)}, u32[]{:S(2)}) collective-permute-start(bf16[1,160,128]{2,1,0:T(8,128)(2,1)S(1)} %bitcast.53), channel_id=1, source_target_pairs={{0,8},{1,9},{2,10},{3,11},{4,12},{5,13},{6,14},{7,15},{8,0},{9,1},... | collective-permute-start | bytes 122888 | tf_op jit(solution)/shard_map/ppermute | solution.py:28
  149.4 10.4 %collective-permute-start.7 = (bf16[2,160,128]{2,1,0:T(8,128)(2,1)S(1)}, bf16[2,160,128]{2,1,0:T(8,128)(2,1)S(1)}, u32[]{:S(2)}, u32[]{:S(2)}) collective-permute-start(bf16[2,160,128]{2,1,0:T(8,128)(2,1)S(1)} %pad_maximum_fusion.3), channel_id=1, source_target_pairs={{0,4},{1,5},{2,6},{3,7},{4,0},{5,1},{6,2},{7,3},{8,12},{9,13},{10,... | collective-permute-start | bytes 245768 | tf_op jit(solution)/shard_map/ppermute | solution.py:28
  159.9 48.4 %copy-start.3 = (bf16[1,128,448]{1,2,0:T(8,128)(2,1)S(1)}, bf16[1,128,448]{1,2,0:T(8,128)(2,1)}, u32[]{:S(2)}) copy-start(bf16[1,128,448]{1,2,0:T(8,128)(2,1)} %param.10) | copy-start | bytes 344068
  159.9 48.4 %copy-start.4 = (bf16[1,128,448]{1,2,0:T(8,128)(2,1)S(1)}, bf16[1,128,448]{1,2,0:T(8,128)(2,1)}, u32[]{:S(2)}) copy-start(bf16[1,128,448]{1,2,0:T(8,128)(2,1)} %param.11) | copy-start | bytes 344068
  159.9 48.3 %copy-start.5 = (bf16[4,80,256]{2,1,0:T(8,128)(2,1)S(1)}, bf16[4,80,256]{2,1,0:T(8,128)(2,1)}, u32[]{:S(2)}) copy-start(bf16[4,80,256]{2,1,0:T(8,128)(2,1)} %get-tuple-element.14.refs_3_) | copy-start | bytes 491524
  159.9 48.3 %copy-start.7 = (f32[8,256]{1,0:T(8,128)S(1)}, f32[8,256]{1,0:T(8,128)}, u32[]{:S(2)}) copy-start(f32[8,256]{1,0:T(8,128)} %get-tuple-element.15.refs_4_) | copy-start | bytes 24580
  175.4 24.9 %collective-permute-start.8 = (bf16[7,80,128]{2,1,0:T(8,128)(2,1)S(1)}, bf16[7,80,128]{2,1,0:T(8,128)(2,1)S(1)}, u32[]{:S(2)}, u32[]{:S(2)}) collective-permute-start(bf16[7,80,128]{2,1,0:T(8,128)(2,1)S(1)} %get-tuple-element.23), channel_id=1, source_target_pairs={{0,16},{1,17},{2,18},{3,19},{4,20},{5,21},{6,22},{7,23},{8,24},{9,... | collective-permute-start | bytes 430088 | tf_op jit(solution)/shard_map/ppermute | solution.py:28
  200.4 7.9 %collective-permute-start.9 = (bf16[8,80,128]{2,1,0:T(8,128)(2,1)S(1)}, bf16[8,80,128]{2,1,0:T(8,128)(2,1)S(1)}, u32[]{:S(2)}, u32[]{:S(2)}) collective-permute-start(bf16[8,80,128]{2,1,0:T(8,128)(2,1)S(1)} %pad_maximum_fusion.2), channel_id=1, source_target_pairs={{0,32},{1,33},{2,34},{3,35},{4,36},{5,37},{6,38},{7,39},{8,40},{9,... | collective-permute-start | bytes 491528 | tf_op jit(solution)/shard_map/ppermute | solution.py:28
  209.2 24.2 %collective-permute-start.10 = (bf16[448,128]{1,0:T(8,128)(2,1)S(1)}, bf16[448,128]{1,0:T(8,128)(2,1)S(1)}, u32[]{:S(2)}, u32[]{:S(2)}) collective-permute-start(bf16[448,128]{1,0:T(8,128)(2,1)S(1)} %get-tuple-element.24), channel_id=1, source_target_pairs={{0,64},{64,128},{128,192},{192,256},{256,320},{320,384},{384,448},... | collective-permute-start | bytes 344072 | tf_op jit(solution)/shard_map/ppermute | solution.py:33
  231.5 8.2 %collective-permute-start.11 = (bf16[448,128]{1,0:T(8,128)(2,1)S(1)}, bf16[448,128]{1,0:T(8,128)(2,1)S(1)}, u32[]{:S(2)}, u32[]{:S(2)}) collective-permute-start(bf16[448,128]{1,0:T(8,128)(2,1)S(1)} %get-tuple-element.25), channel_id=1, source_target_pairs={{0,960},{64,0},{128,64},{192,128},{256,192},{320,256},{384,320},{4... | collective-permute-start | bytes 344072 | tf_op jit(solution)/shard_map/ppermute | solution.py:33

commit v4 on v3

--- a/solution.py
+++ b/solution.py
@@ -127,22 +127,29 @@
     out_ref[...] = (jax.nn.silu(value[:, :128]) * value[:, 128:]).astype(jnp.bfloat16)
 
 
-def down_kernel(place_ref, blocks_ref, down_ref, own_ref, beside_ref, packed_ref, hidden):
+def down_kernel(far, place_ref, blocks_ref, down_ref, *refs):
+    out_refs, hidden = refs[:-1], refs[-1]
     part = place_ref[1]
-    cap = own_ref.shape[0]
+    cap = blocks_ref.shape[2]
     for q in range(NEAR):
         for n in range(NEAR):
-            row = pl.multiple_of(((n % 2) ^ (part // 8)) * 2 * cap, 16)
+            row = pl.multiple_of(((n % 2) ^ (part // 8)) * cap, 16)
             column = pl.multiple_of((((n // 2) ^ (part // 4 % 2)) * NEAR + q) * 128, 128)
-            hidden[pl.ds(row, 2 * cap), pl.ds(column, 128)] = blocks_ref[q, n]
+            hidden[pl.ds(row, cap), pl.ds(column, 128)] = blocks_ref[q, n]
     out = lax.dot_general(hidden[...], down_ref[...], (((1,), (1,)), ((), ())),
                           preferred_element_type=jnp.float32).astype(jnp.bfloat16)
-    pack(out[cap : 2 * cap], out[3 * cap :], packed_ref)
-    own_ref[...] = out[:cap]
-    beside = out[2 * cap : 3 * cap]
+    if far:
+        pack(out[:cap], out[cap:], out_refs[0])
+        return
+    out_refs[0][...] = out[:cap]
+    beside = out[cap:]
     for n in range(3):
-        beside_ref[n] = beside[:, n * 128 : n * 128 + 128]
-    beside_ref[3] = jnp.concatenate([beside[:, 384:]] * 2, axis=1)
+        out_refs[1][n] = beside[:, n * 128 : n * 128 + 128]
+    out_refs[1][3] = jnp.concatenate([beside[:, 384:]] * 2, axis=1)
+
+
+def copy_kernel(in_ref, out_ref):
+    out_ref[...] = in_ref[:, : out_ref.shape[1]]
 
 
 def combine_kernel(place_ref, up_ref, down_ref, mask_ref, share_ref, own_ref, beside_ref, packed_ref,
@@ -200,11 +207,16 @@
     blocks = call(hidden_kernel, (block,), [VMEM], (sums,))[0][None]
     for pattern in (8, 4):
         blocks = jnp.concatenate([blocks, swap(blocks, pattern)])
-    blocks = lax.all_gather(blocks, "expert", axis_index_groups=quads())
-    near_own, near_out, far_out = call(
-        down_kernel, (slot, jax.ShapeDtypeStruct((4, cap, 128), jnp.bfloat16), packed), [SMEM] + [VMEM] * 2, (place, blocks, w_down[0]),
-        scratch=[pltpu.VMEM((4 * cap, 1024), jnp.bfloat16)], flops=2 * 4 * cap * width * 1024, moved=2 * width * 1024)
+    tiles = jax.ShapeDtypeStruct((4, cap, 128), jnp.bfloat16)
+    cost = dict(scratch=[pltpu.VMEM((2 * cap, 1024), jnp.bfloat16)])
+    far_blocks = lax.all_gather(blocks[:, cap:], "expert", axis_index_groups=quads())
+    far_out = call(functools.partial(down_kernel, True), (packed,), [SMEM] + [VMEM] * 2, (place, far_blocks, w_down[0]),
+                   **cost)[0]
     returned = swap(far_out, 16)
+    late = call(copy_kernel, (jax.ShapeDtypeStruct((4, cap, 128), jnp.bfloat16),), [VMEM], (blocks,), after=(far_out,))[0]
+    near_blocks = lax.all_gather(late, "expert", axis_index_groups=quads())
+    near_own, near_out = call(functools.partial(down_kernel, False), (slot, tiles), [SMEM] + [VMEM] * 2,
+                              (place, near_blocks, w_down[0]), **cost)
     beside = swap(jnp.concatenate([near_out, returned[3:]]), 32)
     rows = jax.ShapeDtypeStruct((width, tokens), jnp.bfloat16)
     out_up, out_down = call(combine_kernel, (rows, rows), [SMEM] + [VMEM] * 7,

time: 243 us -> 251 us (1.033)
  blocking collectives: 14.2 us -> 41 us
  starting transfers between devices: 128 us -> 112 us
  waiting for transfers between devices: 82.3 us -> 79.5 us
    all_gather x1 -> x2, blocking collectives: 14.2 us -> 41 us  [the longest x1 28 us: local(): near_blocks = lax.all_gather(late, 'expert', axis_index_groups=quads())]
    ppermute x2, starting transfers between devices: 24.2 us -> 9.57 us  [shift(): lax.ppermute(value, axis, [(i, (i + steps) % count) for i in range(count)])]
    ppermute x10, waiting for transfers between devices: 69 us -> 66.2 us  [swap(): lax.ppermute(value, 'expert', [(i, i ^ pattern) for i in range(count)])]
    pallas_call x6 -> x8, Pallas kernels: 9.59 us -> 10.4 us  [call(): pl.pallas_call(body, out_shape=out_shape, in_specs=[pl.BlockSpec(memory_s...]
  transfers between devices with their start and end apart: 14 -> 14, of which waited for: 10 -> 9; matrix products, arithmetic and copies ran while one was open for 0% -> 0% of each run, Pallas kernels for 0% -> 0%
where the time goes in v4:
time: 251 us; the launch traced here: 250 us
  starting transfers between devices  112 us (45%)
  waiting for transfers between devices  79.5 us (32%)
  blocking collectives  41 us (16%)
  Pallas kernels  10.4 us (4%)
  other arithmetic  4.31 us (2%)
    ppermute x10, starting transfers between devices, swap(): lax.ppermute(value, 'expert', [(i, i ^ pattern) for i in range(count)])  83.4 us
    ppermute x10, waiting for transfers between devices, swap(): lax.ppermute(value, 'expert', [(i, i ^ pattern) for i in range(count)])  66.2 us
    all_gather x1, blocking collectives, local(): near_blocks = lax.all_gather(late, 'expert', axis_index_groups=quads())  28 us
    all_to_all x2, starting transfers between devices, sum_chunk(): lax.all_to_all(sums.astype(SUM), 'expert', 0, 0, axis_index_groups=quads(...  19 us
    all_gather x1, blocking collectives, local(): lax.all_gather(blocks[:, cap:], 'expert', axis_index_groups=quads())  13 us
    pallas_call x8, Pallas kernels, call(): pl.pallas_call(body, out_shape=out_shape, in_specs=[pl.BlockSpec(memory_s...  10.4 us
    ppermute x2, starting transfers between devices, shift(): lax.ppermute(value, axis, [(i, (i + steps) % count) for i in range(count)])  9.57 us
    all_to_all x2, waiting for transfers between devices, sum_chunk(): lax.all_to_all(sums.astype(SUM), 'expert', 0, 0, axis_index_groups=quads(...  7.02 us
  transfers between devices with their start and end apart: 14, of which 9 were waited for; matrix products, arithmetic and copies ran while one was open for 0% of the time, Pallas kernels for 0%

profile of v4, /device:TPU:7, one launch (start us, length us, event | category | flops | bytes accessed | tf_op | source)
XLA Modules:
  0.0 250.2 jit_solution(14998200671747208165)
XLA Ops:
  1.3 2.3 shard_map.113
  3.6 4.8 %collective-permute-start = (bf16[7,80,128]{2,1,0:T(8,128)(2,1)}, bf16[7,80,128]{2,1,0:T(8,128)(2,1)S(1)}, u32[]{:S(2)}, u32[]{:S(2)}) collective-permute-start(bf16[7,80,128]{2,1,0:T(8,128)(2,1)} %get-tuple-element.16), channel_id=1, source_target_pairs={{0,32},{1,33},{2,34},{3,35},{4,36},{5,37},{6,38},{7,39},{8,40},{9,... | collective-permute-start | bytes 430088 | tf_op jit(solution)/shard_map/ppermute | solution.py:28
  8.4 3.4 %collective-permute-done.refs_2_ = bf16[7,80,128]{2,1,0:T(8,128)(2,1)S(1)} collective-permute-done((bf16[7,80,128]{2,1,0:T(8,128)(2,1)}, bf16[7,80,128]{2,1,0:T(8,128)(2,1)S(1)}, u32[]{:S(2)}, u32[]{:S(2)}) %collective-permute-start) | collective-permute-done | bytes 143392 | tf_op jit(solution)/shard_map/ppermute | solution.py:28
  12.5 3.6 %shard_map.114 = (f32[4,4,80,256]{3,2,1,0:T(8,128)}, bf16[7,80,128]{2,1,0:T(8,128)(2,1)}) custom-call(s32[2]{0:T(128)} %pad_add_fusion.refs_0_, bf16[80,448]{1,0:T(8,128)(2,1)} %get-tuple-element.15.refs_1_, bf16[7,80,128]{2,1,0:T(8,128)(2,1)} %copy-done.8, bf16[7,80,128]{2,1,0:T(8,128)(2,1)} %get-tuple-element.17.refs_3_, bf16[448,1024]{1,0:T(8,128)(2,1)} %bitcast.44, ...), custom_call_target="tpu_custom_call" | custom-call | flops 293601280 | bytes 2000000 | tf_op jit(solution)/shard_map/pallas_call | solution.py:42
  16.1 2.3 convert_element_type.34
  18.4 5.7 %all-to-all-start = ((f16[4,4,80,256]{3,2,1,0:T(8,128)(2,1)}), f16[4,4,80,256]{3,2,1,0:T(8,128)(2,1)S(1)}, u32[]{:S(2)}, u32[]{:S(2)}) async-start(f16[4,4,80,256]{3,2,1,0:T(8,128)(2,1)} %convert_element_type.34), calls=%async_computation | async-start | bytes 1310720 | tf_op jit(solution)/shard_map/all_to_all | solution.py:182
  24.1 26.6 %collective-permute-start.3 = (bf16[7,80,128]{2,1,0:T(8,128)(2,1)S(1)}, bf16[7,80,128]{2,1,0:T(8,128)(2,1)S(1)}, u32[]{:S(2)}, u32[]{:S(2)}) collective-permute-start(bf16[7,80,128]{2,1,0:T(8,128)(2,1)S(1)} %copy-done.9), channel_id=1, source_target_pairs={{0,16},{1,17},{2,18},{3,19},{4,20},{5,21},{6,22},{7,23},{8,24},{9,... | collective-permute-start | bytes 430088 | tf_op jit(solution)/shard_map/ppermute | solution.py:28
  50.8 20.3 %collective-permute-done.3.refs_1_ = bf16[7,80,128]{2,1,0:T(8,128)(2,1)S(1)} collective-permute-done((bf16[7,80,128]{2,1,0:T(8,128)(2,1)S(1)}, bf16[7,80,128]{2,1,0:T(8,128)(2,1)S(1)}, u32[]{:S(2)}, u32[]{:S(2)}) %collective-permute-start.3) | collective-permute-done | bytes 143392 | tf_op jit(solution)/shard_map/ppermute | solution.py:28
  71.1 1.4 shard_map.115
  73.6 13.2 %all-to-all-start.1 = ((f16[4,4,80,256]{3,2,1,0:T(8,128)(2,1)}), f16[4,4,80,256]{3,2,1,0:T(8,128)(2,1)S(1)}, u32[]{:S(2)}, u32[]{:S(2)}) async-start(f16[4,4,80,256]{3,2,1,0:T(8,128)(2,1)} %convert_element_type.39), calls=%async_computation.1 | async-start | bytes 1310720 | tf_op jit(solution)/shard_map/all_to_all | solution.py:182
  86.8 2.5 %collective-permute-start.1 = (f16[2,80,256]{2,1,0:T(8,128)(2,1)S(1)}, f16[2,80,256]{2,1,0:T(8,128)(2,1)S(1)}, u32[]{:S(2)}, u32[]{:S(2)}) collective-permute-start(f16[2,80,256]{2,1,0:T(8,128)(2,1)S(1)} %slice_convert_fusion.1), channel_id=1, source_target_pairs={{0,4},{1,5},{2,6},{3,7},{4,0},{5,1},{6,2},{7,3},{8,12},{9,13},{10,... | collective-permute-start | bytes 245768 | tf_op jit(solution)/shard_map/ppermute | solution.py:28
  89.3 6.9 %collective-permute-done.1 = f16[2,80,256]{2,1,0:T(8,128)(2,1)S(1)} collective-permute-done((f16[2,80,256]{2,1,0:T(8,128)(2,1)S(1)}, f16[2,80,256]{2,1,0:T(8,128)(2,1)S(1)}, u32[]{:S(2)}, u32[]{:S(2)}) %collective-permute-start.1) | collective-permute-done | bytes 81952 | tf_op jit(solution)/shard_map/ppermute | solution.py:28
  96.2 7.0 %all-to-all-done.1 = f16[4,4,80,256]{3,2,1,0:T(8,128)(2,1)S(1)} async-done(((f16[4,4,80,256]{3,2,1,0:T(8,128)(2,1)}), f16[4,4,80,256]{3,2,1,0:T(8,128)(2,1)S(1)}, u32[]{:S(2)}, u32[]{:S(2)}) %all-to-all-start.1) | async-done | bytes 655392 | tf_op jit(solution)/shard_map/all_to_all | solution.py:182
  103.4 2.1 collective-permute-start.4
  105.5 16.3 %collective-permute-start.2 = (f16[80,256]{1,0:T(8,128)(2,1)S(1)}, f16[80,256]{1,0:T(8,128)(2,1)S(1)}, u32[]{:S(2)}, u32[]{:S(2)}) collective-permute-start(f16[80,256]{1,0:T(8,128)(2,1)S(1)} %fusion.2), channel_id=1, source_target_pairs={{0,8},{1,9},{2,10},{3,11},{4,12},{5,13},{6,14},{7,15},{8,0},{9,1},... | collective-permute-start | bytes 122888 | tf_op jit(solution)/shard_map/ppermute | solution.py:28
  121.8 2.1 collective-permute-start.5
  123.9 11.8 %collective-permute-done.5 = f16[80,256]{1,0:T(8,128)(2,1)S(1)} collective-permute-done((f16[80,256]{1,0:T(8,128)(2,1)S(1)}, f16[80,256]{1,0:T(8,128)(2,1)S(1)}, u32[]{:S(2)}, u32[]{:S(2)}) %collective-permute-start.5) | collective-permute-done | bytes 40992 | tf_op jit(solution)/shard_map/ppermute | solution.py:28
  135.8 1.9 collective-permute-start.6
  137.7 11.7 %collective-permute-done.6 = bf16[1,160,128]{2,1,0:T(8,128)(2,1)S(1)} collective-permute-done((bf16[1,160,128]{2,1,0:T(8,128)(2,1)S(1)}, bf16[1,160,128]{2,1,0:T(8,128)(2,1)S(1)}, u32[]{:S(2)}, u32[]{:S(2)}) %collective-permute-start.6) | collective-permute-done | bytes 40992 | tf_op jit(solution)/shard_map/ppermute | solution.py:28
  149.4 1.9 collective-permute-start.7
  151.3 9.4 %collective-permute-done.7 = bf16[2,160,128]{2,1,0:T(8,128)(2,1)S(1)} collective-permute-done((bf16[2,160,128]{2,1,0:T(8,128)(2,1)S(1)}, bf16[2,160,128]{2,1,0:T(8,128)(2,1)S(1)}, u32[]{:S(2)}, u32[]{:S(2)}) %collective-permute-start.7) | collective-permute-done | bytes 81952 | tf_op jit(solution)/shard_map/ppermute | solution.py:28
  160.7 13.0 %all-gather = bf16[16,80,128]{2,1,0:T(8,128)(2,1)S(1)} all-gather(bf16[4,80,128]{2,1,0:T(8,128)(2,1)S(1)} %slice.52), channel_id=2, replica_groups={{0,1,2,3},{4,5,6,7},{8,9,10,11},{12,13,14,15},{16,17,18,19},{20,21,22,2..., dimensions={0}, use_global_device_ids=true | all-gather | bytes 409600 | tf_op jit(solution)/shard_map/all_gather | solution.py:212
  173.7 1.0 shard_map.117.refs_1_
  174.8 20.1 %collective-permute-start.8 = (bf16[7,80,128]{2,1,0:T(8,128)(2,1)S(1)}, bf16[7,80,128]{2,1,0:T(8,128)(2,1)S(1)}, u32[]{:S(2)}, u32[]{:S(2)}) collective-permute-start(bf16[7,80,128]{2,1,0:T(8,128)(2,1)S(1)} %shard_map.117.refs_1_), channel_id=1, source_target_pairs={{0,16},{1,17},{2,18},{3,19},{4,20},{5,21},{6,22},{7,23},{8,24},{9,... | collective-permute-start | bytes 430088 | tf_op jit(solution)/shard_map/ppermute | solution.py:28
  194.9 28.0 %all-gather.1 = bf16[16,80,128]{2,1,0:T(8,128)(2,1)S(1)} all-gather(bf16[4,80,128]{2,1,0:T(8,128)(2,1)S(1)} %shard_map.118), channel_id=3, replica_groups={{0,1,2,3},{4,5,6,7},{8,9,10,11},{12,13,14,15},{16,17,18,19},{20,21,22,2..., dimensions={0}, use_global_device_ids=true | all-gather | bytes 409600 | tf_op jit(solution)/shard_map/all_gather | solution.py:217
  223.0 1.0 shard_map.119
  224.1 5.2 %collective-permute-start.9 = (bf16[8,80,128]{2,1,0:T(8,128)(2,1)S(1)}, bf16[8,80,128]{2,1,0:T(8,128)(2,1)S(1)}, u32[]{:S(2)}, u32[]{:S(2)}) collective-permute-start(bf16[8,80,128]{2,1,0:T(8,128)(2,1)S(1)} %pad_maximum_fusion.2), channel_id=1, source_target_pairs={{0,32},{1,33},{2,34},{3,35},{4,36},{5,37},{6,38},{7,39},{8,40},{9,... | collective-permute-start | bytes 491528 | tf_op jit(solution)/shard_map/ppermute | solution.py:28
  229.3 2.7 %collective-permute-done.9.refs_6_ = bf16[8,80,128]{2,1,0:T(8,128)(2,1)S(1)} collective-permute-done((bf16[8,80,128]{2,1,0:T(8,128)(2,1)S(1)}, bf16[8,80,128]{2,1,0:T(8,128)(2,1)S(1)}, u32[]{:S(2)}, u32[]{:S(2)}) %collective-permute-start.9) | collective-permute-done | bytes 163872 | tf_op jit(solution)/shard_map/ppermute | solution.py:28
  232.0 1.0 shard_map.120
  233.0 7.7 %collective-permute-start.10 = (bf16[448,128]{1,0:T(8,128)(2,1)S(1)}, bf16[448,128]{1,0:T(8,128)(2,1)S(1)}, u32[]{:S(2)}, u32[]{:S(2)}) collective-permute-start(bf16[448,128]{1,0:T(8,128)(2,1)S(1)} %get-tuple-element.22), channel_id=1, source_target_pairs={{0,64},{64,128},{128,192},{192,256},{256,320},{320,384},{384,448},... | collective-permute-start | bytes 344072 | tf_op jit(solution)/shard_map/ppermute | solution.py:33
  240.7 1.9 collective-permute-start.11
  242.6 6.3 %collective-permute-done.11 = bf16[448,128]{1,0:T(8,128)(2,1)S(1)} collective-permute-done((bf16[448,128]{1,0:T(8,128)(2,1)S(1)}, bf16[448,128]{1,0:T(8,128)(2,1)S(1)}, u32[]{:S(2)}, u32[]{:S(2)}) %collective-permute-start.11) | collective-permute-done | bytes 114720 | tf_op jit(solution)/shard_map/ppermute | solution.py:33
  (47 shorter events, 4.0 us)
Async XLA Ops:
  3.6 8.2 %collective-permute-start = (bf16[7,80,128]{2,1,0:T(8,128)(2,1)}, bf16[7,80,128]{2,1,0:T(8,128)(2,1)S(1)}, u32[]{:S(2)}, u32[]{:S(2)}) collective-permute-start(bf16[7,80,128]{2,1,0:T(8,128)(2,1)} %get-tuple-element.16), channel_id=1, source_target_pairs={{0,32},{1,33},{2,34},{3,35},{4,36},{5,37},{6,38},{7,39},{8,40},{9,... | collective-permute-start | bytes 430088 | tf_op jit(solution)/shard_map/ppermute | solution.py:28
  11.8 0.7 copy-start.8
  16.1 8.1 %copy-start.9 = (bf16[7,80,128]{2,1,0:T(8,128)(2,1)S(1)}, bf16[7,80,128]{2,1,0:T(8,128)(2,1)}, u32[]{:S(2)}) copy-start(bf16[7,80,128]{2,1,0:T(8,128)(2,1)} %get-tuple-element.19) | copy-start | bytes 430084
  18.4 52.7 %copy-start = (bf16[1,448,1024]{2,1,0:T(8,128)(2,1)S(1)}, bf16[1,448,1024]{2,1,0:T(8,128)(2,1)}, u32[]{:S(2)}) copy-start(bf16[1,448,1024]{2,1,0:T(8,128)(2,1)} %param.17) | copy-start | bytes 2752516
  18.4 52.7 %copy-start.1 = (bf16[1,448,1024]{2,1,0:T(8,128)(2,1)S(1)}, bf16[1,448,1024]{2,1,0:T(8,128)(2,1)}, u32[]{:S(2)}) copy-start(bf16[1,448,1024]{2,1,0:T(8,128)(2,1)} %param.18) | copy-start | bytes 2752516
  18.4 52.7 %copy-start.6 = (s32[2]{0:T(128)S(1)}, s32[2]{0:T(128)}, u32[]{:S(2)}) copy-start(s32[2]{0:T(128)} %pad_add_fusion.refs_0_) | copy-start | bytes 28
  18.4 32.3 %all-to-all-start = ((f16[4,4,80,256]{3,2,1,0:T(8,128)(2,1)}), f16[4,4,80,256]{3,2,1,0:T(8,128)(2,1)S(1)}, u32[]{:S(2)}, u32[]{:S(2)}) async-start(f16[4,4,80,256]{3,2,1,0:T(8,128)(2,1)} %convert_element_type.34), calls=%async_computation | async-start | bytes 1310720 | tf_op jit(solution)/shard_map/all_to_all | solution.py:182
  24.1 47.0 %collective-permute-start.3 = (bf16[7,80,128]{2,1,0:T(8,128)(2,1)S(1)}, bf16[7,80,128]{2,1,0:T(8,128)(2,1)S(1)}, u32[]{:S(2)}, u32[]{:S(2)}) collective-permute-start(bf16[7,80,128]{2,1,0:T(8,128)(2,1)S(1)} %copy-done.9), channel_id=1, source_target_pairs={{0,16},{1,17},{2,18},{3,19},{4,20},{5,21},{6,22},{7,23},{8,24},{9,... | collective-permute-start | bytes 430088 | tf_op jit(solution)/shard_map/ppermute | solution.py:28
  73.6 29.7 %all-to-all-start.1 = ((f16[4,4,80,256]{3,2,1,0:T(8,128)(2,1)}), f16[4,4,80,256]{3,2,1,0:T(8,128)(2,1)S(1)}, u32[]{:S(2)}, u32[]{:S(2)}) async-start(f16[4,4,80,256]{3,2,1,0:T(8,128)(2,1)} %convert_element_type.39), calls=%async_computation.1 | async-start | bytes 1310720 | tf_op jit(solution)/shard_map/all_to_all | solution.py:182
  86.8 9.4 %collective-permute-start.1 = (f16[2,80,256]{2,1,0:T(8,128)(2,1)S(1)}, f16[2,80,256]{2,1,0:T(8,128)(2,1)S(1)}, u32[]{:S(2)}, u32[]{:S(2)}) collective-permute-start(f16[2,80,256]{2,1,0:T(8,128)(2,1)S(1)} %slice_convert_fusion.1), channel_id=1, source_target_pairs={{0,4},{1,5},{2,6},{3,7},{4,0},{5,1},{6,2},{7,3},{8,12},{9,13},{10,... | collective-permute-start | bytes 245768 | tf_op jit(solution)/shard_map/ppermute | solution.py:28
  103.4 70.3 %copy-start.2 = (bf16[1,448,1024]{2,1,0:T(8,128)(2,1)S(1)}, bf16[1,448,1024]{2,1,0:T(8,128)(2,1)}, u32[]{:S(2)}) copy-start(bf16[1,448,1024]{2,1,0:T(8,128)(2,1)} %param.19) | copy-start | bytes 2752516
  103.4 18.4 %collective-permute-start.4 = (f16[2,80,256]{2,1,0:T(8,128)(2,1)S(1)}, f16[2,80,256]{2,1,0:T(8,128)(2,1)S(1)}, u32[]{:S(2)}, u32[]{:S(2)}) collective-permute-start(f16[2,80,256]{2,1,0:T(8,128)(2,1)S(1)} %slice_convert_fusion), channel_id=1, source_target_pairs={{0,4},{1,5},{2,6},{3,7},{4,0},{5,1},{6,2},{7,3},{8,12},{9,13},{10,... | collective-permute-start | bytes 245768 | tf_op jit(solution)/shard_map/ppermute | solution.py:28
  105.5 18.4 %collective-permute-start.2 = (f16[80,256]{1,0:T(8,128)(2,1)S(1)}, f16[80,256]{1,0:T(8,128)(2,1)S(1)}, u32[]{:S(2)}, u32[]{:S(2)}) collective-permute-start(f16[80,256]{1,0:T(8,128)(2,1)S(1)} %fusion.2), channel_id=1, source_target_pairs={{0,8},{1,9},{2,10},{3,11},{4,12},{5,13},{6,14},{7,15},{8,0},{9,1},... | collective-permute-start | bytes 122888 | tf_op jit(solution)/shard_map/ppermute | solution.py:28
  121.8 13.9 %collective-permute-start.5 = (f16[80,256]{1,0:T(8,128)(2,1)S(1)}, f16[80,256]{1,0:T(8,128)(2,1)S(1)}, u32[]{:S(2)}, u32[]{:S(2)}) collective-permute-start(f16[80,256]{1,0:T(8,128)(2,1)S(1)} %fusion.3), channel_id=1, source_target_pairs={{0,8},{1,9},{2,10},{3,11},{4,12},{5,13},{6,14},{7,15},{8,0},{9,1},... | collective-permute-start | bytes 122888 | tf_op jit(solution)/shard_map/ppermute | solution.py:28
  135.8 13.6 %collective-permute-start.6 = (bf16[1,160,128]{2,1,0:T(8,128)(2,1)S(1)}, bf16[1,160,128]{2,1,0:T(8,128)(2,1)S(1)}, u32[]{:S(2)}, u32[]{:S(2)}) collective-permute-start(bf16[1,160,128]{2,1,0:T(8,128)(2,1)S(1)} %bitcast.56), channel_id=1, source_target_pairs={{0,8},{1,9},{2,10},{3,11},{4,12},{5,13},{6,14},{7,15},{8,0},{9,1},... | collective-permute-start | bytes 122888 | tf_op jit(solution)/shard_map/ppermute | solution.py:28
  149.4 11.3 %collective-permute-start.7 = (bf16[2,160,128]{2,1,0:T(8,128)(2,1)S(1)}, bf16[2,160,128]{2,1,0:T(8,128)(2,1)S(1)}, u32[]{:S(2)}, u32[]{:S(2)}) collective-permute-start(bf16[2,160,128]{2,1,0:T(8,128)(2,1)S(1)} %pad_maximum_fusion.3), channel_id=1, source_target_pairs={{0,4},{1,5},{2,6},{3,7},{4,0},{5,1},{6,2},{7,3},{8,12},{9,13},{10,... | collective-permute-start | bytes 245768 | tf_op jit(solution)/shard_map/ppermute | solution.py:28
  174.8 57.2 %copy-start.3 = (bf16[1,128,448]{1,2,0:T(8,128)(2,1)S(1)}, bf16[1,128,448]{1,2,0:T(8,128)(2,1)}, u32[]{:S(2)}) copy-start(bf16[1,128,448]{1,2,0:T(8,128)(2,1)} %param.10) | copy-start | bytes 344068
  174.8 57.2 %copy-start.4 = (bf16[1,128,448]{1,2,0:T(8,128)(2,1)S(1)}, bf16[1,128,448]{1,2,0:T(8,128)(2,1)}, u32[]{:S(2)}) copy-start(bf16[1,128,448]{1,2,0:T(8,128)(2,1)} %param.11) | copy-start | bytes 344068
  174.8 57.2 %copy-start.5 = (bf16[4,80,256]{2,1,0:T(8,128)(2,1)S(1)}, bf16[4,80,256]{2,1,0:T(8,128)(2,1)}, u32[]{:S(2)}) copy-start(bf16[4,80,256]{2,1,0:T(8,128)(2,1)} %get-tuple-element.13.refs_3_) | copy-start | bytes 491524
  174.8 57.2 %copy-start.7 = (f32[8,256]{1,0:T(8,128)S(1)}, f32[8,256]{1,0:T(8,128)}, u32[]{:S(2)}) copy-start(f32[8,256]{1,0:T(8,128)} %get-tuple-element.14.refs_4_) | copy-start | bytes 24580
  174.8 49.2 %collective-permute-start.8 = (bf16[7,80,128]{2,1,0:T(8,128)(2,1)S(1)}, bf16[7,80,128]{2,1,0:T(8,128)(2,1)S(1)}, u32[]{:S(2)}, u32[]{:S(2)}) collective-permute-start(bf16[7,80,128]{2,1,0:T(8,128)(2,1)S(1)} %shard_map.117.refs_1_), channel_id=1, source_target_pairs={{0,16},{1,17},{2,18},{3,19},{4,20},{5,21},{6,22},{7,23},{8,24},{9,... | collective-permute-start | bytes 430088 | tf_op jit(solution)/shard_map/ppermute | solution.py:28
  224.1 7.9 %collective-permute-start.9 = (bf16[8,80,128]{2,1,0:T(8,128)(2,1)S(1)}, bf16[8,80,128]{2,1,0:T(8,128)(2,1)S(1)}, u32[]{:S(2)}, u32[]{:S(2)}) collective-permute-start(bf16[8,80,128]{2,1,0:T(8,128)(2,1)S(1)} %pad_maximum_fusion.2), channel_id=1, source_target_pairs={{0,32},{1,33},{2,34},{3,35},{4,36},{5,37},{6,38},{7,39},{8,40},{9,... | collective-permute-start | bytes 491528 | tf_op jit(solution)/shard_map/ppermute | solution.py:28
  233.0 9.6 %collective-permute-start.10 = (bf16[448,128]{1,0:T(8,128)(2,1)S(1)}, bf16[448,128]{1,0:T(8,128)(2,1)S(1)}, u32[]{:S(2)}, u32[]{:S(2)}) collective-permute-start(bf16[448,128]{1,0:T(8,128)(2,1)S(1)} %get-tuple-element.22), channel_id=1, source_target_pairs={{0,64},{64,128},{128,192},{192,256},{256,320},{320,384},{384,448},... | collective-permute-start | bytes 344072 | tf_op jit(solution)/shard_map/ppermute | solution.py:33
  240.7 8.2 %collective-permute-start.11 = (bf16[448,128]{1,0:T(8,128)(2,1)S(1)}, bf16[448,128]{1,0:T(8,128)(2,1)S(1)}, u32[]{:S(2)}, u32[]{:S(2)}) collective-permute-start(bf16[448,128]{1,0:T(8,128)(2,1)S(1)} %get-tuple-element.23), channel_id=1, source_target_pairs={{0,960},{64,0},{128,64},{192,128},{256,192},{320,256},{384,320},{4... | collective-permute-start | bytes 344072 | tf_op jit(solution)/shard_map/ppermute | solution.py:33

commit v5 on v3

--- a/solution.py
+++ b/solution.py
@@ -194,12 +194,15 @@
     got = swap(sent, 32)
     near_sums, message = sum_chunk(place, (own, got, across), w_gate[0], w_up[0], False)
     far_sums = sum_chunk(place, (swap(message, 16),), w_gate[0], w_up[0], True, after=(near_sums,))[0]
-    sums = [halve(value[:2], value[2:], 4) for value in (near_sums, far_sums)]
-    sums = jnp.concatenate([halve(value[0], value[1], 8) for value in sums])
-    block = jax.ShapeDtypeStruct((2 * cap, 128), jnp.bfloat16)
-    blocks = call(hidden_kernel, (block,), [VMEM], (sums,))[0][None]
-    for pattern in (8, 4):
-        blocks = jnp.concatenate([blocks, swap(blocks, pattern)])
+    block = jax.ShapeDtypeStruct((cap, 128), jnp.bfloat16)
+    chunks = []
+    for value in (near_sums, far_sums):
+        value = halve(value[:2], value[2:], 4)
+        value = halve(value[0], value[1], 8)
+        own_block = call(hidden_kernel, (block,), [VMEM], (value,))[0][None]
+        chunks.append((own_block, swap(own_block, 8)))
+    blocks = jnp.concatenate([jnp.concatenate(pair, axis=1) for pair in zip(*chunks)])
+    blocks = jnp.concatenate([blocks, swap(blocks, 4)])
     blocks = lax.all_gather(blocks, "expert", axis_index_groups=quads())
     near_own, near_out, far_out = call(
         down_kernel, (slot, jax.ShapeDtypeStruct((4, cap, 128), jnp.bfloat16), packed), [SMEM] + [VMEM] * 2, (place, blocks, w_down[0]),

time: 243 us -> 244 us (level)
  starting transfers between devices: 128 us -> 122 us
  blocking collectives: 14.2 us -> 17.9 us
    ppermute x2, starting transfers between devices: 24.2 us -> 12.2 us  [shift(): lax.ppermute(value, axis, [(i, (i + steps) % count) for i in range(count)])]
    ppermute x10 -> x11, starting transfers between devices: 84.5 us -> 91.1 us  [swap(): lax.ppermute(value, 'expert', [(i, i ^ pattern) for i in range(count)])]
    all_gather x1, blocking collectives: 14.2 us -> 17.9 us  [local(): blocks = lax.all_gather(blocks, 'expert', axis_index_groups=quads())]
    ppermute x10 -> x11, waiting for transfers between devices: 69 us -> 71.4 us  [swap(): lax.ppermute(value, 'expert', [(i, i ^ pattern) for i in range(count)])]
    pallas_call x6 -> x7, Pallas kernels: 9.59 us -> 9.62 us  [call(): pl.pallas_call(body, out_shape=out_shape, in_specs=[pl.BlockSpec(memory_s...]
  transfers between devices with their start and end apart: 14 -> 15, of which waited for: 10 -> 10; matrix products, arithmetic and copies ran while one was open for 0% -> 0% of each run, Pallas kernels for 0% -> 0%
where the time goes in v5:
time: 244 us; the launch traced here: 242 us
  starting transfers between devices  122 us (50%)
  waiting for transfers between devices  84.7 us (35%)
  blocking collectives  17.9 us (7%)
  Pallas kernels  9.62 us (4%)
  other arithmetic  4.28 us (2%)
    ppermute x11, starting transfers between devices, swap(): lax.ppermute(value, 'expert', [(i, i ^ pattern) for i in range(count)])  91.1 us
    ppermute x11, waiting for transfers between devices, swap(): lax.ppermute(value, 'expert', [(i, i ^ pattern) for i in range(count)])  71.4 us
    all_to_all x2, starting transfers between devices, sum_chunk(): lax.all_to_all(sums.astype(SUM), 'expert', 0, 0, axis_index_groups=quads(...  19 us
    all_gather x1, blocking collectives, local(): blocks = lax.all_gather(blocks, 'expert', axis_index_groups=quads())  17.9 us
    ppermute x2, starting transfers between devices, shift(): lax.ppermute(value, axis, [(i, (i + steps) % count) for i in range(count)])  12.2 us
    pallas_call x7, Pallas kernels, call(): pl.pallas_call(body, out_shape=out_shape, in_specs=[pl.BlockSpec(memory_s...  9.62 us
    all_to_all x2, waiting for transfers between devices, sum_chunk(): lax.all_to_all(sums.astype(SUM), 'expert', 0, 0, axis_index_groups=quads(...  7.01 us
    ppermute x2, waiting for transfers between devices, shift(): lax.ppermute(value, axis, [(i, (i + steps) % count) for i in range(count)])  6.28 us
  transfers between devices with their start and end apart: 15, of which 10 were waited for; matrix products, arithmetic and copies ran while one was open for 0% of the time, Pallas kernels for 0%

profile of v5, /device:TPU:7, one launch (start us, length us, event | category | flops | bytes accessed | tf_op | source)
XLA Modules:
  0.0 241.8 jit_solution(15059155968626664497)
XLA Ops:
  1.3 2.3 shard_map.113
  3.6 4.8 %collective-permute-start = (bf16[7,80,128]{2,1,0:T(8,128)(2,1)}, bf16[7,80,128]{2,1,0:T(8,128)(2,1)S(1)}, u32[]{:S(2)}, u32[]{:S(2)}) collective-permute-start(bf16[7,80,128]{2,1,0:T(8,128)(2,1)} %get-tuple-element.17), channel_id=1, source_target_pairs={{0,32},{1,33},{2,34},{3,35},{4,36},{5,37},{6,38},{7,39},{8,40},{9,... | collective-permute-start | bytes 430088 | tf_op jit(solution)/shard_map/ppermute | solution.py:28
  8.4 3.4 %collective-permute-done.refs_2_ = bf16[7,80,128]{2,1,0:T(8,128)(2,1)S(1)} collective-permute-done((bf16[7,80,128]{2,1,0:T(8,128)(2,1)}, bf16[7,80,128]{2,1,0:T(8,128)(2,1)S(1)}, u32[]{:S(2)}, u32[]{:S(2)}) %collective-permute-start) | collective-permute-done | bytes 143392 | tf_op jit(solution)/shard_map/ppermute | solution.py:28
  12.5 3.6 %shard_map.114 = (f32[4,4,80,256]{3,2,1,0:T(8,128)}, bf16[7,80,128]{2,1,0:T(8,128)(2,1)}) custom-call(s32[2]{0:T(128)} %pad_add_fusion.refs_0_, bf16[80,448]{1,0:T(8,128)(2,1)} %get-tuple-element.16.refs_1_, bf16[7,80,128]{2,1,0:T(8,128)(2,1)} %copy-done.8, bf16[7,80,128]{2,1,0:T(8,128)(2,1)} %get-tuple-element.18.refs_3_, bf16[448,1024]{1,0:T(8,128)(2,1)} %bitcast.44, ...), custom_call_target="tpu_custom_call" | custom-call | flops 293601280 | bytes 2000000 | tf_op jit(solution)/shard_map/pallas_call | solution.py:42
  16.1 2.3 convert_element_type.34
  18.4 5.7 %all-to-all-start = ((f16[4,4,80,256]{3,2,1,0:T(8,128)(2,1)}), f16[4,4,80,256]{3,2,1,0:T(8,128)(2,1)S(1)}, u32[]{:S(2)}, u32[]{:S(2)}) async-start(f16[4,4,80,256]{3,2,1,0:T(8,128)(2,1)} %convert_element_type.34), calls=%async_computation | async-start | bytes 1310720 | tf_op jit(solution)/shard_map/all_to_all | solution.py:175
  24.1 26.6 %collective-permute-start.3 = (bf16[7,80,128]{2,1,0:T(8,128)(2,1)S(1)}, bf16[7,80,128]{2,1,0:T(8,128)(2,1)S(1)}, u32[]{:S(2)}, u32[]{:S(2)}) collective-permute-start(bf16[7,80,128]{2,1,0:T(8,128)(2,1)S(1)} %copy-done.9), channel_id=1, source_target_pairs={{0,16},{1,17},{2,18},{3,19},{4,20},{5,21},{6,22},{7,23},{8,24},{9,... | collective-permute-start | bytes 430088 | tf_op jit(solution)/shard_map/ppermute | solution.py:28
  50.8 20.3 %collective-permute-done.3.refs_1_ = bf16[7,80,128]{2,1,0:T(8,128)(2,1)S(1)} collective-permute-done((bf16[7,80,128]{2,1,0:T(8,128)(2,1)S(1)}, bf16[7,80,128]{2,1,0:T(8,128)(2,1)S(1)}, u32[]{:S(2)}, u32[]{:S(2)}) %collective-permute-start.3) | collective-permute-done | bytes 143392 | tf_op jit(solution)/shard_map/ppermute | solution.py:28
  71.2 1.4 shard_map.116
  73.6 13.2 %all-to-all-start.1 = ((f16[4,4,80,256]{3,2,1,0:T(8,128)(2,1)}), f16[4,4,80,256]{3,2,1,0:T(8,128)(2,1)S(1)}, u32[]{:S(2)}, u32[]{:S(2)}) async-start(f16[4,4,80,256]{3,2,1,0:T(8,128)(2,1)} %convert_element_type.39), calls=%async_computation.1 | async-start | bytes 1310720 | tf_op jit(solution)/shard_map/all_to_all | solution.py:175
  86.8 2.5 %collective-permute-start.1 = (f16[2,80,256]{2,1,0:T(8,128)(2,1)S(1)}, f16[2,80,256]{2,1,0:T(8,128)(2,1)S(1)}, u32[]{:S(2)}, u32[]{:S(2)}) collective-permute-start(f16[2,80,256]{2,1,0:T(8,128)(2,1)S(1)} %slice_convert_fusion.1), channel_id=1, source_target_pairs={{0,4},{1,5},{2,6},{3,7},{4,0},{5,1},{6,2},{7,3},{8,12},{9,13},{10,... | collective-permute-start | bytes 245768 | tf_op jit(solution)/shard_map/ppermute | solution.py:28
  89.3 6.9 %collective-permute-done.1 = f16[2,80,256]{2,1,0:T(8,128)(2,1)S(1)} collective-permute-done((f16[2,80,256]{2,1,0:T(8,128)(2,1)S(1)}, f16[2,80,256]{2,1,0:T(8,128)(2,1)S(1)}, u32[]{:S(2)}, u32[]{:S(2)}) %collective-permute-start.1) | collective-permute-done | bytes 81952 | tf_op jit(solution)/shard_map/ppermute | solution.py:28
  96.2 7.0 %all-to-all-done.1 = f16[4,4,80,256]{3,2,1,0:T(8,128)(2,1)S(1)} async-done(((f16[4,4,80,256]{3,2,1,0:T(8,128)(2,1)}), f16[4,4,80,256]{3,2,1,0:T(8,128)(2,1)S(1)}, u32[]{:S(2)}, u32[]{:S(2)}) %all-to-all-start.1) | async-done | bytes 655392 | tf_op jit(solution)/shard_map/all_to_all | solution.py:175
  103.3 2.1 collective-permute-start.4
  105.4 16.3 %collective-permute-start.2 = (f16[80,256]{1,0:T(8,128)(2,1)S(1)}, f16[80,256]{1,0:T(8,128)(2,1)S(1)}, u32[]{:S(2)}, u32[]{:S(2)}) collective-permute-start(f16[80,256]{1,0:T(8,128)(2,1)S(1)} %fusion.2), channel_id=1, source_target_pairs={{0,8},{1,9},{2,10},{3,11},{4,12},{5,13},{6,14},{7,15},{8,0},{9,1},... | collective-permute-start | bytes 122888 | tf_op jit(solution)/shard_map/ppermute | solution.py:28
  121.8 2.1 collective-permute-start.5
  123.9 11.9 %collective-permute-start.6 = (bf16[1,80,128]{2,1,0:T(8,128)(2,1)S(1)}, bf16[1,80,128]{2,1,0:T(8,128)(2,1)S(1)}, u32[]{:S(2)}, u32[]{:S(2)}) collective-permute-start(bf16[1,80,128]{2,1,0:T(8,128)(2,1)S(1)} %bitcast.54), channel_id=1, source_target_pairs={{0,8},{1,9},{2,10},{3,11},{4,12},{5,13},{6,14},{7,15},{8,0},{9,1},... | collective-permute-start | bytes 61448 | tf_op jit(solution)/shard_map/ppermute | solution.py:28
  135.9 2.1 collective-permute-start.7
  137.9 2.9 %collective-permute-done.6 = bf16[1,80,128]{2,1,0:T(8,128)(2,1)S(1)} collective-permute-done((bf16[1,80,128]{2,1,0:T(8,128)(2,1)S(1)}, bf16[1,80,128]{2,1,0:T(8,128)(2,1)S(1)}, u32[]{:S(2)}, u32[]{:S(2)}) %collective-permute-start.6) | collective-permute-done | bytes 20512 | tf_op jit(solution)/shard_map/ppermute | solution.py:28
  140.9 8.5 %collective-permute-done.7 = bf16[1,80,128]{2,1,0:T(8,128)(2,1)S(1)} collective-permute-done((bf16[1,80,128]{2,1,0:T(8,128)(2,1)S(1)}, bf16[1,80,128]{2,1,0:T(8,128)(2,1)S(1)}, u32[]{:S(2)}, u32[]{:S(2)}) %collective-permute-start.7) | collective-permute-done | bytes 20512 | tf_op jit(solution)/shard_map/ppermute | solution.py:28
  149.4 1.9 collective-permute-start.8
  151.3 7.8 %collective-permute-done.8 = bf16[2,160,128]{2,1,0:T(8,128)(2,1)S(1)} collective-permute-done((bf16[2,160,128]{2,1,0:T(8,128)(2,1)S(1)}, bf16[2,160,128]{2,1,0:T(8,128)(2,1)S(1)}, u32[]{:S(2)}, u32[]{:S(2)}) %collective-permute-start.8) | collective-permute-done | bytes 81952 | tf_op jit(solution)/shard_map/ppermute | solution.py:28
  159.2 17.9 %all-gather = bf16[16,160,128]{2,1,0:T(8,128)(2,1)S(1)} all-gather(bf16[4,160,128]{2,1,0:T(8,128)(2,1)S(1)} %pad_maximum_fusion), channel_id=2, replica_groups={{0,1,2,3},{4,5,6,7},{8,9,10,11},{12,13,14,15},{16,17,18,19},{20,21,22,2..., dimensions={0}, use_global_device_ids=true | all-gather | bytes 819200 | tf_op jit(solution)/shard_map/all_gather | solution.py:206
  177.1 1.3 shard_map.118
  178.4 16.1 %collective-permute-start.9 = (bf16[7,80,128]{2,1,0:T(8,128)(2,1)S(1)}, bf16[7,80,128]{2,1,0:T(8,128)(2,1)S(1)}, u32[]{:S(2)}, u32[]{:S(2)}) collective-permute-start(bf16[7,80,128]{2,1,0:T(8,128)(2,1)S(1)} %get-tuple-element.23), channel_id=1, source_target_pairs={{0,16},{1,17},{2,18},{3,19},{4,20},{5,21},{6,22},{7,23},{8,24},{9,... | collective-permute-start | bytes 430088 | tf_op jit(solution)/shard_map/ppermute | solution.py:28
  194.5 18.8 %collective-permute-done.9.refs_7_ = bf16[7,80,128]{2,1,0:T(8,128)(2,1)S(1)} collective-permute-done((bf16[7,80,128]{2,1,0:T(8,128)(2,1)S(1)}, bf16[7,80,128]{2,1,0:T(8,128)(2,1)S(1)}, u32[]{:S(2)}, u32[]{:S(2)}) %collective-permute-start.9) | collective-permute-done | bytes 143392 | tf_op jit(solution)/shard_map/ppermute | solution.py:28
  213.4 4.8 %collective-permute-start.10 = (bf16[8,80,128]{2,1,0:T(8,128)(2,1)S(1)}, bf16[8,80,128]{2,1,0:T(8,128)(2,1)S(1)}, u32[]{:S(2)}, u32[]{:S(2)}) collective-permute-start(bf16[8,80,128]{2,1,0:T(8,128)(2,1)S(1)} %pad_maximum_fusion.1), channel_id=1, source_target_pairs={{0,32},{1,33},{2,34},{3,35},{4,36},{5,37},{6,38},{7,39},{8,40},{9,... | collective-permute-start | bytes 491528 | tf_op jit(solution)/shard_map/ppermute | solution.py:28
  218.2 2.7 %collective-permute-done.10.refs_6_ = bf16[8,80,128]{2,1,0:T(8,128)(2,1)S(1)} collective-permute-done((bf16[8,80,128]{2,1,0:T(8,128)(2,1)S(1)}, bf16[8,80,128]{2,1,0:T(8,128)(2,1)S(1)}, u32[]{:S(2)}, u32[]{:S(2)}) %collective-permute-start.10) | collective-permute-done | bytes 163872 | tf_op jit(solution)/shard_map/ppermute | solution.py:28
  220.9 1.0 shard_map.119
  221.9 10.3 %collective-permute-start.11 = (bf16[448,128]{1,0:T(8,128)(2,1)S(1)}, bf16[448,128]{1,0:T(8,128)(2,1)S(1)}, u32[]{:S(2)}, u32[]{:S(2)}) collective-permute-start(bf16[448,128]{1,0:T(8,128)(2,1)S(1)} %get-tuple-element.24), channel_id=1, source_target_pairs={{0,64},{64,128},{128,192},{192,256},{256,320},{320,384},{384,448},... | collective-permute-start | bytes 344072 | tf_op jit(solution)/shard_map/ppermute | solution.py:33
  232.2 1.9 collective-permute-start.12
  234.2 6.3 %collective-permute-done.12 = bf16[448,128]{1,0:T(8,128)(2,1)S(1)} collective-permute-done((bf16[448,128]{1,0:T(8,128)(2,1)S(1)}, bf16[448,128]{1,0:T(8,128)(2,1)S(1)}, u32[]{:S(2)}, u32[]{:S(2)}) %collective-permute-start.12) | collective-permute-done | bytes 114720 | tf_op jit(solution)/shard_map/ppermute | solution.py:33
  (47 shorter events, 4.0 us)
Async XLA Ops:
  3.6 8.2 %collective-permute-start = (bf16[7,80,128]{2,1,0:T(8,128)(2,1)}, bf16[7,80,128]{2,1,0:T(8,128)(2,1)S(1)}, u32[]{:S(2)}, u32[]{:S(2)}) collective-permute-start(bf16[7,80,128]{2,1,0:T(8,128)(2,1)} %get-tuple-element.17), channel_id=1, source_target_pairs={{0,32},{1,33},{2,34},{3,35},{4,36},{5,37},{6,38},{7,39},{8,40},{9,... | collective-permute-start | bytes 430088 | tf_op jit(solution)/shard_map/ppermute | solution.py:28
  11.8 0.7 copy-start.8
  16.1 8.1 %copy-start.9 = (bf16[7,80,128]{2,1,0:T(8,128)(2,1)S(1)}, bf16[7,80,128]{2,1,0:T(8,128)(2,1)}, u32[]{:S(2)}) copy-start(bf16[7,80,128]{2,1,0:T(8,128)(2,1)} %get-tuple-element.20) | copy-start | bytes 430084
  18.4 52.8 %copy-start = (bf16[1,448,1024]{2,1,0:T(8,128)(2,1)S(1)}, bf16[1,448,1024]{2,1,0:T(8,128)(2,1)}, u32[]{:S(2)}) copy-start(bf16[1,448,1024]{2,1,0:T(8,128)(2,1)} %param.17) | copy-start | bytes 2752516
  18.4 52.8 %copy-start.1 = (bf16[1,448,1024]{2,1,0:T(8,128)(2,1)S(1)}, bf16[1,448,1024]{2,1,0:T(8,128)(2,1)}, u32[]{:S(2)}) copy-start(bf16[1,448,1024]{2,1,0:T(8,128)(2,1)} %param.18) | copy-start | bytes 2752516
  18.4 52.8 %copy-start.6 = (s32[2]{0:T(128)S(1)}, s32[2]{0:T(128)}, u32[]{:S(2)}) copy-start(s32[2]{0:T(128)} %pad_add_fusion.refs_0_) | copy-start | bytes 28
  18.4 32.3 %all-to-all-start = ((f16[4,4,80,256]{3,2,1,0:T(8,128)(2,1)}), f16[4,4,80,256]{3,2,1,0:T(8,128)(2,1)S(1)}, u32[]{:S(2)}, u32[]{:S(2)}) async-start(f16[4,4,80,256]{3,2,1,0:T(8,128)(2,1)} %convert_element_type.34), calls=%async_computation | async-start | bytes 1310720 | tf_op jit(solution)/shard_map/all_to_all | solution.py:175
  24.1 47.0 %collective-permute-start.3 = (bf16[7,80,128]{2,1,0:T(8,128)(2,1)S(1)}, bf16[7,80,128]{2,1,0:T(8,128)(2,1)S(1)}, u32[]{:S(2)}, u32[]{:S(2)}) collective-permute-start(bf16[7,80,128]{2,1,0:T(8,128)(2,1)S(1)} %copy-done.9), channel_id=1, source_target_pairs={{0,16},{1,17},{2,18},{3,19},{4,20},{5,21},{6,22},{7,23},{8,24},{9,... | collective-permute-start | bytes 430088 | tf_op jit(solution)/shard_map/ppermute | solution.py:28
  73.6 29.6 %all-to-all-start.1 = ((f16[4,4,80,256]{3,2,1,0:T(8,128)(2,1)}), f16[4,4,80,256]{3,2,1,0:T(8,128)(2,1)S(1)}, u32[]{:S(2)}, u32[]{:S(2)}) async-start(f16[4,4,80,256]{3,2,1,0:T(8,128)(2,1)} %convert_element_type.39), calls=%async_computation.1 | async-start | bytes 1310720 | tf_op jit(solution)/shard_map/all_to_all | solution.py:175
  86.8 9.4 %collective-permute-start.1 = (f16[2,80,256]{2,1,0:T(8,128)(2,1)S(1)}, f16[2,80,256]{2,1,0:T(8,128)(2,1)S(1)}, u32[]{:S(2)}, u32[]{:S(2)}) collective-permute-start(f16[2,80,256]{2,1,0:T(8,128)(2,1)S(1)} %slice_convert_fusion.1), channel_id=1, source_target_pairs={{0,4},{1,5},{2,6},{3,7},{4,0},{5,1},{6,2},{7,3},{8,12},{9,13},{10,... | collective-permute-start | bytes 245768 | tf_op jit(solution)/shard_map/ppermute | solution.py:28
  103.3 73.8 %copy-start.2 = (bf16[1,448,1024]{2,1,0:T(8,128)(2,1)S(1)}, bf16[1,448,1024]{2,1,0:T(8,128)(2,1)}, u32[]{:S(2)}) copy-start(bf16[1,448,1024]{2,1,0:T(8,128)(2,1)} %param.19) | copy-start | bytes 2752516
  103.3 18.3 %collective-permute-start.4 = (f16[2,80,256]{2,1,0:T(8,128)(2,1)S(1)}, f16[2,80,256]{2,1,0:T(8,128)(2,1)S(1)}, u32[]{:S(2)}, u32[]{:S(2)}) collective-permute-start(f16[2,80,256]{2,1,0:T(8,128)(2,1)S(1)} %slice_convert_fusion), channel_id=1, source_target_pairs={{0,4},{1,5},{2,6},{3,7},{4,0},{5,1},{6,2},{7,3},{8,12},{9,13},{10,... | collective-permute-start | bytes 245768 | tf_op jit(solution)/shard_map/ppermute | solution.py:28
  105.4 18.4 %collective-permute-start.2 = (f16[80,256]{1,0:T(8,128)(2,1)S(1)}, f16[80,256]{1,0:T(8,128)(2,1)S(1)}, u32[]{:S(2)}, u32[]{:S(2)}) collective-permute-start(f16[80,256]{1,0:T(8,128)(2,1)S(1)} %fusion.2), channel_id=1, source_target_pairs={{0,8},{1,9},{2,10},{3,11},{4,12},{5,13},{6,14},{7,15},{8,0},{9,1},... | collective-permute-start | bytes 122888 | tf_op jit(solution)/shard_map/ppermute | solution.py:28
  121.8 14.1 %collective-permute-start.5 = (f16[80,256]{1,0:T(8,128)(2,1)S(1)}, f16[80,256]{1,0:T(8,128)(2,1)S(1)}, u32[]{:S(2)}, u32[]{:S(2)}) collective-permute-start(f16[80,256]{1,0:T(8,128)(2,1)S(1)} %fusion.3), channel_id=1, source_target_pairs={{0,8},{1,9},{2,10},{3,11},{4,12},{5,13},{6,14},{7,15},{8,0},{9,1},... | collective-permute-start | bytes 122888 | tf_op jit(solution)/shard_map/ppermute | solution.py:28
  123.9 17.0 %collective-permute-start.6 = (bf16[1,80,128]{2,1,0:T(8,128)(2,1)S(1)}, bf16[1,80,128]{2,1,0:T(8,128)(2,1)S(1)}, u32[]{:S(2)}, u32[]{:S(2)}) collective-permute-start(bf16[1,80,128]{2,1,0:T(8,128)(2,1)S(1)} %bitcast.54), channel_id=1, source_target_pairs={{0,8},{1,9},{2,10},{3,11},{4,12},{5,13},{6,14},{7,15},{8,0},{9,1},... | collective-permute-start | bytes 61448 | tf_op jit(solution)/shard_map/ppermute | solution.py:28
  135.9 13.5 %collective-permute-start.7 = (bf16[1,80,128]{2,1,0:T(8,128)(2,1)S(1)}, bf16[1,80,128]{2,1,0:T(8,128)(2,1)S(1)}, u32[]{:S(2)}, u32[]{:S(2)}) collective-permute-start(bf16[1,80,128]{2,1,0:T(8,128)(2,1)S(1)} %bitcast.57), channel_id=1, source_target_pairs={{0,8},{1,9},{2,10},{3,11},{4,12},{5,13},{6,14},{7,15},{8,0},{9,1},... | collective-permute-start | bytes 61448 | tf_op jit(solution)/shard_map/ppermute | solution.py:28
  149.4 9.8 %collective-permute-start.8 = (bf16[2,160,128]{2,1,0:T(8,128)(2,1)S(1)}, bf16[2,160,128]{2,1,0:T(8,128)(2,1)S(1)}, u32[]{:S(2)}, u32[]{:S(2)}) collective-permute-start(bf16[2,160,128]{2,1,0:T(8,128)(2,1)S(1)} %pad_maximum_fusion.2), channel_id=1, source_target_pairs={{0,4},{1,5},{2,6},{3,7},{4,0},{5,1},{6,2},{7,3},{8,12},{9,13},{10,... | collective-permute-start | bytes 245768 | tf_op jit(solution)/shard_map/ppermute | solution.py:28
  159.2 61.8 %copy-start.3 = (bf16[1,128,448]{1,2,0:T(8,128)(2,1)S(1)}, bf16[1,128,448]{1,2,0:T(8,128)(2,1)}, u32[]{:S(2)}) copy-start(bf16[1,128,448]{1,2,0:T(8,128)(2,1)} %param.10) | copy-start | bytes 344068
  159.2 61.8 %copy-start.4 = (bf16[1,128,448]{1,2,0:T(8,128)(2,1)S(1)}, bf16[1,128,448]{1,2,0:T(8,128)(2,1)}, u32[]{:S(2)}) copy-start(bf16[1,128,448]{1,2,0:T(8,128)(2,1)} %param.11) | copy-start | bytes 344068
  159.2 61.7 %copy-start.5 = (bf16[4,80,256]{2,1,0:T(8,128)(2,1)S(1)}, bf16[4,80,256]{2,1,0:T(8,128)(2,1)}, u32[]{:S(2)}) copy-start(bf16[4,80,256]{2,1,0:T(8,128)(2,1)} %get-tuple-element.14.refs_3_) | copy-start | bytes 491524
  159.2 61.7 %copy-start.7 = (f32[8,256]{1,0:T(8,128)S(1)}, f32[8,256]{1,0:T(8,128)}, u32[]{:S(2)}) copy-start(f32[8,256]{1,0:T(8,128)} %get-tuple-element.15.refs_4_) | copy-start | bytes 24580
  178.4 34.9 %collective-permute-start.9 = (bf16[7,80,128]{2,1,0:T(8,128)(2,1)S(1)}, bf16[7,80,128]{2,1,0:T(8,128)(2,1)S(1)}, u32[]{:S(2)}, u32[]{:S(2)}) collective-permute-start(bf16[7,80,128]{2,1,0:T(8,128)(2,1)S(1)} %get-tuple-element.23), channel_id=1, source_target_pairs={{0,16},{1,17},{2,18},{3,19},{4,20},{5,21},{6,22},{7,23},{8,24},{9,... | collective-permute-start | bytes 430088 | tf_op jit(solution)/shard_map/ppermute | solution.py:28
  213.4 7.6 %collective-permute-start.10 = (bf16[8,80,128]{2,1,0:T(8,128)(2,1)S(1)}, bf16[8,80,128]{2,1,0:T(8,128)(2,1)S(1)}, u32[]{:S(2)}, u32[]{:S(2)}) collective-permute-start(bf16[8,80,128]{2,1,0:T(8,128)(2,1)S(1)} %pad_maximum_fusion.1), channel_id=1, source_target_pairs={{0,32},{1,33},{2,34},{3,35},{4,36},{5,37},{6,38},{7,39},{8,40},{9,... | collective-permute-start | bytes 491528 | tf_op jit(solution)/shard_map/ppermute | solution.py:28
  221.9 12.2 %collective-permute-start.11 = (bf16[448,128]{1,0:T(8,128)(2,1)S(1)}, bf16[448,128]{1,0:T(8,128)(2,1)S(1)}, u32[]{:S(2)}, u32[]{:S(2)}) collective-permute-start(bf16[448,128]{1,0:T(8,128)(2,1)S(1)} %get-tuple-element.24), channel_id=1, source_target_pairs={{0,64},{64,128},{128,192},{192,256},{256,320},{320,384},{384,448},... | collective-permute-start | bytes 344072 | tf_op jit(solution)/shard_map/ppermute | solution.py:33
  232.2 8.2 %collective-permute-start.12 = (bf16[448,128]{1,0:T(8,128)(2,1)S(1)}, bf16[448,128]{1,0:T(8,128)(2,1)S(1)}, u32[]{:S(2)}, u32[]{:S(2)}) collective-permute-start(bf16[448,128]{1,0:T(8,128)(2,1)S(1)} %get-tuple-element.25), channel_id=1, source_target_pairs={{0,960},{64,0},{128,64},{192,128},{256,192},{320,256},{384,320},{4... | collective-permute-start | bytes 344072 | tf_op jit(solution)/shard_map/ppermute | solution.py:33
